TPU v7x, 32 devices: a whole 2x2x4 slice. The times are simulated.
32 devices in a mesh: group: 2 (over x), row: 16 (over z, y, core).
Axes of the slice: x: 2, y: 2, z: 4, core: 2. Of those that a mesh axis runs over, the one named last changes fastest.
Arguments:
- anc_cov: bfloat16 [8192, 4096], P(('group', 'row')), parts along dimension 0, as said below
- mid_factor: bfloat16 [8192, 1024], P(('group', 'row')), parts along dimension 0, may hold values from -0.125 to 0.125
- mid_diag_inv: bfloat16 [2048, 1024], P(('group', 'row')), parts along dimension 0, as said below
- leaf_factor: bfloat16 [10240, 512], P(('group', 'row')), parts along dimension 0, may hold values from -0.125 to 0.125
- leaf_diag_inv: bfloat16 [2048, 512], P(('group', 'row')), parts along dimension 0, as said below
- leaf_rows: int32 [2, 80], replicated, may hold values from 0 to 159, as said below
Outputs:
- mid_block: float32 [2048, 1024], P(('group', 'row')), parts along dimension 0
- leaf_block: float32 [2048, 512], P(('group', 'row')), parts along dimension 0
There are 2 independent parts, one for each index of `group`. A program takes and returns all parts, laid end to end along the dimension named above; an argument that names none is the same for every part. Nothing has to cross between parts.
Inputs may be any that keep to these rules, and one draw needn't show every extreme that they name: `leaf_rows`: each row lists 80 distinct block numbers in increasing order; every row holds the first and the last block. `anc_cov`: symmetric in every draw. `mid_diag_inv`: symmetric in every draw. `leaf_diag_inv`: each of the two stacked 512 x 512 blocks is symmetric in every draw.
All inputs are finite; a program needn't handle non-finite values.
Results may differ from a plain program's by a relative error of at most 0.0003.
Values may be sent and summed in bfloat16 or wider, within the bound.
No kernel may reach another device: no remote copies, remote signals or barrier semaphores. Data moves between devices by JAX's collectives and lax.ppermute only.
A program may use at most 128 MiB of HBM per device.

v0:
```python
import jax
import jax.numpy as jnp
from jax import lax
from jax.sharding import PartitionSpec as P

TILE = 32


def across(left, right):
    return lax.dot_general(
        left.astype(jnp.float32),
        right,
        (((0,), (0,)), ((), ())),
        precision=lax.Precision.HIGHEST,
        preferred_element_type=jnp.float32,
    )


def exact_dot(left, right):
    return jnp.dot(
        left,
        right.astype(jnp.float32),
        precision=lax.Precision.HIGHEST,
        preferred_element_type=jnp.float32,
    )


def embed_factor(block_list, factor, tiles_total):
    listed = block_list.shape[0]
    tiled = factor.reshape(listed, -1)
    matches = block_list[None, :] == jnp.arange(tiles_total, dtype=jnp.int32)[:, None]
    position = jnp.sum(jnp.where(matches, jnp.arange(listed, dtype=jnp.int32)[None, :], 0), axis=1)
    present = jnp.any(matches, axis=1)
    picked = jnp.take(tiled, position, axis=0)
    picked = jnp.where(present[:, None], picked, jnp.zeros_like(picked))
    return picked.reshape(tiles_total * (factor.shape[0] // listed), factor.shape[1])


def embed_both(leaf_rows, leaf_factor, tiles_total):
    halfway = leaf_factor.shape[0] // 2
    first = embed_factor(leaf_rows[0], leaf_factor[:halfway], tiles_total)
    second = embed_factor(leaf_rows[1], leaf_factor[halfway:], tiles_total)
    return jnp.concatenate([first, second], axis=1)


def local(anc_cov, mid_factor, mid_diag_inv, leaf_factor, leaf_diag_inv, leaf_rows):
    device_place = lax.axis_index("row")
    anc_local = anc_cov.shape[0]
    anc_order = anc_cov.shape[1]
    mid_local = mid_diag_inv.shape[0]
    mid_order = mid_factor.shape[1]
    leaf_order = leaf_factor.shape[1]
    product = jnp.dot(
        anc_cov,
        lax.all_gather(mid_factor, "row", axis=0, tiled=True),
        preferred_element_type=jnp.float32,
    )
    cross = -product
    gathered = lax.all_gather(leaf_factor, "row", axis=0, tiled=True)
    tiles_total = (mid_order + anc_order) // TILE
    embedded = embed_both(leaf_rows, gathered, tiles_total)
    embed_mid = embedded[:mid_order]
    spread_low = exact_dot(cross, embed_mid) + jnp.dot(
        anc_cov, embedded[mid_order:], preferred_element_type=jnp.float32
    )
    joined = lax.psum_scatter(
        jnp.concatenate([across(mid_factor, cross), across(mid_factor, spread_low)], axis=1),
        "row",
        scatter_dimension=0,
        tiled=True,
    )
    mid_sum = joined[:, :mid_order]
    image_sum = joined[:, mid_order:]
    mid_block = mid_diag_inv.astype(jnp.float32) - mid_sum
    mid_image = jnp.dot(mid_diag_inv, embed_mid, preferred_element_type=jnp.float32) - image_sum
    own_mid = lax.dynamic_slice_in_dim(embedded, device_place * mid_local, mid_local, 0)
    own_anc = lax.dynamic_slice_in_dim(embedded, mid_order + device_place * anc_local, anc_local, 0)
    own_embed = jnp.concatenate([own_mid, own_anc], axis=0).astype(jnp.float32)
    own_image = jnp.concatenate([mid_image, spread_low], axis=0)
    local_total = own_embed.shape[0]
    child_terms = jnp.einsum(
        "rki,rkj->kij",
        own_embed.reshape(local_total, 2, leaf_order),
        own_image.reshape(local_total, 2, leaf_order),
        precision=lax.Precision.HIGHEST,
        preferred_element_type=jnp.float32,
    ).reshape(2 * leaf_order, leaf_order)
    leaf_sum = lax.psum_scatter(child_terms, "row", scatter_dimension=0, tiled=True)
    leaf_block = leaf_diag_inv.astype(jnp.float32) + leaf_sum
    return (mid_block, leaf_block)


def solution(mesh):
    placed = (
        P(("group", "row"), None),
        P(("group", "row"), None),
        P(("group", "row"), None),
        P(("group", "row"), None),
        P(("group", "row"), None),
        P(),
    )
    return jax.shard_map(
        local,
        mesh=mesh,
        in_specs=placed,
        out_specs=(P(("group", "row"), None), P(("group", "row"), None)),
        check_vma=False,
    )
```

profile of v0, /device:TPU:0, one launch (start us, length us, event | category | flops | bytes accessed | tf_op | source)
XLA Modules:
  0.0 357.2 jit_solution(16803813530244955973)
XLA Ops:
  7.2 0.0 copy-start
  7.2 0.0 all-gather.5.cloned.1.call-start
  7.2 0.7 all-gather.5.cloned.1.call-update
  7.9 0.0 all-gather.3.cloned.1.call-start
  8.0 0.7 all-gather.3.cloned.1.call-update
  8.7 0.0 reduce-scatter.7.cloned.1.call-start
  8.7 0.8 slice_bitcast_fusion
  9.5 0.2 select_reduce_fusion
  9.7 0.2 fusion.23
  9.8 59.2 %all-gather.5.cloned.1.call-done = bf16[5120,512]{1,0:T(8,128)(2,1)} async-done(((bf16[320,512]{1,0:T(8,128)(2,1)}), bf16[5120,512]{1,0:T(8,128)(2,1)}) %all-gather.5.cloned.1.call-update) | async-done | bytes 5242896 | tf_op jit(solution)/shard_map/all_gather | solution.py:59
  69.0 5.1 %fusion.25 = (bf16[2560,512]{1,0:T(8,128)(2,1)}, bf16[2560,512]{1,0:T(8,128)(2,1)}) fusion(bf16[5120,512]{1,0:T(8,128)(2,1)} %all-gather.5.cloned.1.call-done), kind=kLoop, calls=%fused_computation.45 | loop fusion | bytes 10485760 | tf_op jit(solution)/shard_map/slice | solution.py:42
  74.2 5.3 %reshape.32 = bf16[80,16384]{1,0:T(8,128)(2,1)} reshape(bf16[2560,512]{1,0:T(8,128)(2,1)} %get-tuple-element.12) | data formatting | bytes 5242880 | tf_op jit(solution)/shard_map/reshape | solution.py:30
  79.5 12.8 %gather_fusion = bf16[160,16384]{1,0:T(8,128)(2,1)} fusion(bf16[80,16384]{1,0:T(8,128)(2,1)} %reshape.32, s32[1024]{0:T(1024)S(1)} %pad_clamp_fusion.1), kind=kCustom, calls=%fused_computation.clone | custom fusion | bytes 10486400 | tf_op jit(solution)/shard_map/jit(_take)/gather | solution.py:34
  92.3 5.5 %select_select_fusion.1 = bf16[160,16384]{1,0:T(8,128)(2,1)} fusion(bf16[160,16384]{1,0:T(8,128)(2,1)} %gather_fusion, pred[160]{0:T(512)(128)(4,1)S(1)} %compare_and_fusion.1, pred[160]{0:T(512)(128)(4,1)S(1)} %get-tuple-element.18), kind=kLoop, calls=%fused_computation.6 | loop fusion | flops 5242880 | bytes 10486080 | tf_op jit(solution)/shard_map/jit(_where)/select_n | solution.py:35
  97.8 9.1 %reshape.33 = bf16[5120,512]{1,0:T(8,128)(2,1)} reshape(bf16[160,16384]{1,0:T(8,128)(2,1)} %select_select_fusion.1) | data formatting | bytes 10485760 | tf_op jit(solution)/shard_map/reshape | solution.py:36
  106.9 5.3 %reshape.34 = bf16[80,16384]{1,0:T(8,128)(2,1)} reshape(bf16[2560,512]{1,0:T(8,128)(2,1)} %get-tuple-element.11) | data formatting | bytes 5242880 | tf_op jit(solution)/shard_map/reshape | solution.py:30
  112.2 12.8 %gather_fusion.1 = bf16[160,16384]{1,0:T(8,128)(2,1)} fusion(bf16[80,16384]{1,0:T(8,128)(2,1)} %reshape.34, s32[1024]{0:T(1024)S(1)} %pad_clamp_fusion), kind=kCustom, calls=%fused_computation.1.clone | custom fusion | bytes 10486400 | tf_op jit(solution)/shard_map/jit(_take)/gather | solution.py:34
  125.0 5.4 %select_select_fusion = bf16[160,16384]{1,0:T(8,128)(2,1)} fusion(bf16[160,16384]{1,0:T(8,128)(2,1)} %gather_fusion.1, pred[160]{0:T(512)(128)(4,1)S(1)} %compare_and_fusion, pred[160]{0:T(512)(128)(4,1)S(1)} %get-tuple-element.17), kind=kLoop, calls=%fused_computation.5 | loop fusion | flops 5242880 | bytes 10486080 | tf_op jit(solution)/shard_map/jit(_where)/select_n | solution.py:35
  130.5 9.0 %reshape.35 = bf16[5120,512]{1,0:T(8,128)(2,1)} reshape(bf16[160,16384]{1,0:T(8,128)(2,1)} %select_select_fusion) | data formatting | bytes 10485760 | tf_op jit(solution)/shard_map/reshape | solution.py:36
  139.4 0.0 copy-start.1
  139.4 3.5 constant_dynamic-update-slice_fusion.1
  142.9 0.7 copy-done.1
  143.6 1.4 constant_dynamic-update-slice_fusion
  145.0 0.0 copy-start.2
  145.0 4.0 %copy-done.2 = bf16[5120,1024]{1,0:T(8,128)(2,1)} copy-done((bf16[5120,1024]{1,0:T(8,128)(2,1)}, bf16[5120,1024]{1,0:T(8,128)(2,1)S(1)}, u32[]{:S(2)}) %copy-start.2) | copy-done | bytes 10485784
  149.0 0.0 copy-done
  149.0 3.3 fusion.9
  152.3 0.0 copy-start.3
  152.3 0.0 all-gather.3.cloned.1.call-done
  152.3 5.8 %convolution_negate_fusion = f32[256,1024]{1,0:T(8,128)S(1)} fusion(bf16[256,4096]{1,0:T(8,128)(2,1)S(1)} %copy-done, bf16[4096,1024]{1,0:T(8,128)(2,1)} %all-gather.3.cloned.1.call-done), kind=kOutput, calls=%fused_computation.15 | convolution fusion | flops 2147745792 | bytes 11534336 | tf_op jit(solution)/shard_map/dot_general | solution.py:53
  158.1 0.0 copy-done.3
  158.1 0.0 copy-start.6
  158.1 0.0 copy-start.4
  158.1 1.8 convolution_bitcast_fusion.1
  160.0 0.0 copy-done.6
  160.0 3.4 fusion.6
  163.4 0.0 copy-done.4
  163.4 1.8 convolution_bitcast_fusion
  165.3 4.2 %pad_maximum_fusion = f32[1024,2048]{0,1:T(8,128)} fusion(f32[1024,1024]{0,1:T(8,128)S(1)} %convolution_bitcast_fusion, f32[1024,1024]{0,1:T(8,128)S(1)} %convolution_bitcast_fusion.1), kind=kLoop, calls=%fused_computation.4 | loop fusion | flops 2097152 | bytes 16777216 | tf_op jit(solution)/shard_map/concatenate | solution.py:67
  169.5 9.2 %copy.29 = f32[1024,2048]{1,0:T(8,128)} copy(f32[1024,2048]{0,1:T(8,128)} %pad_maximum_fusion) | data formatting | bytes 16777216
  178.6 0.0 copy-start.7
  178.6 0.0 reduce-scatter.7.cloned.1.call-update
  178.6 0.3 reduce-scatter.5.cloned.1.call-start
  179.0 0.9 constant_dynamic-slice_fusion.1
  179.9 1.1 constant_dynamic-slice_fusion
  181.0 0.9 pad_maximum_fusion.2
  181.9 100.2 %reduce-scatter.7.cloned.1.call-done = f32[64,2048]{1,0:T(8,128)} async-done(((f32[1024,2048]{1,0:T(8,128)}), f32[64,2048]{1,0:T(8,128)}) %reduce-scatter.7.cloned.1.call-update) | async-done | bytes 524304 | tf_op jit(solution)/shard_map/reduce_scatter | solution.py:66
  282.1 0.0 copy-done.7
  282.1 0.0 copy-start.5
  282.1 2.1 fusion.18
  284.2 0.1 pad_maximum_fusion.1
  284.3 0.0 slice-start
  284.3 0.0 copy-done.5
  284.3 3.2 fusion.12
  287.6 0.0 reduce-scatter.5.cloned.1.call-update
  287.6 0.2 copy.24
  287.8 0.0 slice-done
  287.8 0.2 copy.31
  288.0 0.9 copy.28
  288.9 60.1 %reduce-scatter.5.cloned.1.call-done = f32[64,512]{1,0:T(8,128)} async-done(((f32[1024,512]{1,0:T(8,128)}), f32[64,512]{1,0:T(8,128)}) %reduce-scatter.5.cloned.1.call-update) | async-done | bytes 131088 | tf_op jit(solution)/shard_map/reduce_scatter | solution.py:88
  349.1 1.6 convert_add_fusion
  (7 shorter events, 0.1 us)
Async XLA Ops:
  7.2 141.8 %copy-start = (bf16[256,4096]{1,0:T(8,128)(2,1)S(1)}, bf16[256,4096]{1,0:T(8,128)(2,1)}, u32[]{:S(2)}) copy-start(bf16[256,4096]{1,0:T(8,128)(2,1)} %param.8) | copy-start | bytes 6291460
  7.2 61.8 %all-gather.5.cloned.1.call-start = ((), (), s32[]{:S(2)}) async-start(), calls=%async_computation.3 | async-start | bytes 5570560 | tf_op jit(solution)/shard_map/all_gather | solution.py:59
  7.9 144.4 %all-gather.3.cloned.1.call-start = ((), (), s32[]{:S(2)}) async-start(), calls=%async_computation.2 | async-start | bytes 8912896 | tf_op jit(solution)/shard_map/all_gather | solution.py:55
  8.7 273.4 %reduce-scatter.7.cloned.1.call-start = ((), (), s32[]{:S(2)}) async-start(), calls=%async_computation.5 | async-start | bytes 8912896 | tf_op jit(solution)/shard_map/reduce_scatter | solution.py:66
  139.4 4.2 %copy-start.1 = (bf16[5120,512]{1,0:T(8,128)(2,1)S(1)}, bf16[5120,512]{1,0:T(8,128)(2,1)}, u32[]{:S(2)}) copy-start(bf16[5120,512]{1,0:T(8,128)(2,1)} %reshape.35) | copy-start | bytes 15728644
  145.0 4.0 %copy-start.2 = (bf16[5120,1024]{1,0:T(8,128)(2,1)}, bf16[5120,1024]{1,0:T(8,128)(2,1)S(1)}, u32[]{:S(2)}) copy-start(bf16[5120,1024]{1,0:T(8,128)(2,1)S(1)} %constant_dynamic-update-slice_fusion) | copy-start | bytes 31457284
  152.3 5.8 %copy-start.3 = (bf16[256,1024]{1,0:T(8,128)(2,1)S(1)}, bf16[256,1024]{1,0:T(8,128)(2,1)}, u32[]{:S(2)}) copy-start(bf16[256,1024]{1,0:T(8,128)(2,1)} %param.9) | copy-start | bytes 1572868
  158.1 1.9 copy-start.6
  158.1 5.3 %copy-start.4 = (bf16[256,1024]{1,0:T(8,128)(2,1)S(1)}, bf16[256,1024]{1,0:T(8,128)(2,1)}, u32[]{:S(2)}) copy-start(bf16[256,1024]{1,0:T(8,128)(2,1)} %param.9) | copy-start | bytes 1572868
  178.6 103.4 %copy-start.7 = (bf16[64,1024]{1,0:T(8,128)(2,1)S(1)}, bf16[64,1024]{1,0:T(8,128)(2,1)}, u32[]{:S(2)}) copy-start(bf16[64,1024]{1,0:T(8,128)(2,1)} %param.10) | copy-start | bytes 393220
  178.6 170.4 %reduce-scatter.5.cloned.1.call-start = ((), (), s32[]{:S(2)}) async-start(), calls=%async_computation.4 | async-start | bytes 2228224 | tf_op jit(solution)/shard_map/reduce_scatter | solution.py:88
  282.1 2.3 copy-start.5
  284.3 3.5 slice-start
Sparse Core Ops, SparseCore 0:
  10.3 58.6 all-gather.4
  71.2 73.4 all-gather.2
  178.8 103.2 reduce-scatter.6
  287.7 61.2 reduce-scatter.4
where the time goes:
time: 358 us; the launch traced here: 357 us
  waiting for transfers between devices  221 us (62%)
  local copies, waits for them, and re-layouts  82.2 us (23%)
  matrix products  21.5 us (6%)
  other arithmetic  18.1 us (5%)
  between operations  14 us (4%)
    reduce_scatter x1, waiting for transfers between devices, local(): lax.psum_scatter(jnp.concatenate([across(mid_factor, cross), across(mid_f...  100 us
    reduce_scatter x1, waiting for transfers between devices, local(): lax.psum_scatter(child_terms, 'row', scatter_dimension=0, tiled=True)  60.1 us
    all_gather x1, waiting for transfers between devices, local(): gathered = lax.all_gather(leaf_factor, 'row', axis=0, tiled=True)  59.2 us
    gather x2, local copies, waits for them, and re-layouts, embed_factor(): picked = jnp.take(tiled, position, axis=0)  25.7 us
    unnamed x21, local copies, waits for them, and re-layouts  18.6 us
    reshape x2, local copies, waits for them, and re-layouts, embed_factor(): picked.reshape(tiles_total * (factor.shape[0] // listed), factor.shape[1])  18.1 us
    select_n x2, other arithmetic, embed_factor(): picked = jnp.where(present[:, None], picked, jnp.zeros_like(picked))  10.9 us
    reshape x2, local copies, waits for them, and re-layouts, embed_factor(): tiled = factor.reshape(listed, -1)  10.6 us
  transfers between devices with their start and end apart: 4, of which 3 were waited for; matrix products, arithmetic and copies ran while one was open for 23% of the time, Pallas kernels for 0%

commit v1 on v0

v1 whole, which is shorter than its diff:
```python
import jax
import jax.numpy as jnp
from jax import lax
from jax.experimental import pallas as pl
from jax.experimental.pallas import tpu as pltpu
from jax.sharding import PartitionSpec as P

TILE = 32
F32 = jnp.float32
BF16 = jnp.bfloat16


def ring_order(chips, parts):
    if parts == 2 and chips % 2 == 0:
        return list(range(0, chips, 2)) + list(range(chips - 1, 0, -2))
    return list(range(chips))


def split(x):
    high = x.astype(BF16)
    return high, (x - high.astype(F32)).astype(BF16)


def mm(a, b):
    return lax.dot_general(a, b, (((1,), (0,)), ((), ())), preferred_element_type=F32)


def mmt(a, b):
    return lax.dot_general(a, b, (((0,), (0,)), ((), ())), preferred_element_type=F32)


def place_of(chip, chips, snake):
    return jnp.where(chip % 2 == 0, chip // 2, chips - 1 - chip // 2) if snake else chip


def chip_at(place, chips, snake):
    place = lax.rem(place, chips)
    return jnp.where(2 * place < chips, 2 * place, 2 * (chips - 1 - place) + 1) if snake else place


def mid_kernel(chips, snake, *refs):
    half = chips // 2
    device_ref, a_refs, f_refs = refs[0], refs[1:3], refs[3 : 3 + 2 * (half + 1)]
    high_ref, low_ref = refs[5 + 2 * half : 7 + 2 * half]
    y_refs = refs[7 + 2 * half : 7 + 2 * half + chips]
    left, right, turned, picked, stacked, sems = refs[7 + 2 * half + chips :]
    device = device_ref[0]
    chip, core = device // 2, device % 2
    place = place_of(chip, chips, snake)
    rows = f_refs[0].shape[0]
    mid = f_refs[0].shape[1]
    copies = []
    for step in range(half + 1):
        owner = chip_at(place + step, chips, snake)
        for side in range(2):
            lane = pl.multiple_of((2 * owner + (core if side == 0 else 1 - core)) * rows, rows)
            at = (2 * step + side) * rows
            for k in range(2):
                source, target = a_refs[k].at[:, pl.ds(lane, rows)], left.at[k * rows : (k + 1) * rows, at : at + rows]
                copies.append(pltpu.make_async_copy(source, target, sems.at[len(copies)]))
            source, target = f_refs[2 * step + side], right.at[at : at + rows, :]
            copies.append(pltpu.make_async_copy(source, target, sems.at[len(copies)]))
    for copy in copies:
        copy.start()
    for copy in copies[:6]:
        copy.wait()
    near = 2 * rows
    left[:, :near] = left[:, :near] * jnp.bfloat16(0.5)
    far = near + 2 * rows * (half // 2)
    for copy in copies[6 : 6 * (1 + half // 2)]:
        copy.wait()
    cross = mm(left[:, :far], right[:far, :])
    for copy in copies[6 * (1 + half // 2) :]:
        copy.wait()
    high, low = split(cross + mm(left[:, far:], right[far:, :]))
    high_ref[...] = high
    low_ref[...] = low
    factor = right[: 2 * rows, :]
    for k, x in enumerate((factor, high, low)):
        turned[k * mid : (k + 1) * mid, :] = x.T
    stacked[: 2 * rows, :] = high
    stacked[2 * rows : 4 * rows, :] = low
    stacked[4 * rows : 6 * rows, :] = factor
    stacked[6 * rows :, :] = factor
    strip = mid // (2 * chips)
    for s in range(chips):
        first = pl.multiple_of((2 * chip_at(place + s, chips, snake) + core) * strip, strip)
        for k, which in enumerate((0, 0, 1, 2)):
            picked[s * strip : (s + 1) * strip, k * 2 * rows : (k + 1) * 2 * rows] = turned[
                pl.ds(which * mid + first, strip), :
            ]
    y = mm(picked[...], stacked[...])
    for s in range(chips):
        y_refs[s][...] = y[s * strip : (s + 1) * strip, :]


def leaf_kernel(chips, snake, *refs):
    half = chips // 2
    device_ref, list_ref, a_refs, f_refs, d_refs = refs[0], refs[1], refs[2:4], refs[4:6], refs[6:8]
    high_ref, low_ref = refs[8:10]
    parts = refs[10 : 10 + 2 * chips]
    keep_refs = refs[10 + 2 * chips : 10 + 3 * chips]
    give_ref, wide, left, right, factors, diags, highs, lows, result, sems, embed_sem = refs[10 + 3 * chips :]
    device = device_ref[0]
    chip, core = device // 2, device % 2
    place = place_of(chip, chips, snake)
    rows, mid = f_refs[0].shape
    leaf = wide.shape[1]
    count = parts[0].shape[0] // TILE
    chip_rows = 2 * rows
    strip = d_refs[0].shape[0]
    copies = []

    def fetch(source, target):
        copies.append(pltpu.make_async_copy(source, target, sems.at[len(copies)]))
        copies[-1].start()

    for k in range(2):
        fetch(f_refs[k], factors.at[k * rows : (k + 1) * rows, :])
        fetch(d_refs[k], diags.at[k * strip : (k + 1) * strip, :])
    fetch(high_ref, highs)
    fetch(low_ref, lows)
    early = len(copies)
    for step in range(half + 1):
        lane = pl.multiple_of(chip_at(place + step, chips, snake) * chip_rows, chip_rows)
        at = step * chip_rows
        for k in range(2):
            fetch(a_refs[k].at[:, pl.ds(lane, chip_rows)], left.at[k * rows : (k + 1) * rows, at : at + chip_rows])
    wide[...] = jnp.zeros_like(wide)
    for slot in range(chips):
        source = chip_at(place + chips - slot, chips, snake)

        @pl.when(source // half == core)
        def _():
            for side in range(2):
                first = (2 * (source % half) + (core if side == 0 else 1 - core)) * count
                for i in range(count):
                    to = pl.multiple_of(list_ref[core, first + i] * TILE, TILE)
                    block = parts[2 * slot + side].at[i * TILE : (i + 1) * TILE, :]
                    pltpu.make_async_copy(block, wide.at[pl.ds(to, TILE), :], embed_sem).start()

    every = wide.at[: chips * count * TILE, :]
    pltpu.make_async_copy(every, every, embed_sem).wait()
    for step in range(half + 1):
        owner = chip_at(place + step, chips, snake)
        lane = pl.multiple_of(owner * chip_rows, chip_rows)
        at = step * chip_rows
        right[at : at + chip_rows, :] = wide[pl.ds(pl.multiple_of(mid + lane, chip_rows), chip_rows), :]
    at = half * chip_rows
    right[at:, :] = jnp.where(place < half, right[at:, :], jnp.zeros_like(right[at:, :]))
    for copy in copies[:early]:
        copy.wait()
    embed_mid = wide[:mid, :]
    other = 2 * chip + 1 - core
    own = jnp.concatenate(
        [wide[pl.ds(pl.multiple_of(mid + d * rows, rows), rows), :].astype(F32) for d in (device, other)]
    )
    g_high, g_low = split(own - mm(factors[...], embed_mid))
    spread = mm(highs[...], embed_mid) + mm(lows[...], embed_mid)
    i_high, i_low = split(mm(diags[...], embed_mid))
    for copy in copies[early:]:
        copy.wait()
    left[:, :chip_rows] = left[:, :chip_rows] * jnp.bfloat16(0.5)
    s_high, s_low = split(mm(left[...], right[...]) - spread)
    inner = mmt(g_high, s_high) + mmt(g_high, s_low) + mmt(g_low, s_high)
    total = inner + inner.T
    own_mid = jnp.concatenate(
        [wide[pl.ds(pl.multiple_of(d * strip, strip), strip), :] for d in (device, other)]
    )
    result[...] = total + mmt(own_mid, i_high) + mmt(own_mid, i_low)
    band = leaf // chips
    for s in range(chips):
        target = chip_at(place + s, chips, snake)
        mine = target // half == core
        for ref, side in ((keep_refs[s], core), (give_ref.at[s * band : (s + 1) * band, :], 1 - core)):
            value = result[pl.ds(pl.multiple_of((2 * (target % half) + side) * band, band), band), :]
            ref[...] = jnp.where(mine, value, jnp.zeros_like(value))


def solution(mesh):
    parts, devices = mesh.shape["group"], mesh.shape["row"]
    chips = devices // 2
    half = chips // 2
    snake = parts == 2
    order = ring_order(chips, parts)

    def perm(step, keep=lambda source, target, core: True):
        pairs = []
        for p in range(chips):
            target = (p + step) % chips
            for core in range(2):
                if keep(p, target, core):
                    pairs.append((order[p] * 2 + core, order[target] * 2 + core))
        return pairs

    def child_of(p):
        return order[p % chips] // half

    swap_pairs = [(d, d ^ 1) for d in range(devices)]

    def swap(x):
        return lax.ppermute(x, "row", swap_pairs)

    def ring_sum(terms):
        far = terms[half]
        cut = far.shape[0] // 2
        up = lax.ppermute(far[:cut], "row", perm(1))
        down = lax.ppermute(far[cut:], "row", perm(-1))
        up = terms[half - 1] + jnp.pad(up, ((0, cut), (0, 0)))
        down = terms[half + 1] + jnp.pad(down, ((cut, 0), (0, 0)))
        for s in range(half - 1, 0, -1):
            up = lax.ppermute(up, "row", perm(1))
            down = lax.ppermute(down, "row", perm(-1))
            if s > 1:
                up = up + terms[s - 1]
                down = down + terms[chips - s + 1]
        return terms[0] + up + down

    vmem = pl.BlockSpec(memory_space=pltpu.VMEM)
    smem = pl.BlockSpec(memory_space=pltpu.SMEM)
    anywhere = pl.BlockSpec(memory_space=pl.ANY)
    mid_params = pltpu.CompilerParams(vmem_limit_bytes=32 * 2**20)
    leaf_params = pltpu.CompilerParams(vmem_limit_bytes=28 * 2**20)

    def local(anc_cov, mid_factor, mid_diag_inv, leaf_factor, leaf_diag_inv, leaf_rows):
        device = lax.axis_index("row")
        device_word = device.astype(jnp.int32).reshape(1)
        rows, anc = anc_cov.shape
        mid = mid_factor.shape[1]
        leaf = leaf_factor.shape[1]

        leaf_flow = leaf_factor
        leaf_parts = [leaf_factor, swap(leaf_factor)]
        flow = mid_factor
        factors = [mid_factor, swap(mid_factor)]
        anc_swapped = swap(anc_cov)
        diag_swapped = swap(mid_diag_inv)
        done = 0
        for step in range(1, chips):
            due = min(half, (step * half - 1) // (chips - 1))
            while done < due:
                done += 1
                pairs = perm(-1, (lambda s, t, c: t < half) if done == half else (lambda s, t, c: True))
                flow = lax.ppermute(flow, "row", pairs)
                factors += [flow, swap(flow)]
                flow, leaf_flow = lax.optimization_barrier((flow, leaf_flow))
            leaf_flow = lax.ppermute(leaf_flow, "row", perm(1))
            leaf_parts += [leaf_flow, swap(leaf_flow)]
        while done < half:
            done += 1
            pairs = perm(-1, (lambda s, t, c: t < half) if done == half else (lambda s, t, c: True))
            flow = lax.ppermute(flow, "row", pairs)
            factors += [flow, swap(flow)]

        strip = mid // devices
        depth = 2 * rows * (half + 1)
        outs = pl.pallas_call(
            lambda *refs: mid_kernel(chips, snake, *refs),
            out_shape=[jax.ShapeDtypeStruct((2 * rows, mid), BF16)] * 2
            + [jax.ShapeDtypeStruct((strip, mid), F32)] * chips,
            in_specs=[smem] + [anywhere] * (2 + len(factors)),
            out_specs=[vmem] * (2 + chips),
            scratch_shapes=[
                pltpu.VMEM((2 * rows, depth), BF16),
                pltpu.VMEM((depth, mid), BF16),
                pltpu.VMEM((3 * mid, 2 * rows), BF16),
                pltpu.VMEM((mid // 2, 8 * rows), BF16),
                pltpu.VMEM((8 * rows, mid), BF16),
                pltpu.SemaphoreType.DMA((6 * (half + 1),)),
            ],
            compiler_params=mid_params,
            cost_estimate=pl.CostEstimate(flops=15 * 10**9, bytes_accessed=14 * 2**20, transcendentals=0),
            name="mid_blocks",
        )(device_word, anc_cov, anc_swapped, *factors)
        c_high, c_low, mid_terms = outs[0], outs[1], outs[2:]
        mid_block = mid_diag_inv.astype(F32) + ring_sum(mid_terms)

        band = leaf // chips
        *keep, give = pl.pallas_call(
            lambda *refs: leaf_kernel(chips, snake, *refs),
            out_shape=[jax.ShapeDtypeStruct((band, leaf), F32)] * chips + [jax.ShapeDtypeStruct((leaf, leaf), F32)],
            in_specs=[smem, smem] + [anywhere] * (8 + 2 * chips),
            out_specs=[vmem] * (chips + 1),
            scratch_shapes=[
                pltpu.VMEM((mid + anc, leaf), BF16),
                pltpu.VMEM((2 * rows, depth), BF16),
                pltpu.VMEM((depth, leaf), BF16),
                pltpu.VMEM((2 * rows, mid), BF16),
                pltpu.VMEM((2 * strip, mid), BF16),
                pltpu.VMEM((2 * rows, mid), BF16),
                pltpu.VMEM((2 * rows, mid), BF16),
                pltpu.VMEM((leaf, leaf), F32),
                pltpu.SemaphoreType.DMA((6 + 2 * (half + 1),)),
                pltpu.SemaphoreType.DMA,
            ],
            compiler_params=leaf_params,
            cost_estimate=pl.CostEstimate(flops=2 * 10**10, bytes_accessed=20 * 2**20, transcendentals=0),
            name="leaf_blocks",
        )(
            device_word, leaf_rows, anc_cov, anc_swapped, factors[0], factors[1], mid_diag_inv, diag_swapped,
            c_high, c_low, *leaf_parts,
        )
        got = swap(give)
        leaf_terms = [keep[s] + got[s * band : (s + 1) * band] for s in range(chips)]
        leaf_block = leaf_diag_inv.astype(F32) + ring_sum(leaf_terms)
        return mid_block, leaf_block

    placed = (
        P(("group", "row"), None),
        P(("group", "row"), None),
        P(("group", "row"), None),
        P(("group", "row"), None),
        P(("group", "row"), None),
        P(),
    )
    return jax.shard_map(
        local,
        mesh=mesh,
        in_specs=placed,
        out_specs=(P(("group", "row"), None), P(("group", "row"), None)),
        check_vma=False,
    )
```

time: 358 us -> 138 us (0.39)
  waiting for transfers between devices: 221 us -> 72.6 us
  local copies, waits for them, and re-layouts: 82.2 us -> 8.16 us
  starting transfers between devices: 0.42 us -> 35.2 us
  matrix products: 21.5 us -> 0 us
  Pallas kernels: 0 us -> 19.3 us
  other arithmetic: 18.1 us -> 1.8 us
  between operations: 14 us -> 1.03 us
    reduce_scatter x2 -> x0, waiting for transfers between devices: 160 us -> none  [the longest x1 100 us: local(): lax.psum_scatter(jnp.concatenate([across(mid_factor, cross), across(mid_f...]
    ppermute x0 -> x43, waiting for transfers between devices: none -> 72.6 us  [the longest x7 35.5 us: local(): leaf_flow = lax.ppermute(leaf_flow, 'row', perm(1))]
    all_gather x2 -> x0, waiting for transfers between devices: 59.2 us -> none  [the longest x1 59.2 us: local(): gathered = lax.all_gather(leaf_factor, 'row', axis=0, tiled=True)]
    ppermute x0 -> x43, starting transfers between devices: none -> 35.2 us  [the longest x6 10.9 us: ring_sum(): up = lax.ppermute(up, 'row', perm(1))]
    reshape x4 -> x0, local copies, waits for them, and re-layouts: 28.7 us -> none  [the longest x2 18.1 us: embed_factor(): picked.reshape(tiles_total * (factor.shape[0] // listed), factor.shape[1])]
    gather x2 -> x0, local copies, waits for them, and re-layouts: 25.7 us -> none  [embed_factor(): picked = jnp.take(tiled, position, axis=0)]
    dot_general x7 -> x0, matrix products: 21.5 us -> none  [the longest x1 5.76 us: local(): jnp.dot(anc_cov, lax.all_gather(mid_factor, 'row', axis=0, tiled=True), p...]
    pallas_call x0 -> x2, Pallas kernels: none -> 19.3 us  [the longest x1 11.1 us: local(): pl.pallas_call(lambda *refs: leaf_kernel(chips, snake, *refs), out_shape=...]
  transfers between devices with their start and end apart: 4 -> 43, of which waited for: 3 -> 20; matrix products, arithmetic and copies ran while one was open for 23% -> 1% of each run, Pallas kernels for 0% -> 6%
where the time goes in v1:
time: 138 us
  waiting for transfers between devices  72.6 us (53%)
  starting transfers between devices  35.2 us (26%)
  Pallas kernels  19.3 us (14%)
  local copies, waits for them, and re-layouts  8.16 us (6%)
  other arithmetic  1.8 us (1%)
    ppermute x7, waiting for transfers between devices, local(): leaf_flow = lax.ppermute(leaf_flow, 'row', perm(1))  35.5 us
    ppermute x4, waiting for transfers between devices, local(): flow = lax.ppermute(flow, 'row', pairs)  16.8 us
    pallas_call x1, Pallas kernels, local(): pl.pallas_call(lambda *refs: leaf_kernel(chips, snake, *refs), out_shape=...  11.1 us
    ppermute x6, starting transfers between devices, ring_sum(): up = lax.ppermute(up, 'row', perm(1))  10.9 us
    ppermute x7, starting transfers between devices, local(): leaf_flow = lax.ppermute(leaf_flow, 'row', perm(1))  9.75 us
    ppermute x6, waiting for transfers between devices, ring_sum(): down = lax.ppermute(down, 'row', perm(-1))  8.99 us
    pallas_call x1, Pallas kernels, local(): pl.pallas_call(lambda *refs: mid_kernel(chips, snake, *refs), out_shape=[...  8.22 us
    unnamed x52, local copies, waits for them, and re-layouts  8.13 us
  transfers between devices with their start and end apart: 43, of which 20 were waited for; matrix products, arithmetic and copies ran while one was open for 1% of the time, Pallas kernels for 6%

profile of v1, /device:TPU:0, one launch (start us, length us, event | category | flops | bytes accessed | tf_op | source)
XLA Modules:
  0.0 138.1 jit_solution(17784503870840978977)
XLA Ops:
  0.6 3.0 %collective-permute-start.2 = (bf16[256,1024]{1,0:T(8,128)(2,1)}, bf16[256,1024]{1,0:T(8,128)(2,1)S(1)}, u32[]{:S(2)}, u32[]{:S(2)}) collective-permute-start(bf16[256,1024]{1,0:T(8,128)(2,1)} %refs_4_.1), channel_id=1, source_target_pairs={{0,2},{1,3},{4,0},{5,1},{8,4},{9,5},{12,8},{13,9},{14,12},{15,13},... | collective-permute-start | bytes 1572872 | tf_op jit(solution)/shard_map/ppermute | solution.py:244
  3.8 9.3 %collective-permute-done.4.refs_12_ = bf16[320,512]{1,0:T(8,128)(2,1)S(1)} collective-permute-done((bf16[320,512]{1,0:T(8,128)(2,1)}, bf16[320,512]{1,0:T(8,128)(2,1)S(1)}, u32[]{:S(2)}, u32[]{:S(2)}) %collective-permute-start.4) | collective-permute-done | bytes 327712 | tf_op jit(solution)/shard_map/ppermute | solution.py:247
  13.0 2.8 %collective-permute-done.2.refs_5_ = bf16[256,1024]{1,0:T(8,128)(2,1)S(1)} collective-permute-done((bf16[256,1024]{1,0:T(8,128)(2,1)}, bf16[256,1024]{1,0:T(8,128)(2,1)S(1)}, u32[]{:S(2)}, u32[]{:S(2)}) %collective-permute-start.2) | collective-permute-done | bytes 524320 | tf_op jit(solution)/shard_map/ppermute | solution.py:244
  15.8 1.7 %collective-permute-start.7 = (bf16[320,512]{1,0:T(8,128)(2,1)S(1)}, bf16[320,512]{1,0:T(8,128)(2,1)S(1)}, u32[]{:S(2)}, u32[]{:S(2)}) collective-permute-start(bf16[320,512]{1,0:T(8,128)(2,1)S(1)} %collective-permute-done.4.refs_12_), channel_id=1, source_target_pairs={{0,4},{1,5},{4,8},{5,9},{8,12},{9,13},{12,14},{13,15},{14,10},{15,... | collective-permute-start | bytes 983048 | tf_op jit(solution)/shard_map/ppermute | solution.py:247
  17.6 0.3 collective-permute-start.5
  17.9 6.9 %collective-permute-done.7.refs_14_ = bf16[320,512]{1,0:T(8,128)(2,1)S(1)} collective-permute-done((bf16[320,512]{1,0:T(8,128)(2,1)S(1)}, bf16[320,512]{1,0:T(8,128)(2,1)S(1)}, u32[]{:S(2)}, u32[]{:S(2)}) %collective-permute-start.7) | collective-permute-done | bytes 327712 | tf_op jit(solution)/shard_map/ppermute | solution.py:247
  24.7 1.4 %collective-permute-start.8 = (bf16[320,512]{1,0:T(8,128)(2,1)S(1)}, bf16[320,512]{1,0:T(8,128)(2,1)S(1)}, u32[]{:S(2)}, u32[]{:S(2)}) collective-permute-start(bf16[320,512]{1,0:T(8,128)(2,1)S(1)} %collective-permute-done.7.refs_14_), channel_id=1, source_target_pairs={{0,4},{1,5},{4,8},{5,9},{8,12},{9,13},{12,14},{13,15},{14,10},{15,... | collective-permute-start | bytes 983048 | tf_op jit(solution)/shard_map/ppermute | solution.py:247
  26.2 4.0 %collective-permute-done.5.refs_7_ = bf16[256,1024]{1,0:T(8,128)(2,1)} collective-permute-done((bf16[256,1024]{1,0:T(8,128)(2,1)S(1)}, bf16[256,1024]{1,0:T(8,128)(2,1)}, u32[]{:S(2)}, u32[]{:S(2)}) %collective-permute-start.5) | collective-permute-done | bytes 524320 | tf_op jit(solution)/shard_map/ppermute | solution.py:244
  30.2 2.6 %collective-permute-done.8.refs_16_ = bf16[320,512]{1,0:T(8,128)(2,1)S(1)} collective-permute-done((bf16[320,512]{1,0:T(8,128)(2,1)S(1)}, bf16[320,512]{1,0:T(8,128)(2,1)S(1)}, u32[]{:S(2)}, u32[]{:S(2)}) %collective-permute-start.8) | collective-permute-done | bytes 327712 | tf_op jit(solution)/shard_map/ppermute | solution.py:247
  32.8 1.1 collective-permute-start.11
  33.9 0.9 collective-permute-start.9
  34.8 5.8 %collective-permute-done.11.refs_18_ = bf16[320,512]{1,0:T(8,128)(2,1)S(1)} collective-permute-done((bf16[320,512]{1,0:T(8,128)(2,1)S(1)}, bf16[320,512]{1,0:T(8,128)(2,1)S(1)}, u32[]{:S(2)}, u32[]{:S(2)}) %collective-permute-start.11) | collective-permute-done | bytes 327712 | tf_op jit(solution)/shard_map/ppermute | solution.py:247
  40.7 1.4 %collective-permute-start.12 = (bf16[320,512]{1,0:T(8,128)(2,1)S(1)}, bf16[320,512]{1,0:T(8,128)(2,1)S(1)}, u32[]{:S(2)}, u32[]{:S(2)}) collective-permute-start(bf16[320,512]{1,0:T(8,128)(2,1)S(1)} %collective-permute-done.11.refs_18_), channel_id=1, source_target_pairs={{0,4},{1,5},{4,8},{5,9},{8,12},{9,13},{12,14},{13,15},{14,10},{15,... | collective-permute-start | bytes 983048 | tf_op jit(solution)/shard_map/ppermute | solution.py:247
  42.1 0.5 collective-permute-start.24
  42.6 2.5 %collective-permute-done.9.refs_9_ = bf16[256,1024]{1,0:T(8,128)(2,1)} collective-permute-done((bf16[256,1024]{1,0:T(8,128)(2,1)}, bf16[256,1024]{1,0:T(8,128)(2,1)}, u32[]{:S(2)}, u32[]{:S(2)}) %collective-permute-start.9) | collective-permute-done | bytes 524320 | tf_op jit(solution)/shard_map/ppermute | solution.py:244
  45.1 2.6 %collective-permute-done.12.refs_20_ = bf16[320,512]{1,0:T(8,128)(2,1)S(1)} collective-permute-done((bf16[320,512]{1,0:T(8,128)(2,1)S(1)}, bf16[320,512]{1,0:T(8,128)(2,1)S(1)}, u32[]{:S(2)}, u32[]{:S(2)}) %collective-permute-start.12) | collective-permute-done | bytes 327712 | tf_op jit(solution)/shard_map/ppermute | solution.py:247
  47.8 0.7 copy-done.22
  48.5 1.3 collective-permute-start.13
  49.8 0.7 copy-done.16
  50.5 0.5 collective-permute-start.25
  51.0 0.7 copy-done.8
  51.8 0.5 collective-permute-done.25.refs_13_
  52.2 0.7 copy-done.18
  53.0 2.6 %collective-permute-start.30 = (bf16[320,512]{1,0:T(8,128)(2,1)S(1)}, bf16[320,512]{1,0:T(8,128)(2,1)}, u32[]{:S(2)}, u32[]{:S(2)}) collective-permute-start(bf16[320,512]{1,0:T(8,128)(2,1)S(1)} %collective-permute-done.12.refs_20_), channel_id=1, source_target_pairs={{0,4},{1,5},{4,8},{5,9},{8,12},{9,13},{12,14},{13,15},{14,10},{15,... | collective-permute-start | bytes 983048 | tf_op jit(solution)/shard_map/ppermute | solution.py:247
  55.5 0.8 copy-done.5
  56.3 0.7 copy-done.20
  57.1 0.5 collective-permute-start.10
  57.6 7.4 %collective-permute-done.13.refs_11_ = bf16[256,1024]{1,0:T(8,128)(2,1)} collective-permute-done((bf16[256,1024]{1,0:T(8,128)(2,1)}, bf16[256,1024]{1,0:T(8,128)(2,1)}, u32[]{:S(2)}, u32[]{:S(2)}) %collective-permute-start.13) | collective-permute-done | bytes 524320 | tf_op jit(solution)/shard_map/ppermute | solution.py:252
  65.0 1.4 %collective-permute-start.32 = (bf16[320,512]{1,0:T(8,128)(2,1)}, bf16[320,512]{1,0:T(8,128)(2,1)}, u32[]{:S(2)}, u32[]{:S(2)}) collective-permute-start(bf16[320,512]{1,0:T(8,128)(2,1)} %collective-permute-done.30.refs_22_), channel_id=1, source_target_pairs={{0,4},{1,5},{4,8},{5,9},{8,12},{9,13},{12,14},{13,15},{14,10},{15,... | collective-permute-start | bytes 983048 | tf_op jit(solution)/shard_map/ppermute | solution.py:247
  66.4 0.2 collective-permute-start.27
  66.6 0.3 collective-permute-start.28
  67.1 8.3 %collective-permute-done.32.refs_24_ = bf16[320,512]{1,0:T(8,128)(2,1)} collective-permute-done((bf16[320,512]{1,0:T(8,128)(2,1)}, bf16[320,512]{1,0:T(8,128)(2,1)}, u32[]{:S(2)}, u32[]{:S(2)}) %collective-permute-start.32) | collective-permute-done | bytes 327712 | tf_op jit(solution)/shard_map/ppermute | solution.py:247
  75.4 0.5 collective-permute-start.33
  75.9 1.6 %copy-done.1 = bf16[256,4096]{1,0:T(8,128)(2,1)S(1)} copy-done((bf16[256,4096]{1,0:T(8,128)(2,1)S(1)}, bf16[256,4096]{1,0:T(8,128)(2,1)}, u32[]{:S(2)}) %copy-start.1) | copy-done | bytes 2097176
  77.5 1.0 copy-done.3
  78.6 1.0 copy-done.6
  79.7 8.2 %mid_blocks.1 = (bf16[512,1024]{1,0:T(8,128)(2,1)S(1)}, bf16[512,1024]{1,0:T(8,128)(2,1)S(1)}, f32[64,1024]{1,0:T(8,128)S(1)}, f32[64,1024]{1,0:T(8,128)S(1)}, f...) custom-call(s32[1]{0:T(128)} %bitcast.refs_0_, ...), custom_call_target="tpu_custom_call" | custom-call | flops 15000000512 | bytes 14680064 | tf_op jit(solution)/shard_map/mid_blocks/pallas_call | solution.py:257
  88.1 11.1 %leaf_blocks.1 = (f32[64,512]{1,0:T(8,128)S(1)}, f32[64,512]{1,0:T(8,128)S(1)}, f32[64,512]{1,0:T(8,128)S(1)}, f32[64,512]{1,0:T(8,128)S(1)}, f32[64,512]{1,0:T(...) custom-call(s32[1]{0:T(128)} %bitcast.refs_0_, ...), custom_call_target="tpu_custom_call" | custom-call | flops 20000000000 | bytes 20971520 | tf_op jit(solution)/shard_map/leaf_blocks/pallas_call | solution.py:279
  99.2 0.4 collective-permute-start.34
  99.7 2.0 %collective-permute-start.15 = (f32[32,1024]{1,0:T(8,128)S(1)}, f32[32,1024]{1,0:T(8,128)S(1)}, u32[]{:S(2)}, u32[]{:S(2)}) collective-permute-start(f32[32,1024]{1,0:T(8,128)S(1)} %get-tuple-element.58), channel_id=1, source_target_pairs={{0,4},{1,5},{4,8},{5,9},{8,12},{9,13},{12,14},{13,15},{14,10},{15,... | collective-permute-start | bytes 393224 | tf_op jit(solution)/shard_map/ppermute | solution.py:207
  101.7 3.7 %collective-permute-done.19 = f32[32,1024]{1,0:T(8,128)S(1)} collective-permute-done((f32[32,1024]{1,0:T(8,128)S(1)}, f32[32,1024]{1,0:T(8,128)S(1)}, u32[]{:S(2)}, u32[]{:S(2)}) %collective-permute-start.19) | collective-permute-done | bytes 131104 | tf_op jit(solution)/shard_map/ppermute | solution.py:208
  105.4 0.3 collective-permute-start.20
  105.7 1.9 %collective-permute-start.35 = (f32[32,512]{1,0:T(8,128)S(1)}, f32[32,512]{1,0:T(8,128)S(1)}, u32[]{:S(2)}, u32[]{:S(2)}) collective-permute-start(f32[32,512]{1,0:T(8,128)S(1)} %get-tuple-element.60), channel_id=1, source_target_pairs={{0,4},{1,5},{4,8},{5,9},{8,12},{9,13},{12,14},{13,15},{14,10},{15,... | collective-permute-start | bytes 196616 | tf_op jit(solution)/shard_map/ppermute | solution.py:207
  107.8 1.9 %collective-permute-start.16 = (f32[64,1024]{1,0:T(8,128)S(1)}, f32[64,1024]{1,0:T(8,128)S(1)}, u32[]{:S(2)}, u32[]{:S(2)}) collective-permute-start(f32[64,1024]{1,0:T(8,128)S(1)} %pad_add_fusion.1), channel_id=1, source_target_pairs={{0,4},{1,5},{4,8},{5,9},{8,12},{9,13},{12,14},{13,15},{14,10},{15,... | collective-permute-start | bytes 786440 | tf_op jit(solution)/shard_map/ppermute | solution.py:212
  109.7 0.9 collective-permute-done.35
  110.6 4.2 %collective-permute-done.39 = f32[32,512]{1,0:T(8,128)S(1)} collective-permute-done((f32[32,512]{1,0:T(8,128)S(1)}, f32[32,512]{1,0:T(8,128)S(1)}, u32[]{:S(2)}, u32[]{:S(2)}) %collective-permute-start.39) | collective-permute-done | bytes 65568 | tf_op jit(solution)/shard_map/ppermute | solution.py:208
  114.8 1.8 %collective-permute-start.36 = (f32[64,512]{1,0:T(8,128)S(1)}, f32[64,512]{1,0:T(8,128)S(1)}, u32[]{:S(2)}, u32[]{:S(2)}) collective-permute-start(f32[64,512]{1,0:T(8,128)S(1)} %get-tuple-element.56), channel_id=1, source_target_pairs={{0,4},{1,5},{4,8},{5,9},{8,12},{9,13},{12,14},{13,15},{14,10},{15,... | collective-permute-start | bytes 393224 | tf_op jit(solution)/shard_map/ppermute | solution.py:212
  116.6 0.3 collective-permute-start.40
  116.9 0.3 collective-permute-start.21
  117.2 1.9 %collective-permute-start.17 = (f32[64,1024]{1,0:T(8,128)S(1)}, f32[64,1024]{1,0:T(8,128)S(1)}, u32[]{:S(2)}, u32[]{:S(2)}) collective-permute-start(f32[64,1024]{1,0:T(8,128)S(1)} %add.87), channel_id=1, source_target_pairs={{0,4},{1,5},{4,8},{5,9},{8,12},{9,13},{12,14},{13,15},{14,10},{15,... | collective-permute-start | bytes 786440 | tf_op jit(solution)/shard_map/ppermute | solution.py:212
  119.1 2.1 %collective-permute-done.36 = f32[64,512]{1,0:T(8,128)S(1)} collective-permute-done((f32[64,512]{1,0:T(8,128)S(1)}, f32[64,512]{1,0:T(8,128)S(1)}, u32[]{:S(2)}, u32[]{:S(2)}) %collective-permute-start.36) | collective-permute-done | bytes 131104 | tf_op jit(solution)/shard_map/ppermute | solution.py:212
  121.2 1.9 %collective-permute-done.40 = f32[64,512]{1,0:T(8,128)S(1)} collective-permute-done((f32[64,512]{1,0:T(8,128)S(1)}, f32[64,512]{1,0:T(8,128)S(1)}, u32[]{:S(2)}, u32[]{:S(2)}) %collective-permute-start.40) | collective-permute-done | bytes 131104 | tf_op jit(solution)/shard_map/ppermute | solution.py:213
  123.1 1.8 %collective-permute-start.37 = (f32[64,512]{1,0:T(8,128)S(1)}, f32[64,512]{1,0:T(8,128)S(1)}, u32[]{:S(2)}, u32[]{:S(2)}) collective-permute-start(f32[64,512]{1,0:T(8,128)S(1)} %get-tuple-element.54), channel_id=1, source_target_pairs={{0,4},{1,5},{4,8},{5,9},{8,12},{9,13},{12,14},{13,15},{14,10},{15,... | collective-permute-start | bytes 393224 | tf_op jit(solution)/shard_map/ppermute | solution.py:212
  124.9 0.3 collective-permute-start.41
  125.2 3.5 %collective-permute-done.21 = f32[64,1024]{1,0:T(8,128)S(1)} collective-permute-done((f32[64,1024]{1,0:T(8,128)S(1)}, f32[64,1024]{1,0:T(8,128)S(1)}, u32[]{:S(2)}, u32[]{:S(2)}) %collective-permute-start.21) | collective-permute-done | bytes 262176 | tf_op jit(solution)/shard_map/ppermute | solution.py:213
  128.7 0.3 collective-permute-start.22
  129.1 1.8 %collective-permute-start.18 = (f32[64,1024]{1,0:T(8,128)S(1)}, f32[64,1024]{1,0:T(8,128)S(1)}, u32[]{:S(2)}, u32[]{:S(2)}) collective-permute-start(f32[64,1024]{1,0:T(8,128)S(1)} %add.88), channel_id=1, source_target_pairs={{0,4},{1,5},{4,8},{5,9},{8,12},{9,13},{12,14},{13,15},{14,10},{15,... | collective-permute-start | bytes 786440 | tf_op jit(solution)/shard_map/ppermute | solution.py:212
  130.9 0.6 collective-permute-done.41
  131.5 0.3 collective-permute-start.42
  131.9 1.7 %collective-permute-start.38 = (f32[64,512]{1,0:T(8,128)S(1)}, f32[64,512]{1,0:T(8,128)S(1)}, u32[]{:S(2)}, u32[]{:S(2)}) collective-permute-start(f32[64,512]{1,0:T(8,128)S(1)} %get-tuple-element.52), channel_id=1, source_target_pairs={{0,4},{1,5},{4,8},{5,9},{8,12},{9,13},{12,14},{13,15},{14,10},{15,... | collective-permute-start | bytes 393224 | tf_op jit(solution)/shard_map/ppermute | solution.py:212
  133.6 2.4 %collective-permute-done.22 = f32[64,1024]{1,0:T(8,128)S(1)} collective-permute-done((f32[64,1024]{1,0:T(8,128)S(1)}, f32[64,1024]{1,0:T(8,128)S(1)}, u32[]{:S(2)}, u32[]{:S(2)}) %collective-permute-start.22) | collective-permute-done | bytes 262176 | tf_op jit(solution)/shard_map/ppermute | solution.py:213
  136.0 0.8 add_add_fusion
  136.8 0.6 collective-permute-done.42
  137.4 0.7 fusion.8
  (90 shorter events, 1.2 us)
Async XLA Ops:
  0.6 15.2 %collective-permute-start.2 = (bf16[256,1024]{1,0:T(8,128)(2,1)}, bf16[256,1024]{1,0:T(8,128)(2,1)S(1)}, u32[]{:S(2)}, u32[]{:S(2)}) collective-permute-start(bf16[256,1024]{1,0:T(8,128)(2,1)} %refs_4_.1), channel_id=1, source_target_pairs={{0,2},{1,3},{4,0},{5,1},{8,4},{9,5},{12,8},{13,9},{14,12},{15,13},... | collective-permute-start | bytes 1572872 | tf_op jit(solution)/shard_map/ppermute | solution.py:244
  3.6 9.4 %collective-permute-start.4 = (bf16[320,512]{1,0:T(8,128)(2,1)}, bf16[320,512]{1,0:T(8,128)(2,1)S(1)}, u32[]{:S(2)}, u32[]{:S(2)}) collective-permute-start(bf16[320,512]{1,0:T(8,128)(2,1)} %refs_10_.1), channel_id=1, source_target_pairs={{0,4},{1,5},{4,8},{5,9},{8,12},{9,13},{12,14},{13,15},{14,10},{15,... | collective-permute-start | bytes 983048 | tf_op jit(solution)/shard_map/ppermute | solution.py:247
  15.8 8.9 %collective-permute-start.7 = (bf16[320,512]{1,0:T(8,128)(2,1)S(1)}, bf16[320,512]{1,0:T(8,128)(2,1)S(1)}, u32[]{:S(2)}, u32[]{:S(2)}) collective-permute-start(bf16[320,512]{1,0:T(8,128)(2,1)S(1)} %collective-permute-done.4.refs_12_), channel_id=1, source_target_pairs={{0,4},{1,5},{4,8},{5,9},{8,12},{9,13},{12,14},{13,15},{14,10},{15,... | collective-permute-start | bytes 983048 | tf_op jit(solution)/shard_map/ppermute | solution.py:247
  17.6 12.6 %collective-permute-start.5 = (bf16[256,1024]{1,0:T(8,128)(2,1)S(1)}, bf16[256,1024]{1,0:T(8,128)(2,1)}, u32[]{:S(2)}, u32[]{:S(2)}) collective-permute-start(bf16[256,1024]{1,0:T(8,128)(2,1)S(1)} %collective-permute-done.2.refs_5_), channel_id=1, source_target_pairs={{0,2},{1,3},{4,0},{5,1},{8,4},{9,5},{12,8},{13,9},{14,12},{15,13},... | collective-permute-start | bytes 1572872 | tf_op jit(solution)/shard_map/ppermute | solution.py:244
  17.9 48.7 %collective-permute-start = (bf16[256,4096]{1,0:T(8,128)(2,1)}, bf16[256,4096]{1,0:T(8,128)(2,1)S(1)}, u32[]{:S(2)}, u32[]{:S(2)}) collective-permute-start(bf16[256,4096]{1,0:T(8,128)(2,1)} %refs_2_.1), channel_id=1, source_target_pairs={{0,1},{1,0},{2,3},{3,2},{4,5},{5,4},{6,7},{7,6},{8,9},{9,8},{10,11... | collective-permute-start | bytes 6291464 | tf_op jit(solution)/shard_map/ppermute | solution.py:202
  24.7 8.1 %collective-permute-start.8 = (bf16[320,512]{1,0:T(8,128)(2,1)S(1)}, bf16[320,512]{1,0:T(8,128)(2,1)S(1)}, u32[]{:S(2)}, u32[]{:S(2)}) collective-permute-start(bf16[320,512]{1,0:T(8,128)(2,1)S(1)} %collective-permute-done.7.refs_14_), channel_id=1, source_target_pairs={{0,4},{1,5},{4,8},{5,9},{8,12},{9,13},{12,14},{13,15},{14,10},{15,... | collective-permute-start | bytes 983048 | tf_op jit(solution)/shard_map/ppermute | solution.py:247
  32.8 12.3 %copy-start.10 = (bf16[320,512]{1,0:T(8,128)(2,1)}, bf16[320,512]{1,0:T(8,128)(2,1)S(1)}, u32[]{:S(2)}) copy-start(bf16[320,512]{1,0:T(8,128)(2,1)S(1)} %collective-permute-done.8.refs_16_) | copy-start | bytes 983044
  32.8 7.9 %collective-permute-start.11 = (bf16[320,512]{1,0:T(8,128)(2,1)S(1)}, bf16[320,512]{1,0:T(8,128)(2,1)S(1)}, u32[]{:S(2)}, u32[]{:S(2)}) collective-permute-start(bf16[320,512]{1,0:T(8,128)(2,1)S(1)} %collective-permute-done.8.refs_16_), channel_id=1, source_target_pairs={{0,4},{1,5},{4,8},{5,9},{8,12},{9,13},{12,14},{13,15},{14,10},{15,... | collective-permute-start | bytes 983048 | tf_op jit(solution)/shard_map/ppermute | solution.py:247
  33.9 11.2 %collective-permute-start.9 = (bf16[256,1024]{1,0:T(8,128)(2,1)}, bf16[256,1024]{1,0:T(8,128)(2,1)}, u32[]{:S(2)}, u32[]{:S(2)}) collective-permute-start(bf16[256,1024]{1,0:T(8,128)(2,1)} %collective-permute-done.5.refs_7_), channel_id=1, source_target_pairs={{0,2},{1,3},{4,0},{5,1},{8,4},{9,5},{12,8},{13,9},{14,12},{15,13},... | collective-permute-start | bytes 1572872 | tf_op jit(solution)/shard_map/ppermute | solution.py:244
  40.7 4.4 %copy-start.12 = (bf16[320,512]{1,0:T(8,128)(2,1)}, bf16[320,512]{1,0:T(8,128)(2,1)S(1)}, u32[]{:S(2)}) copy-start(bf16[320,512]{1,0:T(8,128)(2,1)S(1)} %collective-permute-done.11.refs_18_) | copy-start | bytes 983044
  40.7 7.1 %collective-permute-start.12 = (bf16[320,512]{1,0:T(8,128)(2,1)S(1)}, bf16[320,512]{1,0:T(8,128)(2,1)S(1)}, u32[]{:S(2)}, u32[]{:S(2)}) collective-permute-start(bf16[320,512]{1,0:T(8,128)(2,1)S(1)} %collective-permute-done.11.refs_18_), channel_id=1, source_target_pairs={{0,4},{1,5},{4,8},{5,9},{8,12},{9,13},{12,14},{13,15},{14,10},{15,... | collective-permute-start | bytes 983048 | tf_op jit(solution)/shard_map/ppermute | solution.py:247
  42.1 8.9 %collective-permute-start.1 = (bf16[256,1024]{1,0:T(8,128)(2,1)}, bf16[256,1024]{1,0:T(8,128)(2,1)S(1)}, u32[]{:S(2)}, u32[]{:S(2)}) collective-permute-start(bf16[256,1024]{1,0:T(8,128)(2,1)} %refs_4_.1), channel_id=1, source_target_pairs={{0,1},{1,0},{2,3},{3,2},{4,5},{5,4},{6,7},{7,6},{8,9},{9,8},{10,11... | collective-permute-start | bytes 1572872 | tf_op jit(solution)/shard_map/ppermute | solution.py:202
  42.1 7.7 %collective-permute-start.24 = (bf16[320,512]{1,0:T(8,128)(2,1)}, bf16[320,512]{1,0:T(8,128)(2,1)S(1)}, u32[]{:S(2)}, u32[]{:S(2)}) collective-permute-start(bf16[320,512]{1,0:T(8,128)(2,1)} %refs_10_.1), channel_id=1, source_target_pairs={{0,1},{1,0},{2,3},{3,2},{4,5},{5,4},{6,7},{7,6},{8,9},{9,8},{10,11... | collective-permute-start | bytes 983048 | tf_op jit(solution)/shard_map/ppermute | solution.py:202
  45.1 2.7 %collective-permute-start.23 = (bf16[64,1024]{1,0:T(8,128)(2,1)}, bf16[64,1024]{1,0:T(8,128)(2,1)S(1)}, u32[]{:S(2)}, u32[]{:S(2)}) collective-permute-start(bf16[64,1024]{1,0:T(8,128)(2,1)} %refs_6_.1), channel_id=1, source_target_pairs={{0,1},{1,0},{2,3},{3,2},{4,5},{5,4},{6,7},{7,6},{8,9},{9,8},{10,11... | collective-permute-start | bytes 393224 | tf_op jit(solution)/shard_map/ppermute | solution.py:202
  47.8 8.6 %copy-start.14 = (bf16[320,512]{1,0:T(8,128)(2,1)}, bf16[320,512]{1,0:T(8,128)(2,1)S(1)}, u32[]{:S(2)}) copy-start(bf16[320,512]{1,0:T(8,128)(2,1)S(1)} %collective-permute-done.12.refs_20_) | copy-start | bytes 983044
  47.8 7.7 %collective-permute-start.3 = (bf16[256,1024]{1,0:T(8,128)(2,1)S(1)}, bf16[256,1024]{1,0:T(8,128)(2,1)S(1)}, u32[]{:S(2)}, u32[]{:S(2)}) collective-permute-start(bf16[256,1024]{1,0:T(8,128)(2,1)S(1)} %collective-permute-done.2.refs_5_), channel_id=1, source_target_pairs={{0,1},{1,0},{2,3},{3,2},{4,5},{5,4},{6,7},{7,6},{8,9},{9,8},{10,11... | collective-permute-start | bytes 1572872 | tf_op jit(solution)/shard_map/ppermute | solution.py:202
  48.5 16.5 %collective-permute-start.13 = (bf16[256,1024]{1,0:T(8,128)(2,1)}, bf16[256,1024]{1,0:T(8,128)(2,1)}, u32[]{:S(2)}, u32[]{:S(2)}) collective-permute-start(bf16[256,1024]{1,0:T(8,128)(2,1)} %collective-permute-done.9.refs_9_), channel_id=1, source_target_pairs={{4,0},{5,1},{8,4},{9,5},{12,8},{13,9},{14,12},{15,13},{20,16},{21,... | collective-permute-start | bytes 1572872 | tf_op jit(solution)/shard_map/ppermute | solution.py:252
  50.5 1.7 %collective-permute-start.25 = (bf16[320,512]{1,0:T(8,128)(2,1)S(1)}, bf16[320,512]{1,0:T(8,128)(2,1)S(1)}, u32[]{:S(2)}, u32[]{:S(2)}) collective-permute-start(bf16[320,512]{1,0:T(8,128)(2,1)S(1)} %collective-permute-done.4.refs_12_), channel_id=1, source_target_pairs={{0,1},{1,0},{2,3},{3,2},{4,5},{5,4},{6,7},{7,6},{8,9},{9,8},{10,11... | collective-permute-start | bytes 983048 | tf_op jit(solution)/shard_map/ppermute | solution.py:202
  51.0 5.3 %collective-permute-start.26 = (bf16[320,512]{1,0:T(8,128)(2,1)S(1)}, bf16[320,512]{1,0:T(8,128)(2,1)S(1)}, u32[]{:S(2)}, u32[]{:S(2)}) collective-permute-start(bf16[320,512]{1,0:T(8,128)(2,1)S(1)} %collective-permute-done.7.refs_14_), channel_id=1, source_target_pairs={{0,1},{1,0},{2,3},{3,2},{4,5},{5,4},{6,7},{7,6},{8,9},{9,8},{10,11... | collective-permute-start | bytes 983048 | tf_op jit(solution)/shard_map/ppermute | solution.py:202
  53.0 12.0 %collective-permute-start.30 = (bf16[320,512]{1,0:T(8,128)(2,1)S(1)}, bf16[320,512]{1,0:T(8,128)(2,1)}, u32[]{:S(2)}, u32[]{:S(2)}) collective-permute-start(bf16[320,512]{1,0:T(8,128)(2,1)S(1)} %collective-permute-done.12.refs_20_), channel_id=1, source_target_pairs={{0,4},{1,5},{4,8},{5,9},{8,12},{9,13},{12,14},{13,15},{14,10},{15,... | collective-permute-start | bytes 983048 | tf_op jit(solution)/shard_map/ppermute | solution.py:247
  55.5 0.8 copy-start.5
  56.3 10.1 %collective-permute-start.6 = (bf16[256,1024]{1,0:T(8,128)(2,1)}, bf16[256,1024]{1,0:T(8,128)(2,1)}, u32[]{:S(2)}, u32[]{:S(2)}) collective-permute-start(bf16[256,1024]{1,0:T(8,128)(2,1)} %collective-permute-done.5.refs_7_), channel_id=1, source_target_pairs={{0,1},{1,0},{2,3},{3,2},{4,5},{5,4},{6,7},{7,6},{8,9},{9,8},{10,11... | collective-permute-start | bytes 1572872 | tf_op jit(solution)/shard_map/ppermute | solution.py:202
  57.1 9.8 %collective-permute-start.10 = (bf16[256,1024]{1,0:T(8,128)(2,1)}, bf16[256,1024]{1,0:T(8,128)(2,1)}, u32[]{:S(2)}, u32[]{:S(2)}) collective-permute-start(bf16[256,1024]{1,0:T(8,128)(2,1)} %collective-permute-done.9.refs_9_), channel_id=1, source_target_pairs={{0,1},{1,0},{2,3},{3,2},{4,5},{5,4},{6,7},{7,6},{8,9},{9,8},{10,11... | collective-permute-start | bytes 1572872 | tf_op jit(solution)/shard_map/ppermute | solution.py:202
  65.0 10.5 %collective-permute-start.14 = (bf16[256,1024]{1,0:T(8,128)(2,1)}, bf16[256,1024]{1,0:T(8,128)(2,1)}, u32[]{:S(2)}, u32[]{:S(2)}) collective-permute-start(bf16[256,1024]{1,0:T(8,128)(2,1)} %collective-permute-done.13.refs_11_), channel_id=1, source_target_pairs={{0,1},{1,0},{2,3},{3,2},{4,5},{5,4},{6,7},{7,6},{8,9},{9,8},{10,11... | collective-permute-start | bytes 1572872 | tf_op jit(solution)/shard_map/ppermute | solution.py:202
  65.0 10.4 %collective-permute-start.32 = (bf16[320,512]{1,0:T(8,128)(2,1)}, bf16[320,512]{1,0:T(8,128)(2,1)}, u32[]{:S(2)}, u32[]{:S(2)}) collective-permute-start(bf16[320,512]{1,0:T(8,128)(2,1)} %collective-permute-done.30.refs_22_), channel_id=1, source_target_pairs={{0,4},{1,5},{4,8},{5,9},{8,12},{9,13},{12,14},{13,15},{14,10},{15,... | collective-permute-start | bytes 983048 | tf_op jit(solution)/shard_map/ppermute | solution.py:247
  66.4 21.6 %collective-permute-start.27 = (bf16[320,512]{1,0:T(8,128)(2,1)}, bf16[320,512]{1,0:T(8,128)(2,1)S(1)}, u32[]{:S(2)}, u32[]{:S(2)}) collective-permute-start(bf16[320,512]{1,0:T(8,128)(2,1)} %copy-done.10), channel_id=1, source_target_pairs={{0,1},{1,0},{2,3},{3,2},{4,5},{5,4},{6,7},{7,6},{8,9},{9,8},{10,11... | collective-permute-start | bytes 983048 | tf_op jit(solution)/shard_map/ppermute | solution.py:202
  66.6 21.3 %collective-permute-start.28 = (bf16[320,512]{1,0:T(8,128)(2,1)}, bf16[320,512]{1,0:T(8,128)(2,1)S(1)}, u32[]{:S(2)}, u32[]{:S(2)}) collective-permute-start(bf16[320,512]{1,0:T(8,128)(2,1)} %copy-done.12), channel_id=1, source_target_pairs={{0,1},{1,0},{2,3},{3,2},{4,5},{5,4},{6,7},{7,6},{8,9},{9,8},{10,11... | collective-permute-start | bytes 983048 | tf_op jit(solution)/shard_map/ppermute | solution.py:202
  66.9 21.1 %collective-permute-start.29 = (bf16[320,512]{1,0:T(8,128)(2,1)}, bf16[320,512]{1,0:T(8,128)(2,1)S(1)}, u32[]{:S(2)}, u32[]{:S(2)}) collective-permute-start(bf16[320,512]{1,0:T(8,128)(2,1)} %copy-done.14), channel_id=1, source_target_pairs={{0,1},{1,0},{2,3},{3,2},{4,5},{5,4},{6,7},{7,6},{8,9},{9,8},{10,11... | collective-permute-start | bytes 983048 | tf_op jit(solution)/shard_map/ppermute | solution.py:202
  75.4 12.6 %collective-permute-start.31 = (bf16[320,512]{1,0:T(8,128)(2,1)}, bf16[320,512]{1,0:T(8,128)(2,1)S(1)}, u32[]{:S(2)}, u32[]{:S(2)}) collective-permute-start(bf16[320,512]{1,0:T(8,128)(2,1)} %collective-permute-done.30.refs_22_), channel_id=1, source_target_pairs={{0,1},{1,0},{2,3},{3,2},{4,5},{5,4},{6,7},{7,6},{8,9},{9,8},{10,11... | collective-permute-start | bytes 983048 | tf_op jit(solution)/shard_map/ppermute | solution.py:202
  75.4 12.6 %collective-permute-start.33 = (bf16[320,512]{1,0:T(8,128)(2,1)}, bf16[320,512]{1,0:T(8,128)(2,1)S(1)}, u32[]{:S(2)}, u32[]{:S(2)}) collective-permute-start(bf16[320,512]{1,0:T(8,128)(2,1)} %collective-permute-done.32.refs_24_), channel_id=1, source_target_pairs={{0,1},{1,0},{2,3},{3,2},{4,5},{5,4},{6,7},{7,6},{8,9},{9,8},{10,11... | collective-permute-start | bytes 983048 | tf_op jit(solution)/shard_map/ppermute | solution.py:202
  75.9 1.6 %copy-start.1 = (bf16[256,4096]{1,0:T(8,128)(2,1)S(1)}, bf16[256,4096]{1,0:T(8,128)(2,1)}, u32[]{:S(2)}) copy-start(bf16[256,4096]{1,0:T(8,128)(2,1)} %refs_2_.1) | copy-start | bytes 6291460
  77.5 1.0 copy-start.3
  78.6 1.0 copy-start.6
  79.6 8.4 %copy-start = (bf16[64,1024]{1,0:T(8,128)(2,1)S(1)}, bf16[64,1024]{1,0:T(8,128)(2,1)}, u32[]{:S(2)}) copy-start(bf16[64,1024]{1,0:T(8,128)(2,1)} %refs_6_.1) | copy-start | bytes 393220
  79.6 8.4 %copy-start.2 = (bf16[256,4096]{1,0:T(8,128)(2,1)S(1)}, bf16[256,4096]{1,0:T(8,128)(2,1)}, u32[]{:S(2)}) copy-start(bf16[256,4096]{1,0:T(8,128)(2,1)} %refs_2_.1) | copy-start | bytes 6291460
  79.6 8.4 %copy-start.4 = (bf16[256,1024]{1,0:T(8,128)(2,1)S(1)}, bf16[256,1024]{1,0:T(8,128)(2,1)}, u32[]{:S(2)}) copy-start(bf16[256,1024]{1,0:T(8,128)(2,1)} %refs_4_.1) | copy-start | bytes 1572868
  79.6 8.4 %copy-start.7 = (bf16[320,512]{1,0:T(8,128)(2,1)S(1)}, bf16[320,512]{1,0:T(8,128)(2,1)}, u32[]{:S(2)}) copy-start(bf16[320,512]{1,0:T(8,128)(2,1)} %refs_10_.1) | copy-start | bytes 983044
  79.6 8.4 %copy-start.9 = (bf16[320,512]{1,0:T(8,128)(2,1)S(1)}, bf16[320,512]{1,0:T(8,128)(2,1)}, u32[]{:S(2)}) copy-start(bf16[320,512]{1,0:T(8,128)(2,1)} %copy-done.8) | copy-start | bytes 983044
  79.6 8.4 %copy-start.11 = (bf16[320,512]{1,0:T(8,128)(2,1)S(1)}, bf16[320,512]{1,0:T(8,128)(2,1)}, u32[]{:S(2)}) copy-start(bf16[320,512]{1,0:T(8,128)(2,1)} %copy-done.10) | copy-start | bytes 983044
  79.6 8.4 %copy-start.13 = (bf16[320,512]{1,0:T(8,128)(2,1)S(1)}, bf16[320,512]{1,0:T(8,128)(2,1)}, u32[]{:S(2)}) copy-start(bf16[320,512]{1,0:T(8,128)(2,1)} %copy-done.12) | copy-start | bytes 983044
  79.6 8.4 %copy-start.15 = (bf16[320,512]{1,0:T(8,128)(2,1)S(1)}, bf16[320,512]{1,0:T(8,128)(2,1)}, u32[]{:S(2)}) copy-start(bf16[320,512]{1,0:T(8,128)(2,1)} %copy-done.14) | copy-start | bytes 983044
  79.7 8.4 %copy-start.17 = (bf16[320,512]{1,0:T(8,128)(2,1)S(1)}, bf16[320,512]{1,0:T(8,128)(2,1)}, u32[]{:S(2)}) copy-start(bf16[320,512]{1,0:T(8,128)(2,1)} %copy-done.16) | copy-start | bytes 983044
  79.7 8.4 %copy-start.19 = (bf16[320,512]{1,0:T(8,128)(2,1)S(1)}, bf16[320,512]{1,0:T(8,128)(2,1)}, u32[]{:S(2)}) copy-start(bf16[320,512]{1,0:T(8,128)(2,1)} %copy-done.18) | copy-start | bytes 983044
  79.7 8.4 %copy-start.21 = (bf16[320,512]{1,0:T(8,128)(2,1)S(1)}, bf16[320,512]{1,0:T(8,128)(2,1)}, u32[]{:S(2)}) copy-start(bf16[320,512]{1,0:T(8,128)(2,1)} %copy-done.20) | copy-start | bytes 983044
  79.7 8.4 %copy-start.23 = (bf16[64,1024]{1,0:T(8,128)(2,1)S(1)}, bf16[64,1024]{1,0:T(8,128)(2,1)}, u32[]{:S(2)}) copy-start(bf16[64,1024]{1,0:T(8,128)(2,1)} %copy-done.22) | copy-start | bytes 393220
  79.7 8.4 %copy-start.24 = (s32[2,80]{1,0:T(2,128)S(1)}, s32[2,80]{1,0:T(2,128)}, u32[]{:S(2)}) copy-start(s32[2,80]{1,0:T(2,128)} %refs_1_.3) | copy-start | bytes 1924
  99.2 6.4 %collective-permute-start.34 = (f32[512,512]{1,0:T(8,128)S(1)}, f32[512,512]{1,0:T(8,128)S(1)}, u32[]{:S(2)}, u32[]{:S(2)}) collective-permute-start(f32[512,512]{1,0:T(8,128)S(1)} %get-tuple-element.44), channel_id=1, source_target_pairs={{0,1},{1,0},{2,3},{3,2},{4,5},{5,4},{6,7},{7,6},{8,9},{9,8},{10,11... | collective-permute-start | bytes 3145736 | tf_op jit(solution)/shard_map/ppermute | solution.py:202
  99.6 5.7 %collective-permute-start.19 = (f32[32,1024]{1,0:T(8,128)S(1)}, f32[32,1024]{1,0:T(8,128)S(1)}, u32[]{:S(2)}, u32[]{:S(2)}) collective-permute-start(f32[32,1024]{1,0:T(8,128)S(1)} %get-tuple-element.59), channel_id=1, source_target_pairs={{0,2},{1,3},{4,0},{5,1},{8,4},{9,5},{12,8},{13,9},{14,12},{15,13},... | collective-permute-start | bytes 393224 | tf_op jit(solution)/shard_map/ppermute | solution.py:208
  99.7 8.1 %collective-permute-start.15 = (f32[32,1024]{1,0:T(8,128)S(1)}, f32[32,1024]{1,0:T(8,128)S(1)}, u32[]{:S(2)}, u32[]{:S(2)}) collective-permute-start(f32[32,1024]{1,0:T(8,128)S(1)} %get-tuple-element.58), channel_id=1, source_target_pairs={{0,4},{1,5},{4,8},{5,9},{8,12},{9,13},{12,14},{13,15},{14,10},{15,... | collective-permute-start | bytes 393224 | tf_op jit(solution)/shard_map/ppermute | solution.py:207
  105.4 11.5 %collective-permute-start.20 = (f32[64,1024]{1,0:T(8,128)S(1)}, f32[64,1024]{1,0:T(8,128)S(1)}, u32[]{:S(2)}, u32[]{:S(2)}) collective-permute-start(f32[64,1024]{1,0:T(8,128)S(1)} %pad_add_fusion), channel_id=1, source_target_pairs={{0,2},{1,3},{4,0},{5,1},{8,4},{9,5},{12,8},{13,9},{14,12},{15,13},... | collective-permute-start | bytes 786440 | tf_op jit(solution)/shard_map/ppermute | solution.py:213
  105.7 4.9 %collective-permute-start.35 = (f32[32,512]{1,0:T(8,128)S(1)}, f32[32,512]{1,0:T(8,128)S(1)}, u32[]{:S(2)}, u32[]{:S(2)}) collective-permute-start(f32[32,512]{1,0:T(8,128)S(1)} %get-tuple-element.60), channel_id=1, source_target_pairs={{0,4},{1,5},{4,8},{5,9},{8,12},{9,13},{12,14},{13,15},{14,10},{15,... | collective-permute-start | bytes 196616 | tf_op jit(solution)/shard_map/ppermute | solution.py:207
  107.6 7.2 %collective-permute-start.39 = (f32[32,512]{1,0:T(8,128)S(1)}, f32[32,512]{1,0:T(8,128)S(1)}, u32[]{:S(2)}, u32[]{:S(2)}) collective-permute-start(f32[32,512]{1,0:T(8,128)S(1)} %get-tuple-element.61), channel_id=1, source_target_pairs={{0,2},{1,3},{4,0},{5,1},{8,4},{9,5},{12,8},{13,9},{14,12},{15,13},... | collective-permute-start | bytes 196616 | tf_op jit(solution)/shard_map/ppermute | solution.py:208
  107.8 9.4 %collective-permute-start.16 = (f32[64,1024]{1,0:T(8,128)S(1)}, f32[64,1024]{1,0:T(8,128)S(1)}, u32[]{:S(2)}, u32[]{:S(2)}) collective-permute-start(f32[64,1024]{1,0:T(8,128)S(1)} %pad_add_fusion.1), channel_id=1, source_target_pairs={{0,4},{1,5},{4,8},{5,9},{8,12},{9,13},{12,14},{13,15},{14,10},{15,... | collective-permute-start | bytes 786440 | tf_op jit(solution)/shard_map/ppermute | solution.py:212
  114.8 6.3 %collective-permute-start.36 = (f32[64,512]{1,0:T(8,128)S(1)}, f32[64,512]{1,0:T(8,128)S(1)}, u32[]{:S(2)}, u32[]{:S(2)}) collective-permute-start(f32[64,512]{1,0:T(8,128)S(1)} %get-tuple-element.56), channel_id=1, source_target_pairs={{0,4},{1,5},{4,8},{5,9},{8,12},{9,13},{12,14},{13,15},{14,10},{15,... | collective-permute-start | bytes 393224 | tf_op jit(solution)/shard_map/ppermute | solution.py:212
  116.6 6.4 %collective-permute-start.40 = (f32[64,512]{1,0:T(8,128)S(1)}, f32[64,512]{1,0:T(8,128)S(1)}, u32[]{:S(2)}, u32[]{:S(2)}) collective-permute-start(f32[64,512]{1,0:T(8,128)S(1)} %get-tuple-element.57), channel_id=1, source_target_pairs={{0,2},{1,3},{4,0},{5,1},{8,4},{9,5},{12,8},{13,9},{14,12},{15,13},... | collective-permute-start | bytes 393224 | tf_op jit(solution)/shard_map/ppermute | solution.py:213
  116.9 11.7 %collective-permute-start.21 = (f32[64,1024]{1,0:T(8,128)S(1)}, f32[64,1024]{1,0:T(8,128)S(1)}, u32[]{:S(2)}, u32[]{:S(2)}) collective-permute-start(f32[64,1024]{1,0:T(8,128)S(1)} %add.91), channel_id=1, source_target_pairs={{0,2},{1,3},{4,0},{5,1},{8,4},{9,5},{12,8},{13,9},{14,12},{15,13},... | collective-permute-start | bytes 786440 | tf_op jit(solution)/shard_map/ppermute | solution.py:213
  117.2 11.8 %collective-permute-start.17 = (f32[64,1024]{1,0:T(8,128)S(1)}, f32[64,1024]{1,0:T(8,128)S(1)}, u32[]{:S(2)}, u32[]{:S(2)}) collective-permute-start(f32[64,1024]{1,0:T(8,128)S(1)} %add.87), channel_id=1, source_target_pairs={{0,4},{1,5},{4,8},{5,9},{8,12},{9,13},{12,14},{13,15},{14,10},{15,... | collective-permute-start | bytes 786440 | tf_op jit(solution)/shard_map/ppermute | solution.py:212
  123.1 14.3 %copy-start.25 = (bf16[64,512]{1,0:T(8,128)(2,1)S(1)}, bf16[64,512]{1,0:T(8,128)(2,1)}, u32[]{:S(2)}) copy-start(bf16[64,512]{1,0:T(8,128)(2,1)} %param.10) | copy-start | bytes 196612
  123.1 7.8 %collective-permute-start.37 = (f32[64,512]{1,0:T(8,128)S(1)}, f32[64,512]{1,0:T(8,128)S(1)}, u32[]{:S(2)}, u32[]{:S(2)}) collective-permute-start(f32[64,512]{1,0:T(8,128)S(1)} %get-tuple-element.54), channel_id=1, source_target_pairs={{0,4},{1,5},{4,8},{5,9},{8,12},{9,13},{12,14},{13,15},{14,10},{15,... | collective-permute-start | bytes 393224 | tf_op jit(solution)/shard_map/ppermute | solution.py:212
  124.9 6.6 %collective-permute-start.41 = (f32[64,512]{1,0:T(8,128)S(1)}, f32[64,512]{1,0:T(8,128)S(1)}, u32[]{:S(2)}, u32[]{:S(2)}) collective-permute-start(f32[64,512]{1,0:T(8,128)S(1)} %get-tuple-element.55), channel_id=1, source_target_pairs={{0,2},{1,3},{4,0},{5,1},{8,4},{9,5},{12,8},{13,9},{14,12},{15,13},... | collective-permute-start | bytes 393224 | tf_op jit(solution)/shard_map/ppermute | solution.py:213
  128.7 7.3 %collective-permute-start.22 = (f32[64,1024]{1,0:T(8,128)S(1)}, f32[64,1024]{1,0:T(8,128)S(1)}, u32[]{:S(2)}, u32[]{:S(2)}) collective-permute-start(f32[64,1024]{1,0:T(8,128)S(1)} %add.92), channel_id=1, source_target_pairs={{0,2},{1,3},{4,0},{5,1},{8,4},{9,5},{12,8},{13,9},{14,12},{15,13},... | collective-permute-start | bytes 786440 | tf_op jit(solution)/shard_map/ppermute | solution.py:213
  129.1 6.9 %collective-permute-start.18 = (f32[64,1024]{1,0:T(8,128)S(1)}, f32[64,1024]{1,0:T(8,128)S(1)}, u32[]{:S(2)}, u32[]{:S(2)}) collective-permute-start(f32[64,1024]{1,0:T(8,128)S(1)} %add.88), channel_id=1, source_target_pairs={{0,4},{1,5},{4,8},{5,9},{8,12},{9,13},{12,14},{13,15},{14,10},{15,... | collective-permute-start | bytes 786440 | tf_op jit(solution)/shard_map/ppermute | solution.py:212
  131.5 5.9 %collective-permute-start.42 = (f32[64,512]{1,0:T(8,128)S(1)}, f32[64,512]{1,0:T(8,128)S(1)}, u32[]{:S(2)}, u32[]{:S(2)}) collective-permute-start(f32[64,512]{1,0:T(8,128)S(1)} %get-tuple-element.53), channel_id=1, source_target_pairs={{0,2},{1,3},{4,0},{5,1},{8,4},{9,5},{12,8},{13,9},{14,12},{15,13},... | collective-permute-start | bytes 393224 | tf_op jit(solution)/shard_map/ppermute | solution.py:213
  131.9 5.5 %collective-permute-start.38 = (f32[64,512]{1,0:T(8,128)S(1)}, f32[64,512]{1,0:T(8,128)S(1)}, u32[]{:S(2)}, u32[]{:S(2)}) collective-permute-start(f32[64,512]{1,0:T(8,128)S(1)} %get-tuple-element.52), channel_id=1, source_target_pairs={{0,4},{1,5},{4,8},{5,9},{8,12},{9,13},{12,14},{13,15},{14,10},{15,... | collective-permute-start | bytes 393224 | tf_op jit(solution)/shard_map/ppermute | solution.py:212
  (5 other events, 3.6 us)

commit v2 on v1

--- a/solution.py
+++ b/solution.py
@@ -38,44 +38,70 @@
     return jnp.where(2 * place < chips, 2 * place, 2 * (chips - 1 - place) + 1) if snake else place
 
 
-def mid_kernel(chips, snake, *refs):
+def fetch(copies, source, target, sems):
+    copies.append(pltpu.make_async_copy(source, target, sems.at[len(copies)]))
+    copies[-1].start()
+
+
+def fetch_columns(copies, a_refs, first, rows, target, at, sems):
+    lane = pl.multiple_of(first, rows)
+    for k in range(2):
+        into = target.at[k * rows : (k + 1) * rows, at : at + rows]
+        fetch(copies, a_refs[k].at[:, pl.ds(lane, rows)], into, sems)
+
+
+def near_kernel(chips, snake, *refs):
     half = chips // 2
-    device_ref, a_refs, f_refs = refs[0], refs[1:3], refs[3 : 3 + 2 * (half + 1)]
-    high_ref, low_ref = refs[5 + 2 * half : 7 + 2 * half]
-    y_refs = refs[7 + 2 * half : 7 + 2 * half + chips]
-    left, right, turned, picked, stacked, sems = refs[7 + 2 * half + chips :]
+    device_ref, a_refs, f_refs = refs[0], refs[1:3], refs[3 : 3 + 2 * half]
+    cross_ref, left, right, sems = refs[3 + 2 * half :]
     device = device_ref[0]
     chip, core = device // 2, device % 2
     place = place_of(chip, chips, snake)
     rows = f_refs[0].shape[0]
-    mid = f_refs[0].shape[1]
     copies = []
-    for step in range(half + 1):
+    for step in range(half):
         owner = chip_at(place + step, chips, snake)
         for side in range(2):
-            lane = pl.multiple_of((2 * owner + (core if side == 0 else 1 - core)) * rows, rows)
             at = (2 * step + side) * rows
-            for k in range(2):
-                source, target = a_refs[k].at[:, pl.ds(lane, rows)], left.at[k * rows : (k + 1) * rows, at : at + rows]
-                copies.append(pltpu.make_async_copy(source, target, sems.at[len(copies)]))
-            source, target = f_refs[2 * step + side], right.at[at : at + rows, :]
-            copies.append(pltpu.make_async_copy(source, target, sems.at[len(copies)]))
+            fetch_columns(copies, a_refs, (2 * owner + (core if side == 0 else 1 - core)) * rows, rows, left, at, sems)
+            fetch(copies, f_refs[2 * step + side], right.at[at : at + rows, :], sems)
+    for copy in copies[:6]:
+        copy.wait()
+    left[:, : 2 * rows] = left[:, : 2 * rows] * jnp.bfloat16(0.5)
+    cut = 2 * rows * (half // 2)
+    for copy in copies[6 : 6 * (half // 2)]:
+        copy.wait()
+    cross = mm(left[:, :cut], right[:cut, :])
+    for copy in copies[6 * (half // 2) :]:
+        copy.wait()
+    cross_ref[...] = cross + mm(left[:, cut:], right[cut:, :])
+
+
+def mid_kernel(chips, snake, *refs):
+    half = chips // 2
+    device_ref, a_refs, own_refs, far_refs, cross_ref = refs[0], refs[1:3], refs[3:5], refs[5:7], refs[7]
+    high_ref, low_ref = refs[8:10]
+    y_refs, up_ref, down_ref = refs[10 : 10 + chips], refs[10 + chips], refs[11 + chips]
+    left, right, own, cross, turned, picked, stacked, sems = refs[12 + chips :]
+    device = device_ref[0]
+    chip, core = device // 2, device % 2
+    place = place_of(chip, chips, snake)
+    rows, mid = own_refs[0].shape
+    copies = []
+    fetch(copies, cross_ref, cross, sems)
+    for side in range(2):
+        fetch(copies, own_refs[side], own.at[side * rows : (side + 1) * rows, :], sems)
+    owner = chip_at(place + half, chips, snake)
+    for side in range(2):
+        lane = (2 * owner + (core if side == 0 else 1 - core)) * rows
+        fetch_columns(copies, a_refs, lane, rows, left, side * rows, sems)
+        fetch(copies, far_refs[side], right.at[side * rows : (side + 1) * rows, :], sems)
     for copy in copies:
-        copy.start()
-    for copy in copies[:6]:
-        copy.wait()
-    near = 2 * rows
-    left[:, :near] = left[:, :near] * jnp.bfloat16(0.5)
-    far = near + 2 * rows * (half // 2)
-    for copy in copies[6 : 6 * (1 + half // 2)]:
-        copy.wait()
-    cross = mm(left[:, :far], right[:far, :])
-    for copy in copies[6 * (1 + half // 2) :]:
-        copy.wait()
-    high, low = split(cross + mm(left[:, far:], right[far:, :]))
+        copy.wait()
+    factor = own[...]
+    high, low = split(cross[...] + mm(left[...], right[...]))
     high_ref[...] = high
     low_ref[...] = low
-    factor = right[: 2 * rows, :]
     for k, x in enumerate((factor, high, low)):
         turned[k * mid : (k + 1) * mid, :] = x.T
     stacked[: 2 * rows, :] = high
@@ -92,6 +118,8 @@
     y = mm(picked[...], stacked[...])
     for s in range(chips):
         y_refs[s][...] = y[s * strip : (s + 1) * strip, :]
+    up_ref[...] = y[half * strip : half * strip + strip // 2, :]
+    down_ref[...] = y[half * strip + strip // 2 : (half + 1) * strip, :]
 
 
 def leaf_kernel(chips, snake, *refs):
@@ -111,21 +139,18 @@
     strip = d_refs[0].shape[0]
     copies = []
 
-    def fetch(source, target):
-        copies.append(pltpu.make_async_copy(source, target, sems.at[len(copies)]))
-        copies[-1].start()
-
     for k in range(2):
-        fetch(f_refs[k], factors.at[k * rows : (k + 1) * rows, :])
-        fetch(d_refs[k], diags.at[k * strip : (k + 1) * strip, :])
-    fetch(high_ref, highs)
-    fetch(low_ref, lows)
+        fetch(copies, f_refs[k], factors.at[k * rows : (k + 1) * rows, :], sems)
+        fetch(copies, d_refs[k], diags.at[k * strip : (k + 1) * strip, :], sems)
+    fetch(copies, high_ref, highs, sems)
+    fetch(copies, low_ref, lows, sems)
     early = len(copies)
     for step in range(half + 1):
         lane = pl.multiple_of(chip_at(place + step, chips, snake) * chip_rows, chip_rows)
         at = step * chip_rows
         for k in range(2):
-            fetch(a_refs[k].at[:, pl.ds(lane, chip_rows)], left.at[k * rows : (k + 1) * rows, at : at + chip_rows])
+            into = left.at[k * rows : (k + 1) * rows, at : at + chip_rows]
+            fetch(copies, a_refs[k].at[:, pl.ds(lane, chip_rows)], into, sems)
     wide[...] = jnp.zeros_like(wide)
     for slot in range(chips):
         source = chip_at(place + chips - slot, chips, snake)
@@ -201,26 +226,55 @@
     def swap(x):
         return lax.ppermute(x, "row", swap_pairs)
 
-    def ring_sum(terms):
-        far = terms[half]
-        cut = far.shape[0] // 2
-        up = lax.ppermute(far[:cut], "row", perm(1))
-        down = lax.ppermute(far[cut:], "row", perm(-1))
-        up = terms[half - 1] + jnp.pad(up, ((0, cut), (0, 0)))
-        down = terms[half + 1] + jnp.pad(down, ((cut, 0), (0, 0)))
-        for s in range(half - 1, 0, -1):
-            up = lax.ppermute(up, "row", perm(1))
-            down = lax.ppermute(down, "row", perm(-1))
-            if s > 1:
-                up = up + terms[s - 1]
-                down = down + terms[chips - s + 1]
-        return terms[0] + up + down
+    def tie(x, *others):
+        return lax.optimization_barrier((x, *others))[0] if others else x
+
+    def ring_start(up, down):
+        return lax.ppermute(up, "row", perm(1)), lax.ppermute(down, "row", perm(-1))
+
+    def ring_next(terms, first):
+        cut = first[0].shape[0]
+        up = terms[half - 1] + jnp.pad(first[0], ((0, cut), (0, 0)))
+        down = terms[half + 1] + jnp.pad(first[1], ((cut, 0), (0, 0)))
+        return ring_start(up, down)
+
+    def ring_end(terms, second, after):
+        up, down = second
+        trail = []
+        for s in range(half - 2, 0, -1):
+            if after and s > 1:
+                up, down = tie_pair((up, down), after[len(trail)])
+            up, down = ring_start(up + terms[s], down + terms[chips - s])
+            trail.append((up, down))
+        return terms[0] + up + down, trail
+
+    def tie_pair(pair, others):
+        return lax.optimization_barrier((*pair, *others))[:2]
 
     vmem = pl.BlockSpec(memory_space=pltpu.VMEM)
     smem = pl.BlockSpec(memory_space=pltpu.SMEM)
     anywhere = pl.BlockSpec(memory_space=pl.ANY)
-    mid_params = pltpu.CompilerParams(vmem_limit_bytes=32 * 2**20)
-    leaf_params = pltpu.CompilerParams(vmem_limit_bytes=28 * 2**20)
+    near_params = pltpu.CompilerParams(vmem_limit_bytes=60 * 2**20)
+    mid_params = pltpu.CompilerParams(vmem_limit_bytes=60 * 2**20)
+    leaf_params = pltpu.CompilerParams(vmem_limit_bytes=60 * 2**20)
+
+    def near(word, anc_cov, anc_swapped, flows, flow_swaps):
+        rows, mid = flows[0].shape
+        depth = 2 * rows * half
+        return pl.pallas_call(
+            lambda *refs: near_kernel(chips, snake, *refs),
+            out_shape=jax.ShapeDtypeStruct((2 * rows, mid), F32),
+            in_specs=[smem] + [anywhere] * (2 + 2 * half),
+            out_specs=vmem,
+            scratch_shapes=[
+                pltpu.VMEM((2 * rows, depth), BF16),
+                pltpu.VMEM((depth, mid), BF16),
+                pltpu.SemaphoreType.DMA((6 * half,)),
+            ],
+            compiler_params=near_params,
+            cost_estimate=pl.CostEstimate(flops=7 * 10**9, bytes_accessed=10 * 2**20, transcendentals=0),
+            name="near_product",
+        )(word, anc_cov, anc_swapped, *[x for pair in zip(flows, flow_swaps) for x in pair])
 
     def local(anc_cov, mid_factor, mid_diag_inv, leaf_factor, leaf_diag_inv, leaf_rows):
         device = lax.axis_index("row")
@@ -229,53 +283,70 @@
         mid = mid_factor.shape[1]
         leaf = leaf_factor.shape[1]
 
-        leaf_flow = leaf_factor
-        leaf_parts = [leaf_factor, swap(leaf_factor)]
-        flow = mid_factor
-        factors = [mid_factor, swap(mid_factor)]
+        leaf_flows, leaf_swaps = [leaf_factor], [swap(leaf_factor)]
+        flows, flow_swaps = [mid_factor], [swap(mid_factor)]
         anc_swapped = swap(anc_cov)
         diag_swapped = swap(mid_diag_inv)
-        done = 0
+
+        def factor_step(k):
+            pairs = perm(-1, (lambda s, t, c: t < half) if k == half else (lambda s, t, c: True))
+            deps = [leaf_flows[(3 * (k - 1)) // 2]] + flow_swaps[: k - 1][-1:] if k > 1 else []
+            flows.append(lax.ppermute(tie(flows[-1], *deps), "row", pairs))
+
+        def leaf_step(k):
+            deps = leaf_swaps[: k - 1][-1:] if k < chips - 1 else []
+            if k > 2:
+                deps.append(flows[min(half, (5 * (k - 1)) // 8)])
+            if k == 2:
+                deps.append(diag_swapped)
+            if k == 3:
+                deps.append(anc_swapped)
+            leaf_flows.append(lax.ppermute(tie(leaf_flows[-1], *deps), "row", perm(1)))
+
         for step in range(1, chips):
-            due = min(half, (step * half - 1) // (chips - 1))
-            while done < due:
-                done += 1
-                pairs = perm(-1, (lambda s, t, c: t < half) if done == half else (lambda s, t, c: True))
-                flow = lax.ppermute(flow, "row", pairs)
-                factors += [flow, swap(flow)]
-                flow, leaf_flow = lax.optimization_barrier((flow, leaf_flow))
-            leaf_flow = lax.ppermute(leaf_flow, "row", perm(1))
-            leaf_parts += [leaf_flow, swap(leaf_flow)]
-        while done < half:
-            done += 1
-            pairs = perm(-1, (lambda s, t, c: t < half) if done == half else (lambda s, t, c: True))
-            flow = lax.ppermute(flow, "row", pairs)
-            factors += [flow, swap(flow)]
+            while len(flows) <= half and (3 * (len(flows) - 1)) // 2 < step:
+                factor_step(len(flows))
+                if len(flows) <= half:
+                    flow_swaps.append(swap(flows[-1]))
+            if step == chips - 1:
+                near_word = tie(device_word, leaf_flows[-2])
+                cross = near(near_word, anc_cov, anc_swapped, flows[:half], flow_swaps[:half])
+                leaf_flows[-1] = tie(leaf_flows[-1], cross)
+            leaf_step(step)
+            if step < chips - 1:
+                leaf_swaps.append(swap(leaf_flows[-1]))
+        flow_swaps.append(swap(tie(flows[-1], leaf_flows[-2])))
+        mid_word = tie(device_word, leaf_flows[-2], leaf_swaps[-2])
 
         strip = mid // devices
-        depth = 2 * rows * (half + 1)
         outs = pl.pallas_call(
             lambda *refs: mid_kernel(chips, snake, *refs),
             out_shape=[jax.ShapeDtypeStruct((2 * rows, mid), BF16)] * 2
-            + [jax.ShapeDtypeStruct((strip, mid), F32)] * chips,
-            in_specs=[smem] + [anywhere] * (2 + len(factors)),
-            out_specs=[vmem] * (2 + chips),
+            + [jax.ShapeDtypeStruct((strip, mid), F32)] * chips
+            + [jax.ShapeDtypeStruct((strip // 2, mid), F32)] * 2,
+            in_specs=[smem] + [anywhere] * 7,
+            out_specs=[vmem] * (4 + chips),
             scratch_shapes=[
-                pltpu.VMEM((2 * rows, depth), BF16),
-                pltpu.VMEM((depth, mid), BF16),
+                pltpu.VMEM((2 * rows, 2 * rows), BF16),
+                pltpu.VMEM((2 * rows, mid), BF16),
+                pltpu.VMEM((2 * rows, mid), BF16),
+                pltpu.VMEM((2 * rows, mid), F32),
                 pltpu.VMEM((3 * mid, 2 * rows), BF16),
                 pltpu.VMEM((mid // 2, 8 * rows), BF16),
                 pltpu.VMEM((8 * rows, mid), BF16),
-                pltpu.SemaphoreType.DMA((6 * (half + 1),)),
+                pltpu.SemaphoreType.DMA((9,)),
             ],
             compiler_params=mid_params,
-            cost_estimate=pl.CostEstimate(flops=15 * 10**9, bytes_accessed=14 * 2**20, transcendentals=0),
+            cost_estimate=pl.CostEstimate(flops=20 * 10**9, bytes_accessed=14 * 2**20, transcendentals=0),
             name="mid_blocks",
-        )(device_word, anc_cov, anc_swapped, *factors)
-        c_high, c_low, mid_terms = outs[0], outs[1], outs[2:]
-        mid_block = mid_diag_inv.astype(F32) + ring_sum(mid_terms)
+        )(mid_word, anc_cov, anc_swapped, flows[0], flow_swaps[0], flows[half], flow_swaps[half], cross)
+        c_high, c_low, mid_terms = outs[0], outs[1], outs[2 : 2 + chips]
+        mid_first = ring_start(outs[-2], outs[-1])
+        leaf_swaps.append(swap(tie(leaf_flows[-1], c_high)))
+        leaf_parts = [x for pair in zip(leaf_flows, leaf_swaps) for x in pair]
 
         band = leaf // chips
+        depth = 2 * rows * (half + 1)
         *keep, give = pl.pallas_call(
             lambda *refs: leaf_kernel(chips, snake, *refs),
             out_shape=[jax.ShapeDtypeStruct((band, leaf), F32)] * chips + [jax.ShapeDtypeStruct((leaf, leaf), F32)],
@@ -297,12 +368,19 @@
             cost_estimate=pl.CostEstimate(flops=2 * 10**10, bytes_accessed=20 * 2**20, transcendentals=0),
             name="leaf_blocks",
         )(
-            device_word, leaf_rows, anc_cov, anc_swapped, factors[0], factors[1], mid_diag_inv, diag_swapped,
+            device_word, leaf_rows, anc_cov, anc_swapped, flows[0], flow_swaps[0], mid_diag_inv, diag_swapped,
             c_high, c_low, *leaf_parts,
         )
-        got = swap(give)
+        got = swap(tie(give, *mid_first))
         leaf_terms = [keep[s] + got[s * band : (s + 1) * band] for s in range(chips)]
-        leaf_block = leaf_diag_inv.astype(F32) + ring_sum(leaf_terms)
+        leaf_far = leaf_terms[half]
+        leaf_first = ring_start(leaf_far[: band // 2], leaf_far[band // 2 :])
+        mid_second = ring_next(mid_terms, mid_first)
+        leaf_second = ring_next(leaf_terms, leaf_first)
+        mid_sum, trail = ring_end(mid_terms, mid_second, None)
+        leaf_sum, _ = ring_end(leaf_terms, leaf_second, None)
+        mid_block = mid_diag_inv.astype(F32) + mid_sum
+        leaf_block = leaf_diag_inv.astype(F32) + leaf_sum
         return mid_block, leaf_block
 
     placed = (

time: 138 us -> 124 us (0.90)
  waiting for transfers between devices: 72.6 us -> 60.8 us
  Pallas kernels: 19.3 us -> 24.7 us
  local copies, waits for them, and re-layouts: 8.16 us -> 2.79 us
  starting transfers between devices: 35.2 us -> 31.2 us
  other arithmetic: 1.8 us -> 3.73 us
    ppermute x27, waiting for transfers between devices: 72.1 us -> 55.3 us  [the longest x7 25.7 us: leaf_step(): leaf_flows.append(lax.ppermute(tie(leaf_flows[-1], *deps), 'row', perm(1)))]
    pallas_call x0 -> x1, Pallas kernels: none -> 6.8 us  [near(): pl.pallas_call(lambda *refs: near_kernel(chips, snake, *refs), out_shape=...]
    unnamed x52 -> x64, local copies, waits for them, and re-layouts: 8.13 us -> 2.78 us
    ppermute x16, waiting for transfers between devices: 0.51 us -> 5.53 us  [swap(): return lax.ppermute(x, 'row', swap_pairs)]
    ppermute x27, starting transfers between devices: 32 us -> 28.8 us  [the longest x8 11.2 us: ring_start(): lax.ppermute(up, 'row', perm(1))]
  transfers between devices with their start and end apart: 43 -> 43, of which waited for: 20 -> 23; matrix products, arithmetic and copies ran while one was open for 1% -> 2% of each run, Pallas kernels for 6% -> 20%
where the time goes in v2:
time: 124 us
  waiting for transfers between devices  60.8 us (49%)
  starting transfers between devices  31.2 us (25%)
  Pallas kernels  24.7 us (20%)
  other arithmetic  3.73 us (3%)
  local copies, waits for them, and re-layouts  2.79 us (2%)
    ppermute x7, waiting for transfers between devices, leaf_step(): leaf_flows.append(lax.ppermute(tie(leaf_flows[-1], *deps), 'row', perm(1)))  25.7 us
    ppermute x4, waiting for transfers between devices, factor_step(): flows.append(lax.ppermute(tie(flows[-1], *deps), 'row', pairs))  15.6 us
    ppermute x8, starting transfers between devices, ring_start(): lax.ppermute(up, 'row', perm(1))  11.2 us
    pallas_call x1, Pallas kernels, local(): pl.pallas_call(lambda *refs: leaf_kernel(chips, snake, *refs), out_shape=...  10.7 us
    ppermute x8, waiting for transfers between devices, ring_start(): lax.ppermute(up, 'row', perm(1))  10.1 us
    ppermute x4, starting transfers between devices, factor_step(): flows.append(lax.ppermute(tie(flows[-1], *deps), 'row', pairs))  7.54 us
    pallas_call x1, Pallas kernels, local(): pl.pallas_call(lambda *refs: mid_kernel(chips, snake, *refs), out_shape=[...  7.25 us
    pallas_call x1, Pallas kernels, near(): pl.pallas_call(lambda *refs: near_kernel(chips, snake, *refs), out_shape=...  6.8 us
  transfers between devices with their start and end apart: 43, of which 23 were waited for; matrix products, arithmetic and copies ran while one was open for 2% of the time, Pallas kernels for 20%

profile of v2, /device:TPU:0, one launch (start us, length us, event | category | flops | bytes accessed | tf_op | source)
XLA Modules:
  0.0 124.2 jit_solution(14198134805360854548)
XLA Ops:
  0.6 0.5 collective-permute-start.6
  1.2 2.9 %collective-permute-start.5 = (bf16[256,1024]{1,0:T(8,128)(2,1)}, bf16[256,1024]{1,0:T(8,128)(2,1)S(1)}, u32[]{:S(2)}, u32[]{:S(2)}) collective-permute-start(bf16[256,1024]{1,0:T(8,128)(2,1)} %refs_4_.1), channel_id=1, source_target_pairs={{0,2},{1,3},{4,0},{5,1},{8,4},{9,5},{12,8},{13,9},{14,12},{15,13},... | collective-permute-start | bytes 1572872 | tf_op jit(solution)/shard_map/ppermute | solution.py:294
  4.2 0.1 collective-permute-start
  4.3 1.0 collective-permute-done.2.refs_7_
  5.3 0.4 collective-permute-start.1
  5.7 8.8 %collective-permute-done.refs_12_ = bf16[320,512]{1,0:T(8,128)(2,1)S(1)} collective-permute-done((bf16[320,512]{1,0:T(8,128)(2,1)}, bf16[320,512]{1,0:T(8,128)(2,1)S(1)}, u32[]{:S(2)}, u32[]{:S(2)}) %collective-permute-start) | collective-permute-done | bytes 327712 | tf_op jit(solution)/shard_map/ppermute | solution.py:304
  14.5 0.3 collective-permute-start.3
  14.9 1.8 %collective-permute-done.5.refs_5_ = bf16[256,1024]{1,0:T(8,128)(2,1)S(1)} collective-permute-done((bf16[256,1024]{1,0:T(8,128)(2,1)}, bf16[256,1024]{1,0:T(8,128)(2,1)S(1)}, u32[]{:S(2)}, u32[]{:S(2)}) %collective-permute-start.5) | collective-permute-done | bytes 524320 | tf_op jit(solution)/shard_map/ppermute | solution.py:294
  16.6 1.7 %collective-permute-start.12 = (bf16[256,1024]{1,0:T(8,128)(2,1)S(1)}, bf16[256,1024]{1,0:T(8,128)(2,1)}, u32[]{:S(2)}, u32[]{:S(2)}) collective-permute-start(bf16[256,1024]{1,0:T(8,128)(2,1)S(1)} %collective-permute-done.5.refs_5_), channel_id=1, source_target_pairs={{0,2},{1,3},{4,0},{5,1},{8,4},{9,5},{12,8},{13,9},{14,12},{15,13},... | collective-permute-start | bytes 1572872 | tf_op jit(solution)/shard_map/ppermute | solution.py:294
  18.4 5.5 %collective-permute-done.3.refs_14_ = bf16[320,512]{1,0:T(8,128)(2,1)S(1)} collective-permute-done((bf16[320,512]{1,0:T(8,128)(2,1)S(1)}, bf16[320,512]{1,0:T(8,128)(2,1)S(1)}, u32[]{:S(2)}, u32[]{:S(2)}) %collective-permute-start.3) | collective-permute-done | bytes 327712 | tf_op jit(solution)/shard_map/ppermute | solution.py:304
  23.9 0.4 collective-permute-start.7
  24.3 5.8 %collective-permute-done.12.refs_7_ = bf16[256,1024]{1,0:T(8,128)(2,1)} collective-permute-done((bf16[256,1024]{1,0:T(8,128)(2,1)S(1)}, bf16[256,1024]{1,0:T(8,128)(2,1)}, u32[]{:S(2)}, u32[]{:S(2)}) %collective-permute-start.12) | collective-permute-done | bytes 524320 | tf_op jit(solution)/shard_map/ppermute | solution.py:294
  30.2 0.8 copy-done.17
  31.0 1.6 %collective-permute-done.7.refs_16_ = bf16[320,512]{1,0:T(8,128)(2,1)S(1)} collective-permute-done((bf16[320,512]{1,0:T(8,128)(2,1)S(1)}, bf16[320,512]{1,0:T(8,128)(2,1)S(1)}, u32[]{:S(2)}, u32[]{:S(2)}) %collective-permute-start.7) | collective-permute-done | bytes 327712 | tf_op jit(solution)/shard_map/ppermute | solution.py:304
  32.5 1.6 %collective-permute-start.16 = (bf16[256,1024]{1,0:T(8,128)(2,1)}, bf16[256,1024]{1,0:T(8,128)(2,1)}, u32[]{:S(2)}, u32[]{:S(2)}) collective-permute-start(bf16[256,1024]{1,0:T(8,128)(2,1)} %collective-permute-done.12.refs_7_), channel_id=1, source_target_pairs={{0,2},{1,3},{4,0},{5,1},{8,4},{9,5},{12,8},{13,9},{14,12},{15,13},... | collective-permute-start | bytes 1572872 | tf_op jit(solution)/shard_map/ppermute | solution.py:294
  34.1 1.6 %collective-permute-done.8.refs_15_ = bf16[320,512]{1,0:T(8,128)(2,1)S(1)} collective-permute-done((bf16[320,512]{1,0:T(8,128)(2,1)S(1)}, bf16[320,512]{1,0:T(8,128)(2,1)S(1)}, u32[]{:S(2)}, u32[]{:S(2)}) %collective-permute-start.8) | collective-permute-done | bytes 327712 | tf_op jit(solution)/shard_map/ppermute | solution.py:227
  35.8 0.5 collective-permute-start.9
  36.2 0.5 collective-permute-start.18
  36.7 8.0 %collective-permute-done.16.refs_9_ = bf16[256,1024]{1,0:T(8,128)(2,1)} collective-permute-done((bf16[256,1024]{1,0:T(8,128)(2,1)}, bf16[256,1024]{1,0:T(8,128)(2,1)}, u32[]{:S(2)}, u32[]{:S(2)}) %collective-permute-start.16) | collective-permute-done | bytes 524320 | tf_op jit(solution)/shard_map/ppermute | solution.py:294
  44.7 0.9 collective-permute-done.9.refs_18_
  45.6 0.5 collective-permute-start.13
  46.1 0.2 copy-done.26
  46.4 1.3 %collective-permute-start.21 = (bf16[256,1024]{1,0:T(8,128)(2,1)}, bf16[256,1024]{1,0:T(8,128)(2,1)S(1)}, u32[]{:S(2)}, u32[]{:S(2)}) collective-permute-start(bf16[256,1024]{1,0:T(8,128)(2,1)} %collective-permute-done.16.refs_9_), channel_id=1, source_target_pairs={{4,0},{5,1},{8,4},{9,5},{12,8},{13,9},{14,12},{15,13},{20,16},{21,... | collective-permute-start | bytes 1572872 | tf_op jit(solution)/shard_map/ppermute | solution.py:294
  47.6 7.6 %collective-permute-done.13.refs_20_ = bf16[320,512]{1,0:T(8,128)(2,1)} collective-permute-done((bf16[320,512]{1,0:T(8,128)(2,1)}, bf16[320,512]{1,0:T(8,128)(2,1)}, u32[]{:S(2)}, u32[]{:S(2)}) %collective-permute-start.13) | collective-permute-done | bytes 327712 | tf_op jit(solution)/shard_map/ppermute | solution.py:304
  55.2 0.6 collective-permute-start.17
  55.9 6.8 %near_product.1.refs_7_ = f32[512,1024]{1,0:T(8,128)} custom-call(s32[1]{0:T(128)} %bitcast.refs_0_, bf16[256,4096]{1,0:T(8,128)(2,1)} %refs_2_.1, bf16[256,4096]{1,0:T(8,128)(2,1)} %copy-done.14, bf16[256,1024]{1,0:T(8,128)(2,1)} %refs_4_.1, bf16[256,1024]{1,0:T(8,128)(2,1)} %copy-done.15, bf16[256,1024]{1,0:T(8,128)(2,1)} %copy-done.16, ...), custom_call_target="tpu_custom_call" | custom-call | flops 7000000000 | bytes 10485760 | tf_op jit(solution)/shard_map/near_product/pallas_call | solution.py:264
  62.7 1.2 collective-permute-done.17.refs_22_
  63.9 0.5 collective-permute-start.20
  64.5 0.8 collective-permute-start.32
  65.3 1.2 collective-permute-done.20.refs_21_
  66.5 0.9 copy-done.19
  67.3 7.2 %mid_blocks.1 = (bf16[512,1024]{1,0:T(8,128)(2,1)}, bf16[512,1024]{1,0:T(8,128)(2,1)}, f32[64,1024]{1,0:T(8,128)}, f32[64,1024]{1,0:T(8,128)}, f32[64,1024]{1,0:...) custom-call(s32[1]{0:T(128)} %bitcast.refs_0_, ...), custom_call_target="tpu_custom_call" | custom-call | flops 20000000000 | bytes 14680064 | tf_op jit(solution)/shard_map/mid_blocks/pallas_call | solution.py:322
  74.8 1.2 collective-permute-start.23
  76.1 1.0 collective-permute-start.27
  77.1 0.7 copy-done.28
  77.9 10.7 %leaf_blocks.1 = (f32[64,512]{1,0:T(8,128)}, f32[64,512]{1,0:T(8,128)}, f32[64,512]{1,0:T(8,128)}, f32[64,512]{1,0:T(8,128)}, f32[64,512]{1,0:T(8,128)}, /*index...) custom-call(s32[1]{0:T(128)} %bitcast.refs_0_, s32[2,80]{1,0:T(2,128)} %refs_1_.5, ...), custom_call_target="tpu_custom_call" | custom-call | flops 20000000000 | bytes 20971520 | tf_op jit(solution)/shard_map/leaf_blocks/pallas_call | solution.py:350
  88.6 0.2 collective-permute-start.34
  88.9 1.0 collective-permute-start.24
  89.9 1.7 %collective-permute-done.34 = f32[512,512]{1,0:T(8,128)S(1)} collective-permute-done((f32[512,512]{1,0:T(8,128)}, f32[512,512]{1,0:T(8,128)S(1)}, u32[]{:S(2)}, u32[]{:S(2)}) %collective-permute-start.34) | collective-permute-done | bytes 1048608 | tf_op jit(solution)/shard_map/ppermute | solution.py:227
  91.5 0.9 slice_add_fusion.5
  92.5 1.1 collective-permute-start.35
  93.5 1.0 collective-permute-start.39
  94.6 2.0 %collective-permute-start.28 = (f32[64,1024]{1,0:T(8,128)S(1)}, f32[64,1024]{1,0:T(8,128)S(1)}, u32[]{:S(2)}, u32[]{:S(2)}) collective-permute-start(f32[64,1024]{1,0:T(8,128)S(1)} %pad_add_fusion), channel_id=1, source_target_pairs={{0,2},{1,3},{4,0},{5,1},{8,4},{9,5},{12,8},{13,9},{14,12},{15,13},... | collective-permute-start | bytes 786440 | tf_op jit(solution)/shard_map/ppermute | solution.py:233
  96.6 2.5 %collective-permute-done.35 = f32[32,512]{1,0:T(8,128)S(1)} collective-permute-done((f32[32,512]{1,0:T(8,128)S(1)}, f32[32,512]{1,0:T(8,128)S(1)}, u32[]{:S(2)}, u32[]{:S(2)}) %collective-permute-start.35) | collective-permute-done | bytes 65568 | tf_op jit(solution)/shard_map/ppermute | solution.py:233
  99.1 1.1 fusion.5
  100.2 1.4 %collective-permute-start.36 = (f32[64,512]{1,0:T(8,128)S(1)}, f32[64,512]{1,0:T(8,128)S(1)}, u32[]{:S(2)}, u32[]{:S(2)}) collective-permute-start(f32[64,512]{1,0:T(8,128)S(1)} %get-tuple-element.76), channel_id=1, source_target_pairs={{0,4},{1,5},{4,8},{5,9},{8,12},{9,13},{12,14},{13,15},{14,10},{15,... | collective-permute-start | bytes 393224 | tf_op jit(solution)/shard_map/ppermute | solution.py:233
  101.6 0.7 collective-permute-start.40
  102.3 1.4 %collective-permute-start.25 = (f32[64,1024]{1,0:T(8,128)S(1)}, f32[64,1024]{1,0:T(8,128)S(1)}, u32[]{:S(2)}, u32[]{:S(2)}) collective-permute-start(f32[64,1024]{1,0:T(8,128)S(1)} %add.87), channel_id=1, source_target_pairs={{0,4},{1,5},{4,8},{5,9},{8,12},{9,13},{12,14},{13,15},{14,10},{15,... | collective-permute-start | bytes 786440 | tf_op jit(solution)/shard_map/ppermute | solution.py:233
  103.8 0.8 collective-permute-start.29
  104.6 2.0 %collective-permute-done.36 = f32[64,512]{1,0:T(8,128)S(1)} collective-permute-done((f32[64,512]{1,0:T(8,128)S(1)}, f32[64,512]{1,0:T(8,128)S(1)}, u32[]{:S(2)}, u32[]{:S(2)}) %collective-permute-start.36) | collective-permute-done | bytes 131104 | tf_op jit(solution)/shard_map/ppermute | solution.py:233
  106.7 1.1 collective-permute-done.40
  107.8 1.9 %collective-permute-start.37 = (f32[64,512]{1,0:T(8,128)S(1)}, f32[64,512]{1,0:T(8,128)S(1)}, u32[]{:S(2)}, u32[]{:S(2)}) collective-permute-start(f32[64,512]{1,0:T(8,128)S(1)} %get-tuple-element.74), channel_id=1, source_target_pairs={{0,4},{1,5},{4,8},{5,9},{8,12},{9,13},{12,14},{13,15},{14,10},{15,... | collective-permute-start | bytes 393224 | tf_op jit(solution)/shard_map/ppermute | solution.py:233
  109.9 2.4 %collective-permute-done.25 = f32[64,1024]{1,0:T(8,128)S(1)} collective-permute-done((f32[64,1024]{1,0:T(8,128)S(1)}, f32[64,1024]{1,0:T(8,128)S(1)}, u32[]{:S(2)}, u32[]{:S(2)}) %collective-permute-start.25) | collective-permute-done | bytes 262176 | tf_op jit(solution)/shard_map/ppermute | solution.py:233
  112.3 1.4 %collective-permute-start.26 = (f32[64,1024]{1,0:T(8,128)S(1)}, f32[64,1024]{1,0:T(8,128)S(1)}, u32[]{:S(2)}, u32[]{:S(2)}) collective-permute-start(f32[64,1024]{1,0:T(8,128)S(1)} %add.88), channel_id=1, source_target_pairs={{0,4},{1,5},{4,8},{5,9},{8,12},{9,13},{12,14},{13,15},{14,10},{15,... | collective-permute-start | bytes 786440 | tf_op jit(solution)/shard_map/ppermute | solution.py:233
  113.7 0.7 collective-permute-start.30
  114.5 0.6 collective-permute-done.37
  115.1 1.1 collective-permute-done.41
  116.2 1.8 %collective-permute-start.38 = (f32[64,512]{1,0:T(8,128)S(1)}, f32[64,512]{1,0:T(8,128)S(1)}, u32[]{:S(2)}, u32[]{:S(2)}) collective-permute-start(f32[64,512]{1,0:T(8,128)S(1)} %get-tuple-element.72), channel_id=1, source_target_pairs={{0,4},{1,5},{4,8},{5,9},{8,12},{9,13},{12,14},{13,15},{14,10},{15,... | collective-permute-start | bytes 393224 | tf_op jit(solution)/shard_map/ppermute | solution.py:233
  118.0 0.3 collective-permute-start.42
  118.3 2.6 %collective-permute-done.26 = f32[64,1024]{1,0:T(8,128)S(1)} collective-permute-done((f32[64,1024]{1,0:T(8,128)S(1)}, f32[64,1024]{1,0:T(8,128)S(1)}, u32[]{:S(2)}, u32[]{:S(2)}) %collective-permute-start.26) | collective-permute-done | bytes 262176 | tf_op jit(solution)/shard_map/ppermute | solution.py:233
  120.9 1.1 collective-permute-done.30
  122.0 0.8 add_add_fusion
  122.8 0.6 collective-permute-done.42
  123.5 0.7 fusion.8
  (102 shorter events, 1.1 us)
Async XLA Ops:
  0.6 23.3 %collective-permute-start.6 = (bf16[256,4096]{1,0:T(8,128)(2,1)}, bf16[256,4096]{1,0:T(8,128)(2,1)S(1)}, u32[]{:S(2)}, u32[]{:S(2)}) collective-permute-start(bf16[256,4096]{1,0:T(8,128)(2,1)} %refs_2_.1), channel_id=1, source_target_pairs={{0,1},{1,0},{2,3},{3,2},{4,5},{5,4},{6,7},{7,6},{8,9},{9,8},{10,11... | collective-permute-start | bytes 6291464 | tf_op jit(solution)/shard_map/ppermute | solution.py:227
  1.1 4.2 %collective-permute-start.2 = (bf16[64,1024]{1,0:T(8,128)(2,1)}, bf16[64,1024]{1,0:T(8,128)(2,1)S(1)}, u32[]{:S(2)}, u32[]{:S(2)}) collective-permute-start(bf16[64,1024]{1,0:T(8,128)(2,1)} %refs_6_.1), channel_id=1, source_target_pairs={{0,1},{1,0},{2,3},{3,2},{4,5},{5,4},{6,7},{7,6},{8,9},{9,8},{10,11... | collective-permute-start | bytes 393224 | tf_op jit(solution)/shard_map/ppermute | solution.py:227
  1.2 15.4 %collective-permute-start.5 = (bf16[256,1024]{1,0:T(8,128)(2,1)}, bf16[256,1024]{1,0:T(8,128)(2,1)S(1)}, u32[]{:S(2)}, u32[]{:S(2)}) collective-permute-start(bf16[256,1024]{1,0:T(8,128)(2,1)} %refs_4_.1), channel_id=1, source_target_pairs={{0,2},{1,3},{4,0},{5,1},{8,4},{9,5},{12,8},{13,9},{14,12},{15,13},... | collective-permute-start | bytes 1572872 | tf_op jit(solution)/shard_map/ppermute | solution.py:294
  4.2 12.4 %collective-permute-start.11 = (bf16[256,1024]{1,0:T(8,128)(2,1)}, bf16[256,1024]{1,0:T(8,128)(2,1)S(1)}, u32[]{:S(2)}, u32[]{:S(2)}) collective-permute-start(bf16[256,1024]{1,0:T(8,128)(2,1)} %refs_4_.1), channel_id=1, source_target_pairs={{0,1},{1,0},{2,3},{3,2},{4,5},{5,4},{6,7},{7,6},{8,9},{9,8},{10,11... | collective-permute-start | bytes 1572872 | tf_op jit(solution)/shard_map/ppermute | solution.py:227
  4.2 10.3 %collective-permute-start = (bf16[320,512]{1,0:T(8,128)(2,1)}, bf16[320,512]{1,0:T(8,128)(2,1)S(1)}, u32[]{:S(2)}, u32[]{:S(2)}) collective-permute-start(bf16[320,512]{1,0:T(8,128)(2,1)} %refs_10_.1), channel_id=1, source_target_pairs={{0,4},{1,5},{4,8},{5,9},{8,12},{9,13},{12,14},{13,15},{14,10},{15,... | collective-permute-start | bytes 983048 | tf_op jit(solution)/shard_map/ppermute | solution.py:304
  5.3 57.4 %copy-start.31 = (bf16[64,1024]{1,0:T(8,128)(2,1)}, bf16[64,1024]{1,0:T(8,128)(2,1)S(1)}, u32[]{:S(2)}) copy-start(bf16[64,1024]{1,0:T(8,128)(2,1)S(1)} %collective-permute-done.2.refs_7_) | copy-start | bytes 393220
  5.3 9.2 %collective-permute-start.1 = (bf16[320,512]{1,0:T(8,128)(2,1)}, bf16[320,512]{1,0:T(8,128)(2,1)S(1)}, u32[]{:S(2)}, u32[]{:S(2)}) collective-permute-start(bf16[320,512]{1,0:T(8,128)(2,1)} %refs_10_.1), channel_id=1, source_target_pairs={{0,1},{1,0},{2,3},{3,2},{4,5},{5,4},{6,7},{7,6},{8,9},{9,8},{10,11... | collective-permute-start | bytes 983048 | tf_op jit(solution)/shard_map/ppermute | solution.py:227
  14.5 18.0 %copy-start.20 = (bf16[320,512]{1,0:T(8,128)(2,1)}, bf16[320,512]{1,0:T(8,128)(2,1)S(1)}, u32[]{:S(2)}) copy-start(bf16[320,512]{1,0:T(8,128)(2,1)S(1)} %collective-permute-done.refs_12_) | copy-start | bytes 983044
  14.5 9.4 %collective-permute-start.3 = (bf16[320,512]{1,0:T(8,128)(2,1)S(1)}, bf16[320,512]{1,0:T(8,128)(2,1)S(1)}, u32[]{:S(2)}, u32[]{:S(2)}) collective-permute-start(bf16[320,512]{1,0:T(8,128)(2,1)S(1)} %collective-permute-done.refs_12_), channel_id=1, source_target_pairs={{0,4},{1,5},{4,8},{5,9},{8,12},{9,13},{12,14},{13,15},{14,10},{15,... | collective-permute-start | bytes 983048 | tf_op jit(solution)/shard_map/ppermute | solution.py:304
  14.8 9.1 %collective-permute-start.4 = (bf16[320,512]{1,0:T(8,128)(2,1)S(1)}, bf16[320,512]{1,0:T(8,128)(2,1)S(1)}, u32[]{:S(2)}, u32[]{:S(2)}) collective-permute-start(bf16[320,512]{1,0:T(8,128)(2,1)S(1)} %collective-permute-done.refs_12_), channel_id=1, source_target_pairs={{0,1},{1,0},{2,3},{3,2},{4,5},{5,4},{6,7},{7,6},{8,9},{9,8},{10,11... | collective-permute-start | bytes 983048 | tf_op jit(solution)/shard_map/ppermute | solution.py:227
  16.6 39.3 %copy-start.16 = (bf16[256,1024]{1,0:T(8,128)(2,1)}, bf16[256,1024]{1,0:T(8,128)(2,1)S(1)}, u32[]{:S(2)}) copy-start(bf16[256,1024]{1,0:T(8,128)(2,1)S(1)} %collective-permute-done.5.refs_5_) | copy-start | bytes 1572868
  16.6 39.2 %copy-start.15 = (bf16[256,1024]{1,0:T(8,128)(2,1)}, bf16[256,1024]{1,0:T(8,128)(2,1)S(1)}, u32[]{:S(2)}) copy-start(bf16[256,1024]{1,0:T(8,128)(2,1)S(1)} %collective-permute-done.11.refs_4_.refs_5_) | copy-start | bytes 1572868
  16.6 13.5 %collective-permute-start.12 = (bf16[256,1024]{1,0:T(8,128)(2,1)S(1)}, bf16[256,1024]{1,0:T(8,128)(2,1)}, u32[]{:S(2)}, u32[]{:S(2)}) collective-permute-start(bf16[256,1024]{1,0:T(8,128)(2,1)S(1)} %collective-permute-done.5.refs_5_), channel_id=1, source_target_pairs={{0,2},{1,3},{4,0},{5,1},{8,4},{9,5},{12,8},{13,9},{14,12},{15,13},... | collective-permute-start | bytes 1572872 | tf_op jit(solution)/shard_map/ppermute | solution.py:294
  18.4 11.8 %collective-permute-start.15 = (bf16[256,1024]{1,0:T(8,128)(2,1)S(1)}, bf16[256,1024]{1,0:T(8,128)(2,1)S(1)}, u32[]{:S(2)}, u32[]{:S(2)}) collective-permute-start(bf16[256,1024]{1,0:T(8,128)(2,1)S(1)} %collective-permute-done.5.refs_5_), channel_id=1, source_target_pairs={{0,1},{1,0},{2,3},{3,2},{4,5},{5,4},{6,7},{7,6},{8,9},{9,8},{10,11... | collective-permute-start | bytes 1572872 | tf_op jit(solution)/shard_map/ppermute | solution.py:227
  23.9 10.2 %copy-start.22 = (bf16[320,512]{1,0:T(8,128)(2,1)}, bf16[320,512]{1,0:T(8,128)(2,1)S(1)}, u32[]{:S(2)}) copy-start(bf16[320,512]{1,0:T(8,128)(2,1)S(1)} %collective-permute-done.3.refs_14_) | copy-start | bytes 983044
  23.9 11.8 %copy-start.23 = (bf16[320,512]{1,0:T(8,128)(2,1)}, bf16[320,512]{1,0:T(8,128)(2,1)S(1)}, u32[]{:S(2)}) copy-start(bf16[320,512]{1,0:T(8,128)(2,1)S(1)} %collective-permute-done.4.refs_13_) | copy-start | bytes 983044
  23.9 31.9 %copy-start.14 = (bf16[256,4096]{1,0:T(8,128)(2,1)}, bf16[256,4096]{1,0:T(8,128)(2,1)S(1)}, u32[]{:S(2)}) copy-start(bf16[256,4096]{1,0:T(8,128)(2,1)S(1)} %collective-permute-done.6.refs_2_.refs_3_) | copy-start | bytes 6291460
  23.9 8.6 %collective-permute-start.7 = (bf16[320,512]{1,0:T(8,128)(2,1)S(1)}, bf16[320,512]{1,0:T(8,128)(2,1)S(1)}, u32[]{:S(2)}, u32[]{:S(2)}) collective-permute-start(bf16[320,512]{1,0:T(8,128)(2,1)S(1)} %collective-permute-done.3.refs_14_), channel_id=1, source_target_pairs={{0,4},{1,5},{4,8},{5,9},{8,12},{9,13},{12,14},{13,15},{14,10},{15,... | collective-permute-start | bytes 983048 | tf_op jit(solution)/shard_map/ppermute | solution.py:304
  32.5 12.2 %collective-permute-start.16 = (bf16[256,1024]{1,0:T(8,128)(2,1)}, bf16[256,1024]{1,0:T(8,128)(2,1)}, u32[]{:S(2)}, u32[]{:S(2)}) collective-permute-start(bf16[256,1024]{1,0:T(8,128)(2,1)} %collective-permute-done.12.refs_7_), channel_id=1, source_target_pairs={{0,2},{1,3},{4,0},{5,1},{8,4},{9,5},{12,8},{13,9},{14,12},{15,13},... | collective-permute-start | bytes 1572872 | tf_op jit(solution)/shard_map/ppermute | solution.py:294
  34.1 1.6 %collective-permute-start.8 = (bf16[320,512]{1,0:T(8,128)(2,1)S(1)}, bf16[320,512]{1,0:T(8,128)(2,1)S(1)}, u32[]{:S(2)}, u32[]{:S(2)}) collective-permute-start(bf16[320,512]{1,0:T(8,128)(2,1)S(1)} %collective-permute-done.3.refs_14_), channel_id=1, source_target_pairs={{0,1},{1,0},{2,3},{3,2},{4,5},{5,4},{6,7},{7,6},{8,9},{9,8},{10,11... | collective-permute-start | bytes 983048 | tf_op jit(solution)/shard_map/ppermute | solution.py:227
  35.8 9.9 %collective-permute-start.9 = (bf16[320,512]{1,0:T(8,128)(2,1)S(1)}, bf16[320,512]{1,0:T(8,128)(2,1)}, u32[]{:S(2)}, u32[]{:S(2)}) collective-permute-start(bf16[320,512]{1,0:T(8,128)(2,1)S(1)} %collective-permute-done.7.refs_16_), channel_id=1, source_target_pairs={{0,4},{1,5},{4,8},{5,9},{8,12},{9,13},{12,14},{13,15},{14,10},{15,... | collective-permute-start | bytes 983048 | tf_op jit(solution)/shard_map/ppermute | solution.py:304
  36.2 9.4 %collective-permute-start.10 = (bf16[320,512]{1,0:T(8,128)(2,1)S(1)}, bf16[320,512]{1,0:T(8,128)(2,1)S(1)}, u32[]{:S(2)}, u32[]{:S(2)}) collective-permute-start(bf16[320,512]{1,0:T(8,128)(2,1)S(1)} %collective-permute-done.7.refs_16_), channel_id=1, source_target_pairs={{0,1},{1,0},{2,3},{3,2},{4,5},{5,4},{6,7},{7,6},{8,9},{9,8},{10,11... | collective-permute-start | bytes 983048 | tf_op jit(solution)/shard_map/ppermute | solution.py:227
  36.2 10.1 %collective-permute-start.18 = (bf16[256,1024]{1,0:T(8,128)(2,1)}, bf16[256,1024]{1,0:T(8,128)(2,1)}, u32[]{:S(2)}, u32[]{:S(2)}) collective-permute-start(bf16[256,1024]{1,0:T(8,128)(2,1)} %collective-permute-done.12.refs_7_), channel_id=1, source_target_pairs={{0,1},{1,0},{2,3},{3,2},{4,5},{5,4},{6,7},{7,6},{8,9},{9,8},{10,11... | collective-permute-start | bytes 1572872 | tf_op jit(solution)/shard_map/ppermute | solution.py:227
  44.7 11.1 %collective-permute-start.19 = (bf16[256,1024]{1,0:T(8,128)(2,1)}, bf16[256,1024]{1,0:T(8,128)(2,1)}, u32[]{:S(2)}, u32[]{:S(2)}) collective-permute-start(bf16[256,1024]{1,0:T(8,128)(2,1)} %collective-permute-done.16.refs_9_), channel_id=1, source_target_pairs={{0,1},{1,0},{2,3},{3,2},{4,5},{5,4},{6,7},{7,6},{8,9},{9,8},{10,11... | collective-permute-start | bytes 1572872 | tf_op jit(solution)/shard_map/ppermute | solution.py:227
  45.6 9.6 %collective-permute-start.13 = (bf16[320,512]{1,0:T(8,128)(2,1)}, bf16[320,512]{1,0:T(8,128)(2,1)}, u32[]{:S(2)}, u32[]{:S(2)}) collective-permute-start(bf16[320,512]{1,0:T(8,128)(2,1)} %collective-permute-done.9.refs_18_), channel_id=1, source_target_pairs={{0,4},{1,5},{4,8},{5,9},{8,12},{9,13},{12,14},{13,15},{14,10},{15,... | collective-permute-start | bytes 983048 | tf_op jit(solution)/shard_map/ppermute | solution.py:304
  46.4 8.9 %collective-permute-start.14 = (bf16[320,512]{1,0:T(8,128)(2,1)}, bf16[320,512]{1,0:T(8,128)(2,1)}, u32[]{:S(2)}, u32[]{:S(2)}) collective-permute-start(bf16[320,512]{1,0:T(8,128)(2,1)} %collective-permute-done.9.refs_18_), channel_id=1, source_target_pairs={{0,1},{1,0},{2,3},{3,2},{4,5},{5,4},{6,7},{7,6},{8,9},{9,8},{10,11... | collective-permute-start | bytes 983048 | tf_op jit(solution)/shard_map/ppermute | solution.py:227
  46.4 17.5 %collective-permute-start.21 = (bf16[256,1024]{1,0:T(8,128)(2,1)}, bf16[256,1024]{1,0:T(8,128)(2,1)S(1)}, u32[]{:S(2)}, u32[]{:S(2)}) collective-permute-start(bf16[256,1024]{1,0:T(8,128)(2,1)} %collective-permute-done.16.refs_9_), channel_id=1, source_target_pairs={{4,0},{5,1},{8,4},{9,5},{12,8},{13,9},{14,12},{15,13},{20,16},{21,... | collective-permute-start | bytes 1572872 | tf_op jit(solution)/shard_map/ppermute | solution.py:294
  55.2 8.6 %collective-permute-start.17 = (bf16[320,512]{1,0:T(8,128)(2,1)}, bf16[320,512]{1,0:T(8,128)(2,1)}, u32[]{:S(2)}, u32[]{:S(2)}) collective-permute-start(bf16[320,512]{1,0:T(8,128)(2,1)} %collective-permute-done.13.refs_20_), channel_id=1, source_target_pairs={{0,4},{1,5},{4,8},{5,9},{8,12},{9,13},{12,14},{13,15},{14,10},{15,... | collective-permute-start | bytes 983048 | tf_op jit(solution)/shard_map/ppermute | solution.py:304
  63.9 2.6 %collective-permute-start.22 = (bf16[256,1024]{1,0:T(8,128)(2,1)S(1)}, bf16[256,1024]{1,0:T(8,128)(2,1)S(1)}, u32[]{:S(2)}, u32[]{:S(2)}) collective-permute-start(bf16[256,1024]{1,0:T(8,128)(2,1)S(1)} %collective-permute-done.21.refs_5_), channel_id=1, source_target_pairs={{0,1},{1,0},{2,3},{3,2},{4,5},{5,4},{6,7},{7,6},{8,9},{9,8},{10,11... | collective-permute-start | bytes 1572872 | tf_op jit(solution)/shard_map/ppermute | solution.py:227
  63.9 2.6 %collective-permute-start.20 = (bf16[320,512]{1,0:T(8,128)(2,1)}, bf16[320,512]{1,0:T(8,128)(2,1)S(1)}, u32[]{:S(2)}, u32[]{:S(2)}) collective-permute-start(bf16[320,512]{1,0:T(8,128)(2,1)} %collective-permute-done.13.refs_20_), channel_id=1, source_target_pairs={{0,1},{1,0},{2,3},{3,2},{4,5},{5,4},{6,7},{7,6},{8,9},{9,8},{10,11... | collective-permute-start | bytes 983048 | tf_op jit(solution)/shard_map/ppermute | solution.py:227
  64.4 12.7 %collective-permute-start.31 = (bf16[320,512]{1,0:T(8,128)(2,1)}, bf16[320,512]{1,0:T(8,128)(2,1)S(1)}, u32[]{:S(2)}, u32[]{:S(2)}) collective-permute-start(bf16[320,512]{1,0:T(8,128)(2,1)} %collective-permute-done.17.refs_22_), channel_id=1, source_target_pairs={{0,1},{1,0},{2,3},{3,2},{4,5},{5,4},{6,7},{7,6},{8,9},{9,8},{10,11... | collective-permute-start | bytes 983048 | tf_op jit(solution)/shard_map/ppermute | solution.py:227
  64.5 10.3 %collective-permute-start.32 = (bf16[320,512]{1,0:T(8,128)(2,1)}, bf16[320,512]{1,0:T(8,128)(2,1)S(1)}, u32[]{:S(2)}, u32[]{:S(2)}) collective-permute-start(bf16[320,512]{1,0:T(8,128)(2,1)} %collective-permute-done.17.refs_22_), channel_id=1, source_target_pairs={{0,4},{1,5},{4,8},{5,9},{8,12},{9,13},{12,14},{13,15},{14,10},{15,... | collective-permute-start | bytes 983048 | tf_op jit(solution)/shard_map/ppermute | solution.py:304
  74.7 2.3 %collective-permute-start.33 = (bf16[320,512]{1,0:T(8,128)(2,1)S(1)}, bf16[320,512]{1,0:T(8,128)(2,1)S(1)}, u32[]{:S(2)}, u32[]{:S(2)}) collective-permute-start(bf16[320,512]{1,0:T(8,128)(2,1)S(1)} %collective-permute-done.32.refs_24_), channel_id=1, source_target_pairs={{0,1},{1,0},{2,3},{3,2},{4,5},{5,4},{6,7},{7,6},{8,9},{9,8},{10,11... | collective-permute-start | bytes 983048 | tf_op jit(solution)/shard_map/ppermute | solution.py:227
  74.8 13.8 %collective-permute-start.23 = (f32[32,1024]{1,0:T(8,128)}, f32[32,1024]{1,0:T(8,128)S(1)}, u32[]{:S(2)}, u32[]{:S(2)}) collective-permute-start(f32[32,1024]{1,0:T(8,128)} %get-tuple-element.51), channel_id=1, source_target_pairs={{0,4},{1,5},{4,8},{5,9},{8,12},{9,13},{12,14},{13,15},{14,10},{15,... | collective-permute-start | bytes 393224 | tf_op jit(solution)/shard_map/ppermute | solution.py:233
  76.1 12.5 %collective-permute-start.27 = (f32[32,1024]{1,0:T(8,128)}, f32[32,1024]{1,0:T(8,128)S(1)}, u32[]{:S(2)}, u32[]{:S(2)}) collective-permute-start(f32[32,1024]{1,0:T(8,128)} %get-tuple-element.55), channel_id=1, source_target_pairs={{0,2},{1,3},{4,0},{5,1},{8,4},{9,5},{12,8},{13,9},{14,12},{15,13},... | collective-permute-start | bytes 393224 | tf_op jit(solution)/shard_map/ppermute | solution.py:233
  77.9 11.0 %copy-start.5 = (f32[64,1024]{1,0:T(8,128)S(1)}, f32[64,1024]{1,0:T(8,128)}, u32[]{:S(2)}) copy-start(f32[64,1024]{1,0:T(8,128)} %get-tuple-element.50) | copy-start | bytes 786436
  77.9 16.7 %copy-start.4 = (f32[64,1024]{1,0:T(8,128)S(1)}, f32[64,1024]{1,0:T(8,128)}, u32[]{:S(2)}) copy-start(f32[64,1024]{1,0:T(8,128)} %get-tuple-element.54) | copy-start | bytes 786436
  88.6 13.7 %copy-start.3 = (f32[64,1024]{1,0:T(8,128)S(1)}, f32[64,1024]{1,0:T(8,128)}, u32[]{:S(2)}) copy-start(f32[64,1024]{1,0:T(8,128)} %get-tuple-element.52) | copy-start | bytes 786436
  88.6 15.2 %copy-start.2 = (f32[64,1024]{1,0:T(8,128)S(1)}, f32[64,1024]{1,0:T(8,128)}, u32[]{:S(2)}) copy-start(f32[64,1024]{1,0:T(8,128)} %get-tuple-element.56) | copy-start | bytes 786436
  88.6 2.9 %collective-permute-start.34 = (f32[512,512]{1,0:T(8,128)}, f32[512,512]{1,0:T(8,128)S(1)}, u32[]{:S(2)}, u32[]{:S(2)}) collective-permute-start(f32[512,512]{1,0:T(8,128)} %get-tuple-element.64), channel_id=1, source_target_pairs={{0,1},{1,0},{2,3},{3,2},{4,5},{5,4},{6,7},{7,6},{8,9},{9,8},{10,11... | collective-permute-start | bytes 3145736 | tf_op jit(solution)/shard_map/ppermute | solution.py:227
  88.9 18.9 %copy-start.11 = (f32[64,512]{1,0:T(8,128)S(1)}, f32[64,512]{1,0:T(8,128)}, u32[]{:S(2)}) copy-start(f32[64,512]{1,0:T(8,128)} %get-tuple-element.67) | copy-start | bytes 393220
  88.9 18.9 %copy-start.12 = (f32[64,512]{1,0:T(8,128)S(1)}, f32[64,512]{1,0:T(8,128)}, u32[]{:S(2)}) copy-start(f32[64,512]{1,0:T(8,128)} %get-tuple-element.70) | copy-start | bytes 393220
  88.9 13.4 %collective-permute-start.24 = (f32[64,1024]{1,0:T(8,128)S(1)}, f32[64,1024]{1,0:T(8,128)S(1)}, u32[]{:S(2)}, u32[]{:S(2)}) collective-permute-start(f32[64,1024]{1,0:T(8,128)S(1)} %pad_add_fusion.1), channel_id=1, source_target_pairs={{0,4},{1,5},{4,8},{5,9},{8,12},{9,13},{12,14},{13,15},{14,10},{15,... | collective-permute-start | bytes 786440 | tf_op jit(solution)/shard_map/ppermute | solution.py:233
  92.5 6.6 %collective-permute-start.35 = (f32[32,512]{1,0:T(8,128)S(1)}, f32[32,512]{1,0:T(8,128)S(1)}, u32[]{:S(2)}, u32[]{:S(2)}) collective-permute-start(f32[32,512]{1,0:T(8,128)S(1)} %get-tuple-element.78), channel_id=1, source_target_pairs={{0,4},{1,5},{4,8},{5,9},{8,12},{9,13},{12,14},{13,15},{14,10},{15,... | collective-permute-start | bytes 196616 | tf_op jit(solution)/shard_map/ppermute | solution.py:233
  93.5 5.6 %collective-permute-start.39 = (f32[32,512]{1,0:T(8,128)S(1)}, f32[32,512]{1,0:T(8,128)S(1)}, u32[]{:S(2)}, u32[]{:S(2)}) collective-permute-start(f32[32,512]{1,0:T(8,128)S(1)} %get-tuple-element.79), channel_id=1, source_target_pairs={{0,2},{1,3},{4,0},{5,1},{8,4},{9,5},{12,8},{13,9},{14,12},{15,13},... | collective-permute-start | bytes 196616 | tf_op jit(solution)/shard_map/ppermute | solution.py:233
  94.6 17.7 %copy-start.1 = (f32[64,1024]{1,0:T(8,128)S(1)}, f32[64,1024]{1,0:T(8,128)}, u32[]{:S(2)}) copy-start(f32[64,1024]{1,0:T(8,128)} %get-tuple-element.53) | copy-start | bytes 786436
  94.6 9.1 %collective-permute-start.28 = (f32[64,1024]{1,0:T(8,128)S(1)}, f32[64,1024]{1,0:T(8,128)S(1)}, u32[]{:S(2)}, u32[]{:S(2)}) collective-permute-start(f32[64,1024]{1,0:T(8,128)S(1)} %pad_add_fusion), channel_id=1, source_target_pairs={{0,2},{1,3},{4,0},{5,1},{8,4},{9,5},{12,8},{13,9},{14,12},{15,13},... | collective-permute-start | bytes 786440 | tf_op jit(solution)/shard_map/ppermute | solution.py:233
  99.1 14.6 %copy-start = (f32[64,1024]{1,0:T(8,128)S(1)}, f32[64,1024]{1,0:T(8,128)}, u32[]{:S(2)}) copy-start(f32[64,1024]{1,0:T(8,128)} %get-tuple-element.57) | copy-start | bytes 786436
  100.2 6.4 %collective-permute-start.36 = (f32[64,512]{1,0:T(8,128)S(1)}, f32[64,512]{1,0:T(8,128)S(1)}, u32[]{:S(2)}, u32[]{:S(2)}) collective-permute-start(f32[64,512]{1,0:T(8,128)S(1)} %get-tuple-element.76), channel_id=1, source_target_pairs={{0,4},{1,5},{4,8},{5,9},{8,12},{9,13},{12,14},{13,15},{14,10},{15,... | collective-permute-start | bytes 393224 | tf_op jit(solution)/shard_map/ppermute | solution.py:233
  101.6 6.1 %collective-permute-start.40 = (f32[64,512]{1,0:T(8,128)S(1)}, f32[64,512]{1,0:T(8,128)S(1)}, u32[]{:S(2)}, u32[]{:S(2)}) collective-permute-start(f32[64,512]{1,0:T(8,128)S(1)} %get-tuple-element.77), channel_id=1, source_target_pairs={{0,2},{1,3},{4,0},{5,1},{8,4},{9,5},{12,8},{13,9},{14,12},{15,13},... | collective-permute-start | bytes 393224 | tf_op jit(solution)/shard_map/ppermute | solution.py:233
  102.3 13.9 %copy-start.9 = (f32[64,512]{1,0:T(8,128)S(1)}, f32[64,512]{1,0:T(8,128)}, u32[]{:S(2)}) copy-start(f32[64,512]{1,0:T(8,128)} %get-tuple-element.68) | copy-start | bytes 393220
  102.3 13.9 %copy-start.10 = (f32[64,512]{1,0:T(8,128)S(1)}, f32[64,512]{1,0:T(8,128)}, u32[]{:S(2)}) copy-start(f32[64,512]{1,0:T(8,128)} %get-tuple-element.71) | copy-start | bytes 393220
  102.3 9.9 %collective-permute-start.25 = (f32[64,1024]{1,0:T(8,128)S(1)}, f32[64,1024]{1,0:T(8,128)S(1)}, u32[]{:S(2)}, u32[]{:S(2)}) collective-permute-start(f32[64,1024]{1,0:T(8,128)S(1)} %add.87), channel_id=1, source_target_pairs={{0,4},{1,5},{4,8},{5,9},{8,12},{9,13},{12,14},{13,15},{14,10},{15,... | collective-permute-start | bytes 786440 | tf_op jit(solution)/shard_map/ppermute | solution.py:233
  103.8 18.3 %copy-start.6 = (f32[64,1024]{1,0:T(8,128)S(1)}, f32[64,1024]{1,0:T(8,128)}, u32[]{:S(2)}) copy-start(f32[64,1024]{1,0:T(8,128)} %get-tuple-element.49) | copy-start | bytes 786436
  103.8 18.3 %copy-start.7 = (bf16[64,1024]{1,0:T(8,128)(2,1)S(1)}, bf16[64,1024]{1,0:T(8,128)(2,1)}, u32[]{:S(2)}) copy-start(bf16[64,1024]{1,0:T(8,128)(2,1)} %refs_6_.1) | copy-start | bytes 393220
  103.8 9.9 %collective-permute-start.29 = (f32[64,1024]{1,0:T(8,128)S(1)}, f32[64,1024]{1,0:T(8,128)S(1)}, u32[]{:S(2)}, u32[]{:S(2)}) collective-permute-start(f32[64,1024]{1,0:T(8,128)S(1)} %add.91), channel_id=1, source_target_pairs={{0,2},{1,3},{4,0},{5,1},{8,4},{9,5},{12,8},{13,9},{14,12},{15,13},... | collective-permute-start | bytes 786440 | tf_op jit(solution)/shard_map/ppermute | solution.py:233
  107.8 15.7 %copy-start.8 = (f32[64,512]{1,0:T(8,128)S(1)}, f32[64,512]{1,0:T(8,128)}, u32[]{:S(2)}) copy-start(f32[64,512]{1,0:T(8,128)} %get-tuple-element.62) | copy-start | bytes 393220
  107.8 15.6 %copy-start.13 = (bf16[64,512]{1,0:T(8,128)(2,1)S(1)}, bf16[64,512]{1,0:T(8,128)(2,1)}, u32[]{:S(2)}) copy-start(bf16[64,512]{1,0:T(8,128)(2,1)} %param.10) | copy-start | bytes 196612
  107.8 7.3 %collective-permute-start.37 = (f32[64,512]{1,0:T(8,128)S(1)}, f32[64,512]{1,0:T(8,128)S(1)}, u32[]{:S(2)}, u32[]{:S(2)}) collective-permute-start(f32[64,512]{1,0:T(8,128)S(1)} %get-tuple-element.74), channel_id=1, source_target_pairs={{0,4},{1,5},{4,8},{5,9},{8,12},{9,13},{12,14},{13,15},{14,10},{15,... | collective-permute-start | bytes 393224 | tf_op jit(solution)/shard_map/ppermute | solution.py:233
  109.8 6.4 %collective-permute-start.41 = (f32[64,512]{1,0:T(8,128)S(1)}, f32[64,512]{1,0:T(8,128)S(1)}, u32[]{:S(2)}, u32[]{:S(2)}) collective-permute-start(f32[64,512]{1,0:T(8,128)S(1)} %get-tuple-element.75), channel_id=1, source_target_pairs={{0,2},{1,3},{4,0},{5,1},{8,4},{9,5},{12,8},{13,9},{14,12},{15,13},... | collective-permute-start | bytes 393224 | tf_op jit(solution)/shard_map/ppermute | solution.py:233
  112.3 8.6 %collective-permute-start.26 = (f32[64,1024]{1,0:T(8,128)S(1)}, f32[64,1024]{1,0:T(8,128)S(1)}, u32[]{:S(2)}, u32[]{:S(2)}) collective-permute-start(f32[64,1024]{1,0:T(8,128)S(1)} %add.88), channel_id=1, source_target_pairs={{0,4},{1,5},{4,8},{5,9},{8,12},{9,13},{12,14},{13,15},{14,10},{15,... | collective-permute-start | bytes 786440 | tf_op jit(solution)/shard_map/ppermute | solution.py:233
  113.7 8.3 %collective-permute-start.30 = (f32[64,1024]{1,0:T(8,128)S(1)}, f32[64,1024]{1,0:T(8,128)S(1)}, u32[]{:S(2)}, u32[]{:S(2)}) collective-permute-start(f32[64,1024]{1,0:T(8,128)S(1)} %add.92), channel_id=1, source_target_pairs={{0,2},{1,3},{4,0},{5,1},{8,4},{9,5},{12,8},{13,9},{14,12},{15,13},... | collective-permute-start | bytes 786440 | tf_op jit(solution)/shard_map/ppermute | solution.py:233
  116.2 6.6 %collective-permute-start.38 = (f32[64,512]{1,0:T(8,128)S(1)}, f32[64,512]{1,0:T(8,128)S(1)}, u32[]{:S(2)}, u32[]{:S(2)}) collective-permute-start(f32[64,512]{1,0:T(8,128)S(1)} %get-tuple-element.72), channel_id=1, source_target_pairs={{0,4},{1,5},{4,8},{5,9},{8,12},{9,13},{12,14},{13,15},{14,10},{15,... | collective-permute-start | bytes 393224 | tf_op jit(solution)/shard_map/ppermute | solution.py:233
  118.0 5.5 %collective-permute-start.42 = (f32[64,512]{1,0:T(8,128)S(1)}, f32[64,512]{1,0:T(8,128)S(1)}, u32[]{:S(2)}, u32[]{:S(2)}) collective-permute-start(f32[64,512]{1,0:T(8,128)S(1)} %get-tuple-element.73), channel_id=1, source_target_pairs={{0,2},{1,3},{4,0},{5,1},{8,4},{9,5},{12,8},{13,9},{14,12},{15,13},... | collective-permute-start | bytes 393224 | tf_op jit(solution)/shard_map/ppermute | solution.py:233
  (11 other events, 32.7 us)

commit v3 on v2

--- a/solution.py
+++ b/solution.py
@@ -81,8 +81,8 @@
     half = chips // 2
     device_ref, a_refs, own_refs, far_refs, cross_ref = refs[0], refs[1:3], refs[3:5], refs[5:7], refs[7]
     high_ref, low_ref = refs[8:10]
-    y_refs, up_ref, down_ref = refs[10 : 10 + chips], refs[10 + chips], refs[11 + chips]
-    left, right, own, cross, turned, picked, stacked, sems = refs[12 + chips :]
+    y_refs = refs[10 : 10 + chips]
+    left, right, own, cross, turned, picked, stacked, sems = refs[10 + chips :]
     device = device_ref[0]
     chip, core = device // 2, device % 2
     place = place_of(chip, chips, snake)
@@ -118,8 +118,6 @@
     y = mm(picked[...], stacked[...])
     for s in range(chips):
         y_refs[s][...] = y[s * strip : (s + 1) * strip, :]
-    up_ref[...] = y[half * strip : half * strip + strip // 2, :]
-    down_ref[...] = y[half * strip + strip // 2 : (half + 1) * strip, :]
 
 
 def leaf_kernel(chips, snake, *refs):
@@ -229,24 +227,12 @@
     def tie(x, *others):
         return lax.optimization_barrier((x, *others))[0] if others else x
 
-    def ring_start(up, down):
+    def send(up, down):
         return lax.ppermute(up, "row", perm(1)), lax.ppermute(down, "row", perm(-1))
 
-    def ring_next(terms, first):
-        cut = first[0].shape[0]
-        up = terms[half - 1] + jnp.pad(first[0], ((0, cut), (0, 0)))
-        down = terms[half + 1] + jnp.pad(first[1], ((cut, 0), (0, 0)))
-        return ring_start(up, down)
-
-    def ring_end(terms, second, after):
-        up, down = second
-        trail = []
-        for s in range(half - 2, 0, -1):
-            if after and s > 1:
-                up, down = tie_pair((up, down), after[len(trail)])
-            up, down = ring_start(up + terms[s], down + terms[chips - s])
-            trail.append((up, down))
-        return terms[0] + up + down, trail
+    def add_half(term, part, low):
+        gap = term.shape[0] - part.shape[0]
+        return term + jnp.pad(part, ((0, gap) if low else (gap, 0), (0, 0)))
 
     def tie_pair(pair, others):
         return lax.optimization_barrier((*pair, *others))[:2]
@@ -297,9 +283,9 @@
             deps = leaf_swaps[: k - 1][-1:] if k < chips - 1 else []
             if k > 2:
                 deps.append(flows[min(half, (5 * (k - 1)) // 8)])
-            if k == 2:
+            if k == 4:
                 deps.append(diag_swapped)
-            if k == 3:
+            if k == 5:
                 deps.append(anc_swapped)
             leaf_flows.append(lax.ppermute(tie(leaf_flows[-1], *deps), "row", perm(1)))
 
@@ -322,10 +308,9 @@
         outs = pl.pallas_call(
             lambda *refs: mid_kernel(chips, snake, *refs),
             out_shape=[jax.ShapeDtypeStruct((2 * rows, mid), BF16)] * 2
-            + [jax.ShapeDtypeStruct((strip, mid), F32)] * chips
-            + [jax.ShapeDtypeStruct((strip // 2, mid), F32)] * 2,
+            + [jax.ShapeDtypeStruct((strip, mid), F32)] * chips,
             in_specs=[smem] + [anywhere] * 7,
-            out_specs=[vmem] * (4 + chips),
+            out_specs=[vmem] * (2 + chips),
             scratch_shapes=[
                 pltpu.VMEM((2 * rows, 2 * rows), BF16),
                 pltpu.VMEM((2 * rows, mid), BF16),
@@ -340,8 +325,8 @@
             cost_estimate=pl.CostEstimate(flops=20 * 10**9, bytes_accessed=14 * 2**20, transcendentals=0),
             name="mid_blocks",
         )(mid_word, anc_cov, anc_swapped, flows[0], flow_swaps[0], flows[half], flow_swaps[half], cross)
-        c_high, c_low, mid_terms = outs[0], outs[1], outs[2 : 2 + chips]
-        mid_first = ring_start(outs[-2], outs[-1])
+        c_high, c_low, mid_terms = outs[0], outs[1], outs[2:]
+        mid_steps = [send(mid_terms[half], mid_terms[half + 1])]
         leaf_swaps.append(swap(tie(leaf_flows[-1], c_high)))
         leaf_parts = [x for pair in zip(leaf_flows, leaf_swaps) for x in pair]
 
@@ -371,14 +356,27 @@
             device_word, leaf_rows, anc_cov, anc_swapped, flows[0], flow_swaps[0], mid_diag_inv, diag_swapped,
             c_high, c_low, *leaf_parts,
         )
-        got = swap(tie(give, *mid_first))
+        got = swap(tie(give, *mid_steps[0]))
         leaf_terms = [keep[s] + got[s * band : (s + 1) * band] for s in range(chips)]
         leaf_far = leaf_terms[half]
-        leaf_first = ring_start(leaf_far[: band // 2], leaf_far[band // 2 :])
-        mid_second = ring_next(mid_terms, mid_first)
-        leaf_second = ring_next(leaf_terms, leaf_first)
-        mid_sum, trail = ring_end(mid_terms, mid_second, None)
-        leaf_sum, _ = ring_end(leaf_terms, leaf_second, None)
+        leaf_steps = [send(leaf_far[: band // 2], leaf_far[band // 2 :])]
+        for k in range(1, half):
+            up, down = mid_steps[-1]
+            up = up + mid_terms[half - k]
+            if k < half - 1:
+                mid_steps.append(send(up, down + mid_terms[half + 1 + k]))
+            else:
+                mid_steps.append((lax.ppermute(up, "row", perm(1)), down))
+            up, down = leaf_steps[-1]
+            if k == 1:
+                up, down = tie_pair((up, down), mid_steps[-1])
+            if k == 1:
+                up, down = add_half(leaf_terms[half - 1], up, True), add_half(leaf_terms[half + 1], down, False)
+            else:
+                up, down = up + leaf_terms[half - k], down + leaf_terms[half + k]
+            leaf_steps.append(send(up, down))
+        mid_sum = mid_terms[0] + mid_steps[-1][0] + mid_steps[-1][1]
+        leaf_sum = leaf_terms[0] + leaf_steps[-1][0] + leaf_steps[-1][1]
         mid_block = mid_diag_inv.astype(F32) + mid_sum
         leaf_block = leaf_diag_inv.astype(F32) + leaf_sum
         return mid_block, leaf_block

time: 124 us -> 123 us (level)
    ppermute x7, waiting for transfers between devices: 25.7 us -> 32.2 us  [leaf_step(): leaf_flows.append(lax.ppermute(tie(leaf_flows[-1], *deps), 'row', perm(1)))]
    ppermute x4, waiting for transfers between devices: 15.6 us -> 9.82 us  [factor_step(): flows.append(lax.ppermute(tie(flows[-1], *deps), 'row', pairs))]
    ppermute x16 -> x15, waiting for transfers between devices: 14 us -> 16.7 us  [the longest x7 10.1 us: send(): lax.ppermute(up, 'row', perm(1))]
    ppermute x16, waiting for transfers between devices: 5.53 us -> 2.88 us  [swap(): return lax.ppermute(x, 'row', swap_pairs)]
    ppermute x16 -> x15, starting transfers between devices: 17.9 us -> 16.4 us  [the longest x7 11.6 us: send(): lax.ppermute(up, 'row', perm(1))]
    unnamed x64 -> x68, local copies, waits for them, and re-layouts: 2.78 us -> 1.98 us
  transfers between devices with their start and end apart: 43 -> 42, of which waited for: 23 -> 21; matrix products, arithmetic and copies ran while one was open for 2% -> 2% of each run, Pallas kernels for 20% -> 20%
where the time goes in v3:
time: 123 us; the launch traced here: 122 us
  waiting for transfers between devices  61.6 us (50%)
  starting transfers between devices  30.4 us (25%)
  Pallas kernels  24.7 us (20%)
  other arithmetic  2.73 us (2%)
  local copies, waits for them, and re-layouts  1.99 us (2%)
    ppermute x7, waiting for transfers between devices, leaf_step(): leaf_flows.append(lax.ppermute(tie(leaf_flows[-1], *deps), 'row', perm(1)))  32.2 us
    ppermute x7, starting transfers between devices, send(): lax.ppermute(up, 'row', perm(1))  11.6 us
    pallas_call x1, Pallas kernels, local(): pl.pallas_call(lambda *refs: leaf_kernel(chips, snake, *refs), out_shape=...  10.7 us
    ppermute x7, waiting for transfers between devices, send(): lax.ppermute(up, 'row', perm(1))  10.1 us
    ppermute x4, waiting for transfers between devices, factor_step(): flows.append(lax.ppermute(tie(flows[-1], *deps), 'row', pairs))  9.82 us
    ppermute x4, starting transfers between devices, factor_step(): flows.append(lax.ppermute(tie(flows[-1], *deps), 'row', pairs))  7.23 us
    pallas_call x1, Pallas kernels, local(): pl.pallas_call(lambda *refs: mid_kernel(chips, snake, *refs), out_shape=[...  7.19 us
    pallas_call x1, Pallas kernels, near(): pl.pallas_call(lambda *refs: near_kernel(chips, snake, *refs), out_shape=...  6.79 us
  transfers between devices with their start and end apart: 42, of which 21 were waited for; matrix products, arithmetic and copies ran while one was open for 2% of the time, Pallas kernels for 20%

profile of v3, /device:TPU:0, one launch (start us, length us, event | category | flops | bytes accessed | tf_op | source)
XLA Modules:
  0.0 122.4 jit_solution(9797212700331783622)
XLA Ops:
  0.6 0.5 collective-permute-start.12
  1.1 2.6 %collective-permute-start.4 = (bf16[256,1024]{1,0:T(8,128)(2,1)}, bf16[256,1024]{1,0:T(8,128)(2,1)S(1)}, u32[]{:S(2)}, u32[]{:S(2)}) collective-permute-start(bf16[256,1024]{1,0:T(8,128)(2,1)} %refs_4_.1), channel_id=1, source_target_pairs={{0,2},{1,3},{4,0},{5,1},{8,4},{9,5},{12,8},{13,9},{14,12},{15,13},... | collective-permute-start | bytes 1572872 | tf_op jit(solution)/shard_map/ppermute | solution.py:280
  3.7 0.2 collective-permute-start.10
  3.9 0.3 collective-permute-start
  4.2 9.8 %collective-permute-done.refs_12_ = bf16[320,512]{1,0:T(8,128)(2,1)S(1)} collective-permute-done((bf16[320,512]{1,0:T(8,128)(2,1)}, bf16[320,512]{1,0:T(8,128)(2,1)S(1)}, u32[]{:S(2)}, u32[]{:S(2)}) %collective-permute-start) | collective-permute-done | bytes 327712 | tf_op jit(solution)/shard_map/ppermute | solution.py:290
  14.1 0.3 collective-permute-start.2
  14.4 2.1 %collective-permute-done.4.refs_5_ = bf16[256,1024]{1,0:T(8,128)(2,1)S(1)} collective-permute-done((bf16[256,1024]{1,0:T(8,128)(2,1)}, bf16[256,1024]{1,0:T(8,128)(2,1)S(1)}, u32[]{:S(2)}, u32[]{:S(2)}) %collective-permute-start.4) | collective-permute-done | bytes 524320 | tf_op jit(solution)/shard_map/ppermute | solution.py:280
  16.5 1.7 %collective-permute-start.11 = (bf16[256,1024]{1,0:T(8,128)(2,1)S(1)}, bf16[256,1024]{1,0:T(8,128)(2,1)}, u32[]{:S(2)}, u32[]{:S(2)}) collective-permute-start(bf16[256,1024]{1,0:T(8,128)(2,1)S(1)} %collective-permute-done.4.refs_5_), channel_id=1, source_target_pairs={{0,2},{1,3},{4,0},{5,1},{8,4},{9,5},{12,8},{13,9},{14,12},{15,13},... | collective-permute-start | bytes 1572872 | tf_op jit(solution)/shard_map/ppermute | solution.py:280
  18.3 5.0 %collective-permute-done.2.refs_14_ = bf16[320,512]{1,0:T(8,128)(2,1)S(1)} collective-permute-done((bf16[320,512]{1,0:T(8,128)(2,1)S(1)}, bf16[320,512]{1,0:T(8,128)(2,1)S(1)}, u32[]{:S(2)}, u32[]{:S(2)}) %collective-permute-start.2) | collective-permute-done | bytes 327712 | tf_op jit(solution)/shard_map/ppermute | solution.py:290
  23.3 0.3 collective-permute-start.5
  23.6 8.1 %collective-permute-done.5.refs_16_ = bf16[320,512]{1,0:T(8,128)(2,1)S(1)} collective-permute-done((bf16[320,512]{1,0:T(8,128)(2,1)S(1)}, bf16[320,512]{1,0:T(8,128)(2,1)S(1)}, u32[]{:S(2)}, u32[]{:S(2)}) %collective-permute-start.5) | collective-permute-done | bytes 327712 | tf_op jit(solution)/shard_map/ppermute | solution.py:290
  31.7 1.6 %collective-permute-start.16 = (bf16[256,1024]{1,0:T(8,128)(2,1)}, bf16[256,1024]{1,0:T(8,128)(2,1)}, u32[]{:S(2)}, u32[]{:S(2)}) collective-permute-start(bf16[256,1024]{1,0:T(8,128)(2,1)} %collective-permute-done.11.refs_7_), channel_id=1, source_target_pairs={{0,2},{1,3},{4,0},{5,1},{8,4},{9,5},{12,8},{13,9},{14,12},{15,13},... | collective-permute-start | bytes 1572872 | tf_op jit(solution)/shard_map/ppermute | solution.py:280
  33.3 0.5 collective-permute-start.7
  33.9 1.3 %collective-permute-done.7.refs_7_ = bf16[64,1024]{1,0:T(8,128)(2,1)S(1)} collective-permute-done((bf16[64,1024]{1,0:T(8,128)(2,1)}, bf16[64,1024]{1,0:T(8,128)(2,1)S(1)}, u32[]{:S(2)}, u32[]{:S(2)}) %collective-permute-start.7) | collective-permute-done | bytes 131104 | tf_op jit(solution)/shard_map/ppermute | solution.py:225
  35.2 0.5 collective-permute-start.8
  35.6 0.5 collective-permute-start.18
  36.1 7.7 %collective-permute-done.16.refs_9_ = bf16[256,1024]{1,0:T(8,128)(2,1)} collective-permute-done((bf16[256,1024]{1,0:T(8,128)(2,1)}, bf16[256,1024]{1,0:T(8,128)(2,1)}, u32[]{:S(2)}, u32[]{:S(2)}) %collective-permute-start.16) | collective-permute-done | bytes 524320 | tf_op jit(solution)/shard_map/ppermute | solution.py:280
  43.8 1.2 %collective-permute-done.8.refs_18_ = bf16[320,512]{1,0:T(8,128)(2,1)S(1)} collective-permute-done((bf16[320,512]{1,0:T(8,128)(2,1)S(1)}, bf16[320,512]{1,0:T(8,128)(2,1)S(1)}, u32[]{:S(2)}, u32[]{:S(2)}) %collective-permute-start.8) | collective-permute-done | bytes 327712 | tf_op jit(solution)/shard_map/ppermute | solution.py:290
  45.1 0.5 collective-permute-start.13
  45.7 0.2 copy-done.28
  45.9 1.3 %collective-permute-start.21 = (bf16[256,1024]{1,0:T(8,128)(2,1)}, bf16[256,1024]{1,0:T(8,128)(2,1)S(1)}, u32[]{:S(2)}, u32[]{:S(2)}) collective-permute-start(bf16[256,1024]{1,0:T(8,128)(2,1)} %collective-permute-done.16.refs_9_), channel_id=1, source_target_pairs={{4,0},{5,1},{8,4},{9,5},{12,8},{13,9},{14,12},{15,13},{20,16},{21,... | collective-permute-start | bytes 1572872 | tf_op jit(solution)/shard_map/ppermute | solution.py:280
  47.2 7.2 %collective-permute-done.13.refs_20_ = bf16[320,512]{1,0:T(8,128)(2,1)} collective-permute-done((bf16[320,512]{1,0:T(8,128)(2,1)S(1)}, bf16[320,512]{1,0:T(8,128)(2,1)}, u32[]{:S(2)}, u32[]{:S(2)}) %collective-permute-start.13) | collective-permute-done | bytes 327712 | tf_op jit(solution)/shard_map/ppermute | solution.py:290
  54.4 0.8 collective-permute-start.17
  55.2 6.8 %near_product.1.refs_7_ = f32[512,1024]{1,0:T(8,128)} custom-call(s32[1]{0:T(128)} %bitcast.refs_0_, bf16[256,4096]{1,0:T(8,128)(2,1)} %refs_2_.1, bf16[256,4096]{1,0:T(8,128)(2,1)} %copy-done.15, bf16[256,1024]{1,0:T(8,128)(2,1)} %refs_4_.1, bf16[256,1024]{1,0:T(8,128)(2,1)} %copy-done.16, bf16[256,1024]{1,0:T(8,128)(2,1)} %copy-done.17, ...), custom_call_target="tpu_custom_call" | custom-call | flops 7000000000 | bytes 10485760 | tf_op jit(solution)/shard_map/near_product/pallas_call | solution.py:250
  62.0 0.9 collective-permute-done.17.refs_22_
  62.9 0.5 collective-permute-start.20
  63.4 1.2 collective-permute-start.31
  64.6 0.9 collective-permute-done.20.refs_21_
  65.5 0.1 collective-permute-start.30
  65.6 0.8 copy-done.20
  66.5 7.2 %mid_blocks.1 = (bf16[512,1024]{1,0:T(8,128)(2,1)}, bf16[512,1024]{1,0:T(8,128)(2,1)}, f32[64,1024]{1,0:T(8,128)}, f32[64,1024]{1,0:T(8,128)}, f32[64,1024]{1,0:...) custom-call(s32[1]{0:T(128)} %bitcast.refs_0_, ...), custom_call_target="tpu_custom_call" | custom-call | flops 20000000000 | bytes 14680064 | tf_op jit(solution)/shard_map/mid_blocks/pallas_call | solution.py:308
  73.7 0.4 collective-permute-start.32
  74.1 1.4 %collective-permute-start.23 = (f32[64,1024]{1,0:T(8,128)}, f32[64,1024]{1,0:T(8,128)S(1)}, u32[]{:S(2)}, u32[]{:S(2)}) collective-permute-start(f32[64,1024]{1,0:T(8,128)} %get-tuple-element.51), channel_id=1, source_target_pairs={{0,4},{1,5},{4,8},{5,9},{8,12},{9,13},{12,14},{13,15},{14,10},{15,... | collective-permute-start | bytes 786440 | tf_op jit(solution)/shard_map/ppermute | solution.py:231
  75.6 0.6 collective-permute-start.27
  76.2 0.7 copy-done.31
  76.9 0.1 copy-done.32
  77.0 10.7 %leaf_blocks.1 = (f32[64,512]{1,0:T(8,128)}, f32[64,512]{1,0:T(8,128)}, f32[64,512]{1,0:T(8,128)}, f32[64,512]{1,0:T(8,128)}, f32[64,512]{1,0:T(8,128)}, /*index...) custom-call(s32[1]{0:T(128)} %bitcast.refs_0_, s32[2,80]{1,0:T(2,128)} %refs_1_.5, ...), custom_call_target="tpu_custom_call" | custom-call | flops 20000000000 | bytes 20971520 | tf_op jit(solution)/shard_map/leaf_blocks/pallas_call | solution.py:335
  87.9 1.6 %collective-permute-start.24 = (f32[64,1024]{1,0:T(8,128)S(1)}, f32[64,1024]{1,0:T(8,128)S(1)}, u32[]{:S(2)}, u32[]{:S(2)}) collective-permute-start(f32[64,1024]{1,0:T(8,128)S(1)} %add.79), channel_id=1, source_target_pairs={{0,4},{1,5},{4,8},{5,9},{8,12},{9,13},{12,14},{13,15},{14,10},{15,... | collective-permute-start | bytes 786440 | tf_op jit(solution)/shard_map/ppermute | solution.py:231
  89.5 0.6 collective-permute-start.28
  90.1 0.6 collective-permute-done.33
  90.7 1.0 slice_add_fusion.5
  91.7 1.6 %collective-permute-start.34 = (f32[32,512]{1,0:T(8,128)S(1)}, f32[32,512]{1,0:T(8,128)S(1)}, u32[]{:S(2)}, u32[]{:S(2)}) collective-permute-start(f32[32,512]{1,0:T(8,128)S(1)} %get-tuple-element.81), channel_id=1, source_target_pairs={{0,4},{1,5},{4,8},{5,9},{8,12},{9,13},{12,14},{13,15},{14,10},{15,... | collective-permute-start | bytes 196616 | tf_op jit(solution)/shard_map/ppermute | solution.py:231
  93.2 0.5 collective-permute-start.35
  93.8 3.3 %collective-permute-done.24 = f32[64,1024]{1,0:T(8,128)S(1)} collective-permute-done((f32[64,1024]{1,0:T(8,128)S(1)}, f32[64,1024]{1,0:T(8,128)S(1)}, u32[]{:S(2)}, u32[]{:S(2)}) %collective-permute-start.24) | collective-permute-done | bytes 262176 | tf_op jit(solution)/shard_map/ppermute | solution.py:231
  97.0 1.6 %collective-permute-done.28 = f32[64,1024]{1,0:T(8,128)S(1)} collective-permute-done((f32[64,1024]{1,0:T(8,128)S(1)}, f32[64,1024]{1,0:T(8,128)S(1)}, u32[]{:S(2)}, u32[]{:S(2)}) %collective-permute-start.28) | collective-permute-done | bytes 262176 | tf_op jit(solution)/shard_map/ppermute | solution.py:231
  98.6 1.0 collective-permute-done.35
  99.7 1.8 %collective-permute-start.36 = (f32[64,512]{1,0:T(8,128)S(1)}, f32[64,512]{1,0:T(8,128)S(1)}, u32[]{:S(2)}, u32[]{:S(2)}) collective-permute-start(f32[64,512]{1,0:T(8,128)S(1)} %get-tuple-element.78), channel_id=1, source_target_pairs={{0,4},{1,5},{4,8},{5,9},{8,12},{9,13},{12,14},{13,15},{14,10},{15,... | collective-permute-start | bytes 393224 | tf_op jit(solution)/shard_map/ppermute | solution.py:231
  101.5 0.3 collective-permute-start.39
  101.8 1.8 %collective-permute-start.25 = (f32[64,1024]{1,0:T(8,128)S(1)}, f32[64,1024]{1,0:T(8,128)S(1)}, u32[]{:S(2)}, u32[]{:S(2)}) collective-permute-start(f32[64,1024]{1,0:T(8,128)S(1)} %add.80), channel_id=1, source_target_pairs={{0,4},{1,5},{4,8},{5,9},{8,12},{9,13},{12,14},{13,15},{14,10},{15,... | collective-permute-start | bytes 786440 | tf_op jit(solution)/shard_map/ppermute | solution.py:231
  103.6 2.5 %collective-permute-done.36 = f32[64,512]{1,0:T(8,128)S(1)} collective-permute-done((f32[64,512]{1,0:T(8,128)S(1)}, f32[64,512]{1,0:T(8,128)S(1)}, u32[]{:S(2)}, u32[]{:S(2)}) %collective-permute-start.36) | collective-permute-done | bytes 131104 | tf_op jit(solution)/shard_map/ppermute | solution.py:231
  106.1 0.4 collective-permute-done.39
  106.6 1.6 %collective-permute-start.37 = (f32[64,512]{1,0:T(8,128)S(1)}, f32[64,512]{1,0:T(8,128)S(1)}, u32[]{:S(2)}, u32[]{:S(2)}) collective-permute-start(f32[64,512]{1,0:T(8,128)S(1)} %get-tuple-element.76), channel_id=1, source_target_pairs={{0,4},{1,5},{4,8},{5,9},{8,12},{9,13},{12,14},{13,15},{14,10},{15,... | collective-permute-start | bytes 393224 | tf_op jit(solution)/shard_map/ppermute | solution.py:231
  108.2 0.5 collective-permute-start.40
  108.7 0.3 collective-permute-start.29
  109.0 2.7 %collective-permute-done.25 = f32[64,1024]{1,0:T(8,128)S(1)} collective-permute-done((f32[64,1024]{1,0:T(8,128)S(1)}, f32[64,1024]{1,0:T(8,128)S(1)}, u32[]{:S(2)}, u32[]{:S(2)}) %collective-permute-start.25) | collective-permute-done | bytes 262176 | tf_op jit(solution)/shard_map/ppermute | solution.py:231
  111.8 1.8 %collective-permute-start.26 = (f32[64,1024]{1,0:T(8,128)S(1)}, f32[64,1024]{1,0:T(8,128)S(1)}, u32[]{:S(2)}, u32[]{:S(2)}) collective-permute-start(f32[64,1024]{1,0:T(8,128)S(1)} %add.81), channel_id=1, source_target_pairs={{0,4},{1,5},{4,8},{5,9},{8,12},{9,13},{12,14},{13,15},{14,10},{15,... | collective-permute-start | bytes 786440 | tf_op jit(solution)/shard_map/ppermute | solution.py:369
  113.6 1.0 collective-permute-done.37
  114.6 1.8 %collective-permute-start.38 = (f32[64,512]{1,0:T(8,128)S(1)}, f32[64,512]{1,0:T(8,128)S(1)}, u32[]{:S(2)}, u32[]{:S(2)}) collective-permute-start(f32[64,512]{1,0:T(8,128)S(1)} %get-tuple-element.74), channel_id=1, source_target_pairs={{0,4},{1,5},{4,8},{5,9},{8,12},{9,13},{12,14},{13,15},{14,10},{15,... | collective-permute-start | bytes 393224 | tf_op jit(solution)/shard_map/ppermute | solution.py:231
  116.4 0.3 collective-permute-start.41
  116.7 1.5 %collective-permute-done.29 = f32[64,1024]{1,0:T(8,128)S(1)} collective-permute-done((f32[64,1024]{1,0:T(8,128)S(1)}, f32[64,1024]{1,0:T(8,128)S(1)}, u32[]{:S(2)}, u32[]{:S(2)}) %collective-permute-start.29) | collective-permute-done | bytes 262176 | tf_op jit(solution)/shard_map/ppermute | solution.py:231
  118.2 2.1 %collective-permute-done.26 = f32[64,1024]{1,0:T(8,128)S(1)} collective-permute-done((f32[64,1024]{1,0:T(8,128)S(1)}, f32[64,1024]{1,0:T(8,128)S(1)}, u32[]{:S(2)}, u32[]{:S(2)}) %collective-permute-start.26) | collective-permute-done | bytes 262176 | tf_op jit(solution)/shard_map/ppermute | solution.py:369
  120.3 0.8 add_add_fusion
  121.1 0.6 collective-permute-done.38
  121.7 0.7 fusion.8
  (103 shorter events, 0.6 us)
Async XLA Ops:
  0.6 44.5 %collective-permute-start.12 = (bf16[256,4096]{1,0:T(8,128)(2,1)}, bf16[256,4096]{1,0:T(8,128)(2,1)S(1)}, u32[]{:S(2)}, u32[]{:S(2)}) collective-permute-start(bf16[256,4096]{1,0:T(8,128)(2,1)} %refs_2_.1), channel_id=1, source_target_pairs={{0,1},{1,0},{2,3},{3,2},{4,5},{5,4},{6,7},{7,6},{8,9},{9,8},{10,11... | collective-permute-start | bytes 6291464 | tf_op jit(solution)/shard_map/ppermute | solution.py:225
  1.1 15.4 %collective-permute-start.4 = (bf16[256,1024]{1,0:T(8,128)(2,1)}, bf16[256,1024]{1,0:T(8,128)(2,1)S(1)}, u32[]{:S(2)}, u32[]{:S(2)}) collective-permute-start(bf16[256,1024]{1,0:T(8,128)(2,1)} %refs_4_.1), channel_id=1, source_target_pairs={{0,2},{1,3},{4,0},{5,1},{8,4},{9,5},{12,8},{13,9},{14,12},{15,13},... | collective-permute-start | bytes 1572872 | tf_op jit(solution)/shard_map/ppermute | solution.py:280
  3.7 12.8 %collective-permute-start.10 = (bf16[256,1024]{1,0:T(8,128)(2,1)}, bf16[256,1024]{1,0:T(8,128)(2,1)S(1)}, u32[]{:S(2)}, u32[]{:S(2)}) collective-permute-start(bf16[256,1024]{1,0:T(8,128)(2,1)} %refs_4_.1), channel_id=1, source_target_pairs={{0,1},{1,0},{2,3},{3,2},{4,5},{5,4},{6,7},{7,6},{8,9},{9,8},{10,11... | collective-permute-start | bytes 1572872 | tf_op jit(solution)/shard_map/ppermute | solution.py:225
  3.9 10.2 %collective-permute-start = (bf16[320,512]{1,0:T(8,128)(2,1)}, bf16[320,512]{1,0:T(8,128)(2,1)S(1)}, u32[]{:S(2)}, u32[]{:S(2)}) collective-permute-start(bf16[320,512]{1,0:T(8,128)(2,1)} %refs_10_.1), channel_id=1, source_target_pairs={{0,4},{1,5},{4,8},{5,9},{8,12},{9,13},{12,14},{13,15},{14,10},{15,... | collective-permute-start | bytes 983048 | tf_op jit(solution)/shard_map/ppermute | solution.py:290
  4.2 9.8 %collective-permute-start.1 = (bf16[320,512]{1,0:T(8,128)(2,1)}, bf16[320,512]{1,0:T(8,128)(2,1)S(1)}, u32[]{:S(2)}, u32[]{:S(2)}) collective-permute-start(bf16[320,512]{1,0:T(8,128)(2,1)} %refs_10_.1), channel_id=1, source_target_pairs={{0,1},{1,0},{2,3},{3,2},{4,5},{5,4},{6,7},{7,6},{8,9},{9,8},{10,11... | collective-permute-start | bytes 983048 | tf_op jit(solution)/shard_map/ppermute | solution.py:225
  14.1 47.9 %copy-start.21 = (bf16[320,512]{1,0:T(8,128)(2,1)}, bf16[320,512]{1,0:T(8,128)(2,1)S(1)}, u32[]{:S(2)}) copy-start(bf16[320,512]{1,0:T(8,128)(2,1)S(1)} %collective-permute-done.refs_12_) | copy-start | bytes 983044
  14.1 9.2 %collective-permute-start.2 = (bf16[320,512]{1,0:T(8,128)(2,1)S(1)}, bf16[320,512]{1,0:T(8,128)(2,1)S(1)}, u32[]{:S(2)}, u32[]{:S(2)}) collective-permute-start(bf16[320,512]{1,0:T(8,128)(2,1)S(1)} %collective-permute-done.refs_12_), channel_id=1, source_target_pairs={{0,4},{1,5},{4,8},{5,9},{8,12},{9,13},{12,14},{13,15},{14,10},{15,... | collective-permute-start | bytes 983048 | tf_op jit(solution)/shard_map/ppermute | solution.py:290
  14.4 8.9 %collective-permute-start.3 = (bf16[320,512]{1,0:T(8,128)(2,1)S(1)}, bf16[320,512]{1,0:T(8,128)(2,1)S(1)}, u32[]{:S(2)}, u32[]{:S(2)}) collective-permute-start(bf16[320,512]{1,0:T(8,128)(2,1)S(1)} %collective-permute-done.refs_12_), channel_id=1, source_target_pairs={{0,1},{1,0},{2,3},{3,2},{4,5},{5,4},{6,7},{7,6},{8,9},{9,8},{10,11... | collective-permute-start | bytes 983048 | tf_op jit(solution)/shard_map/ppermute | solution.py:225
  16.5 28.6 %copy-start.17 = (bf16[256,1024]{1,0:T(8,128)(2,1)}, bf16[256,1024]{1,0:T(8,128)(2,1)S(1)}, u32[]{:S(2)}) copy-start(bf16[256,1024]{1,0:T(8,128)(2,1)S(1)} %collective-permute-done.4.refs_5_) | copy-start | bytes 1572868
  16.5 38.6 %copy-start.16 = (bf16[256,1024]{1,0:T(8,128)(2,1)}, bf16[256,1024]{1,0:T(8,128)(2,1)S(1)}, u32[]{:S(2)}) copy-start(bf16[256,1024]{1,0:T(8,128)(2,1)S(1)} %collective-permute-done.10.refs_4_.refs_5_) | copy-start | bytes 1572868
  16.5 15.2 %collective-permute-start.11 = (bf16[256,1024]{1,0:T(8,128)(2,1)S(1)}, bf16[256,1024]{1,0:T(8,128)(2,1)}, u32[]{:S(2)}, u32[]{:S(2)}) collective-permute-start(bf16[256,1024]{1,0:T(8,128)(2,1)S(1)} %collective-permute-done.4.refs_5_), channel_id=1, source_target_pairs={{0,2},{1,3},{4,0},{5,1},{8,4},{9,5},{12,8},{13,9},{14,12},{15,13},... | collective-permute-start | bytes 1572872 | tf_op jit(solution)/shard_map/ppermute | solution.py:280
  18.3 13.4 %collective-permute-start.15 = (bf16[256,1024]{1,0:T(8,128)(2,1)S(1)}, bf16[256,1024]{1,0:T(8,128)(2,1)S(1)}, u32[]{:S(2)}, u32[]{:S(2)}) collective-permute-start(bf16[256,1024]{1,0:T(8,128)(2,1)S(1)} %collective-permute-done.4.refs_5_), channel_id=1, source_target_pairs={{0,1},{1,0},{2,3},{3,2},{4,5},{5,4},{6,7},{7,6},{8,9},{9,8},{10,11... | collective-permute-start | bytes 1572872 | tf_op jit(solution)/shard_map/ppermute | solution.py:225
  23.3 22.3 %copy-start.23 = (bf16[320,512]{1,0:T(8,128)(2,1)}, bf16[320,512]{1,0:T(8,128)(2,1)S(1)}, u32[]{:S(2)}) copy-start(bf16[320,512]{1,0:T(8,128)(2,1)S(1)} %collective-permute-done.2.refs_14_) | copy-start | bytes 983044
  23.3 22.3 %copy-start.24 = (bf16[320,512]{1,0:T(8,128)(2,1)}, bf16[320,512]{1,0:T(8,128)(2,1)S(1)}, u32[]{:S(2)}) copy-start(bf16[320,512]{1,0:T(8,128)(2,1)S(1)} %collective-permute-done.3.refs_13_) | copy-start | bytes 983044
  23.3 8.4 %collective-permute-start.5 = (bf16[320,512]{1,0:T(8,128)(2,1)S(1)}, bf16[320,512]{1,0:T(8,128)(2,1)S(1)}, u32[]{:S(2)}, u32[]{:S(2)}) collective-permute-start(bf16[320,512]{1,0:T(8,128)(2,1)S(1)} %collective-permute-done.2.refs_14_), channel_id=1, source_target_pairs={{0,4},{1,5},{4,8},{5,9},{8,12},{9,13},{12,14},{13,15},{14,10},{15,... | collective-permute-start | bytes 983048 | tf_op jit(solution)/shard_map/ppermute | solution.py:290
  31.7 13.9 %copy-start.25 = (bf16[320,512]{1,0:T(8,128)(2,1)}, bf16[320,512]{1,0:T(8,128)(2,1)S(1)}, u32[]{:S(2)}) copy-start(bf16[320,512]{1,0:T(8,128)(2,1)S(1)} %collective-permute-done.5.refs_16_) | copy-start | bytes 983044
  31.7 13.9 %copy-start.18 = (bf16[256,1024]{1,0:T(8,128)(2,1)}, bf16[256,1024]{1,0:T(8,128)(2,1)S(1)}, u32[]{:S(2)}) copy-start(bf16[256,1024]{1,0:T(8,128)(2,1)S(1)} %collective-permute-done.15.refs_6_) | copy-start | bytes 1572868
  31.7 12.1 %collective-permute-start.16 = (bf16[256,1024]{1,0:T(8,128)(2,1)}, bf16[256,1024]{1,0:T(8,128)(2,1)}, u32[]{:S(2)}, u32[]{:S(2)}) collective-permute-start(bf16[256,1024]{1,0:T(8,128)(2,1)} %collective-permute-done.11.refs_7_), channel_id=1, source_target_pairs={{0,2},{1,3},{4,0},{5,1},{8,4},{9,5},{12,8},{13,9},{14,12},{15,13},... | collective-permute-start | bytes 1572872 | tf_op jit(solution)/shard_map/ppermute | solution.py:280
  33.3 1.8 %collective-permute-start.6 = (bf16[320,512]{1,0:T(8,128)(2,1)S(1)}, bf16[320,512]{1,0:T(8,128)(2,1)S(1)}, u32[]{:S(2)}, u32[]{:S(2)}) collective-permute-start(bf16[320,512]{1,0:T(8,128)(2,1)S(1)} %collective-permute-done.2.refs_14_), channel_id=1, source_target_pairs={{0,1},{1,0},{2,3},{3,2},{4,5},{5,4},{6,7},{7,6},{8,9},{9,8},{10,11... | collective-permute-start | bytes 983048 | tf_op jit(solution)/shard_map/ppermute | solution.py:225
  33.3 1.8 %collective-permute-start.7 = (bf16[64,1024]{1,0:T(8,128)(2,1)}, bf16[64,1024]{1,0:T(8,128)(2,1)S(1)}, u32[]{:S(2)}, u32[]{:S(2)}) collective-permute-start(bf16[64,1024]{1,0:T(8,128)(2,1)} %refs_6_.1), channel_id=1, source_target_pairs={{0,1},{1,0},{2,3},{3,2},{4,5},{5,4},{6,7},{7,6},{8,9},{9,8},{10,11... | collective-permute-start | bytes 393224 | tf_op jit(solution)/shard_map/ppermute | solution.py:225
  35.1 26.9 %copy-start.33 = (bf16[64,1024]{1,0:T(8,128)(2,1)}, bf16[64,1024]{1,0:T(8,128)(2,1)S(1)}, u32[]{:S(2)}) copy-start(bf16[64,1024]{1,0:T(8,128)(2,1)S(1)} %collective-permute-done.7.refs_7_) | copy-start | bytes 393220
  35.2 9.9 %collective-permute-start.8 = (bf16[320,512]{1,0:T(8,128)(2,1)S(1)}, bf16[320,512]{1,0:T(8,128)(2,1)S(1)}, u32[]{:S(2)}, u32[]{:S(2)}) collective-permute-start(bf16[320,512]{1,0:T(8,128)(2,1)S(1)} %collective-permute-done.5.refs_16_), channel_id=1, source_target_pairs={{0,4},{1,5},{4,8},{5,9},{8,12},{9,13},{12,14},{13,15},{14,10},{15,... | collective-permute-start | bytes 983048 | tf_op jit(solution)/shard_map/ppermute | solution.py:290
  35.6 9.5 %collective-permute-start.9 = (bf16[320,512]{1,0:T(8,128)(2,1)S(1)}, bf16[320,512]{1,0:T(8,128)(2,1)S(1)}, u32[]{:S(2)}, u32[]{:S(2)}) collective-permute-start(bf16[320,512]{1,0:T(8,128)(2,1)S(1)} %collective-permute-done.5.refs_16_), channel_id=1, source_target_pairs={{0,1},{1,0},{2,3},{3,2},{4,5},{5,4},{6,7},{7,6},{8,9},{9,8},{10,11... | collective-permute-start | bytes 983048 | tf_op jit(solution)/shard_map/ppermute | solution.py:225
  35.6 10.2 %collective-permute-start.18 = (bf16[256,1024]{1,0:T(8,128)(2,1)}, bf16[256,1024]{1,0:T(8,128)(2,1)}, u32[]{:S(2)}, u32[]{:S(2)}) collective-permute-start(bf16[256,1024]{1,0:T(8,128)(2,1)} %collective-permute-done.11.refs_7_), channel_id=1, source_target_pairs={{0,1},{1,0},{2,3},{3,2},{4,5},{5,4},{6,7},{7,6},{8,9},{9,8},{10,11... | collective-permute-start | bytes 1572872 | tf_op jit(solution)/shard_map/ppermute | solution.py:225
  43.8 11.3 %collective-permute-start.19 = (bf16[256,1024]{1,0:T(8,128)(2,1)}, bf16[256,1024]{1,0:T(8,128)(2,1)}, u32[]{:S(2)}, u32[]{:S(2)}) collective-permute-start(bf16[256,1024]{1,0:T(8,128)(2,1)} %collective-permute-done.16.refs_9_), channel_id=1, source_target_pairs={{0,1},{1,0},{2,3},{3,2},{4,5},{5,4},{6,7},{7,6},{8,9},{9,8},{10,11... | collective-permute-start | bytes 1572872 | tf_op jit(solution)/shard_map/ppermute | solution.py:225
  45.1 16.9 %copy-start.27 = (bf16[320,512]{1,0:T(8,128)(2,1)}, bf16[320,512]{1,0:T(8,128)(2,1)S(1)}, u32[]{:S(2)}) copy-start(bf16[320,512]{1,0:T(8,128)(2,1)S(1)} %collective-permute-done.8.refs_18_) | copy-start | bytes 983044
  45.1 9.3 %collective-permute-start.13 = (bf16[320,512]{1,0:T(8,128)(2,1)S(1)}, bf16[320,512]{1,0:T(8,128)(2,1)}, u32[]{:S(2)}, u32[]{:S(2)}) collective-permute-start(bf16[320,512]{1,0:T(8,128)(2,1)S(1)} %collective-permute-done.8.refs_18_), channel_id=1, source_target_pairs={{0,4},{1,5},{4,8},{5,9},{8,12},{9,13},{12,14},{13,15},{14,10},{15,... | collective-permute-start | bytes 983048 | tf_op jit(solution)/shard_map/ppermute | solution.py:290
  45.6 8.8 %collective-permute-start.14 = (bf16[320,512]{1,0:T(8,128)(2,1)S(1)}, bf16[320,512]{1,0:T(8,128)(2,1)}, u32[]{:S(2)}, u32[]{:S(2)}) collective-permute-start(bf16[320,512]{1,0:T(8,128)(2,1)S(1)} %collective-permute-done.8.refs_18_), channel_id=1, source_target_pairs={{0,1},{1,0},{2,3},{3,2},{4,5},{5,4},{6,7},{7,6},{8,9},{9,8},{10,11... | collective-permute-start | bytes 983048 | tf_op jit(solution)/shard_map/ppermute | solution.py:225
  45.9 17.0 %collective-permute-start.21 = (bf16[256,1024]{1,0:T(8,128)(2,1)}, bf16[256,1024]{1,0:T(8,128)(2,1)S(1)}, u32[]{:S(2)}, u32[]{:S(2)}) collective-permute-start(bf16[256,1024]{1,0:T(8,128)(2,1)} %collective-permute-done.16.refs_9_), channel_id=1, source_target_pairs={{4,0},{5,1},{8,4},{9,5},{12,8},{13,9},{14,12},{15,13},{20,16},{21,... | collective-permute-start | bytes 1572872 | tf_op jit(solution)/shard_map/ppermute | solution.py:280
  54.4 8.5 %collective-permute-start.17 = (bf16[320,512]{1,0:T(8,128)(2,1)}, bf16[320,512]{1,0:T(8,128)(2,1)}, u32[]{:S(2)}, u32[]{:S(2)}) collective-permute-start(bf16[320,512]{1,0:T(8,128)(2,1)} %collective-permute-done.13.refs_20_), channel_id=1, source_target_pairs={{0,4},{1,5},{4,8},{5,9},{8,12},{9,13},{12,14},{13,15},{14,10},{15,... | collective-permute-start | bytes 983048 | tf_op jit(solution)/shard_map/ppermute | solution.py:290
  62.9 2.7 %collective-permute-start.22 = (bf16[256,1024]{1,0:T(8,128)(2,1)S(1)}, bf16[256,1024]{1,0:T(8,128)(2,1)S(1)}, u32[]{:S(2)}, u32[]{:S(2)}) collective-permute-start(bf16[256,1024]{1,0:T(8,128)(2,1)S(1)} %collective-permute-done.21.refs_5_), channel_id=1, source_target_pairs={{0,1},{1,0},{2,3},{3,2},{4,5},{5,4},{6,7},{7,6},{8,9},{9,8},{10,11... | collective-permute-start | bytes 1572872 | tf_op jit(solution)/shard_map/ppermute | solution.py:225
  62.9 2.6 %collective-permute-start.20 = (bf16[320,512]{1,0:T(8,128)(2,1)}, bf16[320,512]{1,0:T(8,128)(2,1)S(1)}, u32[]{:S(2)}, u32[]{:S(2)}) collective-permute-start(bf16[320,512]{1,0:T(8,128)(2,1)} %collective-permute-done.13.refs_20_), channel_id=1, source_target_pairs={{0,1},{1,0},{2,3},{3,2},{4,5},{5,4},{6,7},{7,6},{8,9},{9,8},{10,11... | collective-permute-start | bytes 983048 | tf_op jit(solution)/shard_map/ppermute | solution.py:225
  63.4 10.3 %collective-permute-start.31 = (bf16[320,512]{1,0:T(8,128)(2,1)}, bf16[320,512]{1,0:T(8,128)(2,1)S(1)}, u32[]{:S(2)}, u32[]{:S(2)}) collective-permute-start(bf16[320,512]{1,0:T(8,128)(2,1)} %collective-permute-done.17.refs_22_), channel_id=1, source_target_pairs={{0,4},{1,5},{4,8},{5,9},{8,12},{9,13},{12,14},{13,15},{14,10},{15,... | collective-permute-start | bytes 983048 | tf_op jit(solution)/shard_map/ppermute | solution.py:290
  65.5 10.7 %collective-permute-start.30 = (bf16[320,512]{1,0:T(8,128)(2,1)}, bf16[320,512]{1,0:T(8,128)(2,1)S(1)}, u32[]{:S(2)}, u32[]{:S(2)}) collective-permute-start(bf16[320,512]{1,0:T(8,128)(2,1)} %collective-permute-done.17.refs_22_), channel_id=1, source_target_pairs={{0,1},{1,0},{2,3},{3,2},{4,5},{5,4},{6,7},{7,6},{8,9},{9,8},{10,11... | collective-permute-start | bytes 983048 | tf_op jit(solution)/shard_map/ppermute | solution.py:225
  73.7 2.5 %collective-permute-start.32 = (bf16[320,512]{1,0:T(8,128)(2,1)S(1)}, bf16[320,512]{1,0:T(8,128)(2,1)S(1)}, u32[]{:S(2)}, u32[]{:S(2)}) collective-permute-start(bf16[320,512]{1,0:T(8,128)(2,1)S(1)} %collective-permute-done.31.refs_24_), channel_id=1, source_target_pairs={{0,1},{1,0},{2,3},{3,2},{4,5},{5,4},{6,7},{7,6},{8,9},{9,8},{10,11... | collective-permute-start | bytes 983048 | tf_op jit(solution)/shard_map/ppermute | solution.py:225
  74.1 13.6 %collective-permute-start.23 = (f32[64,1024]{1,0:T(8,128)}, f32[64,1024]{1,0:T(8,128)S(1)}, u32[]{:S(2)}, u32[]{:S(2)}) collective-permute-start(f32[64,1024]{1,0:T(8,128)} %get-tuple-element.51), channel_id=1, source_target_pairs={{0,4},{1,5},{4,8},{5,9},{8,12},{9,13},{12,14},{13,15},{14,10},{15,... | collective-permute-start | bytes 786440 | tf_op jit(solution)/shard_map/ppermute | solution.py:231
  75.6 12.2 %collective-permute-start.27 = (f32[64,1024]{1,0:T(8,128)}, f32[64,1024]{1,0:T(8,128)S(1)}, u32[]{:S(2)}, u32[]{:S(2)}) collective-permute-start(f32[64,1024]{1,0:T(8,128)} %get-tuple-element.55), channel_id=1, source_target_pairs={{0,2},{1,3},{4,0},{5,1},{8,4},{9,5},{12,8},{13,9},{14,12},{15,13},... | collective-permute-start | bytes 786440 | tf_op jit(solution)/shard_map/ppermute | solution.py:231
  77.0 12.4 %copy-start.3 = (f32[64,1024]{1,0:T(8,128)S(1)}, f32[64,1024]{1,0:T(8,128)}, u32[]{:S(2)}) copy-start(f32[64,1024]{1,0:T(8,128)} %get-tuple-element.56) | copy-start | bytes 786436
  87.7 12.0 %copy-start.7 = (f32[64,512]{1,0:T(8,128)S(1)}, f32[64,512]{1,0:T(8,128)}, u32[]{:S(2)}) copy-start(f32[64,512]{1,0:T(8,128)} %get-tuple-element.65) | copy-start | bytes 393220
  87.7 14.1 %copy-start.2 = (f32[64,1024]{1,0:T(8,128)S(1)}, f32[64,1024]{1,0:T(8,128)}, u32[]{:S(2)}) copy-start(f32[64,1024]{1,0:T(8,128)} %get-tuple-element.53) | copy-start | bytes 786436
  87.7 18.8 %copy-start.12 = (f32[64,512]{1,0:T(8,128)S(1)}, f32[64,512]{1,0:T(8,128)}, u32[]{:S(2)}) copy-start(f32[64,512]{1,0:T(8,128)} %get-tuple-element.68) | copy-start | bytes 393220
  87.7 18.7 %copy-start.13 = (f32[64,512]{1,0:T(8,128)S(1)}, f32[64,512]{1,0:T(8,128)}, u32[]{:S(2)}) copy-start(f32[64,512]{1,0:T(8,128)} %get-tuple-element.72) | copy-start | bytes 393220
  87.8 2.9 %collective-permute-start.33 = (f32[512,512]{1,0:T(8,128)}, f32[512,512]{1,0:T(8,128)S(1)}, u32[]{:S(2)}, u32[]{:S(2)}) collective-permute-start(f32[512,512]{1,0:T(8,128)} %get-tuple-element.64), channel_id=1, source_target_pairs={{0,1},{1,0},{2,3},{3,2},{4,5},{5,4},{6,7},{7,6},{8,9},{9,8},{10,11... | collective-permute-start | bytes 3145736 | tf_op jit(solution)/shard_map/ppermute | solution.py:225
  87.9 9.2 %collective-permute-start.24 = (f32[64,1024]{1,0:T(8,128)S(1)}, f32[64,1024]{1,0:T(8,128)S(1)}, u32[]{:S(2)}, u32[]{:S(2)}) collective-permute-start(f32[64,1024]{1,0:T(8,128)S(1)} %add.79), channel_id=1, source_target_pairs={{0,4},{1,5},{4,8},{5,9},{8,12},{9,13},{12,14},{13,15},{14,10},{15,... | collective-permute-start | bytes 786440 | tf_op jit(solution)/shard_map/ppermute | solution.py:231
  89.4 19.2 %copy-start.1 = (f32[64,1024]{1,0:T(8,128)S(1)}, f32[64,1024]{1,0:T(8,128)}, u32[]{:S(2)}) copy-start(f32[64,1024]{1,0:T(8,128)} %get-tuple-element.57) | copy-start | bytes 786436
  89.5 9.2 %collective-permute-start.28 = (f32[64,1024]{1,0:T(8,128)S(1)}, f32[64,1024]{1,0:T(8,128)S(1)}, u32[]{:S(2)}, u32[]{:S(2)}) collective-permute-start(f32[64,1024]{1,0:T(8,128)S(1)} %add.83), channel_id=1, source_target_pairs={{0,2},{1,3},{4,0},{5,1},{8,4},{9,5},{12,8},{13,9},{14,12},{15,13},... | collective-permute-start | bytes 786440 | tf_op jit(solution)/shard_map/ppermute | solution.py:231
  90.7 21.0 %copy-start = (f32[64,1024]{1,0:T(8,128)S(1)}, f32[64,1024]{1,0:T(8,128)}, u32[]{:S(2)}) copy-start(f32[64,1024]{1,0:T(8,128)} %get-tuple-element.54) | copy-start | bytes 786436
  91.7 7.0 %collective-permute-start.34 = (f32[32,512]{1,0:T(8,128)S(1)}, f32[32,512]{1,0:T(8,128)S(1)}, u32[]{:S(2)}, u32[]{:S(2)}) collective-permute-start(f32[32,512]{1,0:T(8,128)S(1)} %get-tuple-element.81), channel_id=1, source_target_pairs={{0,4},{1,5},{4,8},{5,9},{8,12},{9,13},{12,14},{13,15},{14,10},{15,... | collective-permute-start | bytes 196616 | tf_op jit(solution)/shard_map/ppermute | solution.py:231
  93.2 6.4 %collective-permute-start.35 = (f32[32,512]{1,0:T(8,128)S(1)}, f32[32,512]{1,0:T(8,128)S(1)}, u32[]{:S(2)}, u32[]{:S(2)}) collective-permute-start(f32[32,512]{1,0:T(8,128)S(1)} %get-tuple-element.80), channel_id=1, source_target_pairs={{0,2},{1,3},{4,0},{5,1},{8,4},{9,5},{12,8},{13,9},{14,12},{15,13},... | collective-permute-start | bytes 196616 | tf_op jit(solution)/shard_map/ppermute | solution.py:231
  99.6 14.9 %copy-start.10 = (f32[64,512]{1,0:T(8,128)S(1)}, f32[64,512]{1,0:T(8,128)}, u32[]{:S(2)}) copy-start(f32[64,512]{1,0:T(8,128)} %get-tuple-element.69) | copy-start | bytes 393220
  99.7 14.9 %copy-start.11 = (f32[64,512]{1,0:T(8,128)S(1)}, f32[64,512]{1,0:T(8,128)}, u32[]{:S(2)}) copy-start(f32[64,512]{1,0:T(8,128)} %get-tuple-element.73) | copy-start | bytes 393220
  99.7 6.4 %collective-permute-start.36 = (f32[64,512]{1,0:T(8,128)S(1)}, f32[64,512]{1,0:T(8,128)S(1)}, u32[]{:S(2)}, u32[]{:S(2)}) collective-permute-start(f32[64,512]{1,0:T(8,128)S(1)} %get-tuple-element.78), channel_id=1, source_target_pairs={{0,4},{1,5},{4,8},{5,9},{8,12},{9,13},{12,14},{13,15},{14,10},{15,... | collective-permute-start | bytes 393224 | tf_op jit(solution)/shard_map/ppermute | solution.py:231
  101.5 5.0 %collective-permute-start.39 = (f32[64,512]{1,0:T(8,128)S(1)}, f32[64,512]{1,0:T(8,128)S(1)}, u32[]{:S(2)}, u32[]{:S(2)}) collective-permute-start(f32[64,512]{1,0:T(8,128)S(1)} %get-tuple-element.79), channel_id=1, source_target_pairs={{0,2},{1,3},{4,0},{5,1},{8,4},{9,5},{12,8},{13,9},{14,12},{15,13},... | collective-permute-start | bytes 393224 | tf_op jit(solution)/shard_map/ppermute | solution.py:231
  101.8 18.5 %copy-start.5 = (f32[64,1024]{1,0:T(8,128)S(1)}, f32[64,1024]{1,0:T(8,128)}, u32[]{:S(2)}) copy-start(f32[64,1024]{1,0:T(8,128)} %get-tuple-element.50) | copy-start | bytes 786436
  101.8 18.5 %copy-start.6 = (bf16[64,1024]{1,0:T(8,128)(2,1)S(1)}, bf16[64,1024]{1,0:T(8,128)(2,1)}, u32[]{:S(2)}) copy-start(bf16[64,1024]{1,0:T(8,128)(2,1)} %refs_6_.1) | copy-start | bytes 393220
  101.8 9.9 %collective-permute-start.25 = (f32[64,1024]{1,0:T(8,128)S(1)}, f32[64,1024]{1,0:T(8,128)S(1)}, u32[]{:S(2)}, u32[]{:S(2)}) collective-permute-start(f32[64,1024]{1,0:T(8,128)S(1)} %add.80), channel_id=1, source_target_pairs={{0,4},{1,5},{4,8},{5,9},{8,12},{9,13},{12,14},{13,15},{14,10},{15,... | collective-permute-start | bytes 786440 | tf_op jit(solution)/shard_map/ppermute | solution.py:231
  106.5 15.2 %copy-start.9 = (f32[64,512]{1,0:T(8,128)S(1)}, f32[64,512]{1,0:T(8,128)}, u32[]{:S(2)}) copy-start(f32[64,512]{1,0:T(8,128)} %get-tuple-element.62) | copy-start | bytes 393220
  106.5 15.2 %copy-start.14 = (bf16[64,512]{1,0:T(8,128)(2,1)S(1)}, bf16[64,512]{1,0:T(8,128)(2,1)}, u32[]{:S(2)}) copy-start(bf16[64,512]{1,0:T(8,128)(2,1)} %param.10) | copy-start | bytes 196612
  106.6 8.0 %collective-permute-start.37 = (f32[64,512]{1,0:T(8,128)S(1)}, f32[64,512]{1,0:T(8,128)S(1)}, u32[]{:S(2)}, u32[]{:S(2)}) collective-permute-start(f32[64,512]{1,0:T(8,128)S(1)} %get-tuple-element.76), channel_id=1, source_target_pairs={{0,4},{1,5},{4,8},{5,9},{8,12},{9,13},{12,14},{13,15},{14,10},{15,... | collective-permute-start | bytes 393224 | tf_op jit(solution)/shard_map/ppermute | solution.py:231
  108.2 6.4 %collective-permute-start.40 = (f32[64,512]{1,0:T(8,128)S(1)}, f32[64,512]{1,0:T(8,128)S(1)}, u32[]{:S(2)}, u32[]{:S(2)}) collective-permute-start(f32[64,512]{1,0:T(8,128)S(1)} %get-tuple-element.77), channel_id=1, source_target_pairs={{0,2},{1,3},{4,0},{5,1},{8,4},{9,5},{12,8},{13,9},{14,12},{15,13},... | collective-permute-start | bytes 393224 | tf_op jit(solution)/shard_map/ppermute | solution.py:231
  108.7 9.6 %collective-permute-start.29 = (f32[64,1024]{1,0:T(8,128)S(1)}, f32[64,1024]{1,0:T(8,128)S(1)}, u32[]{:S(2)}, u32[]{:S(2)}) collective-permute-start(f32[64,1024]{1,0:T(8,128)S(1)} %add.84), channel_id=1, source_target_pairs={{0,2},{1,3},{4,0},{5,1},{8,4},{9,5},{12,8},{13,9},{14,12},{15,13},... | collective-permute-start | bytes 786440 | tf_op jit(solution)/shard_map/ppermute | solution.py:231
  111.8 8.5 %collective-permute-start.26 = (f32[64,1024]{1,0:T(8,128)S(1)}, f32[64,1024]{1,0:T(8,128)S(1)}, u32[]{:S(2)}, u32[]{:S(2)}) collective-permute-start(f32[64,1024]{1,0:T(8,128)S(1)} %add.81), channel_id=1, source_target_pairs={{0,4},{1,5},{4,8},{5,9},{8,12},{9,13},{12,14},{13,15},{14,10},{15,... | collective-permute-start | bytes 786440 | tf_op jit(solution)/shard_map/ppermute | solution.py:369
  114.6 7.1 %collective-permute-start.38 = (f32[64,512]{1,0:T(8,128)S(1)}, f32[64,512]{1,0:T(8,128)S(1)}, u32[]{:S(2)}, u32[]{:S(2)}) collective-permute-start(f32[64,512]{1,0:T(8,128)S(1)} %get-tuple-element.74), channel_id=1, source_target_pairs={{0,4},{1,5},{4,8},{5,9},{8,12},{9,13},{12,14},{13,15},{14,10},{15,... | collective-permute-start | bytes 393224 | tf_op jit(solution)/shard_map/ppermute | solution.py:231
  116.4 5.3 %collective-permute-start.41 = (f32[64,512]{1,0:T(8,128)S(1)}, f32[64,512]{1,0:T(8,128)S(1)}, u32[]{:S(2)}, u32[]{:S(2)}) collective-permute-start(f32[64,512]{1,0:T(8,128)S(1)} %get-tuple-element.75), channel_id=1, source_target_pairs={{0,2},{1,3},{4,0},{5,1},{8,4},{9,5},{12,8},{13,9},{14,12},{15,13},... | collective-permute-start | bytes 393224 | tf_op jit(solution)/shard_map/ppermute | solution.py:231
  (12 other events, 62.4 us)

commit v4 on v3

--- a/solution.py
+++ b/solution.py
@@ -143,12 +143,6 @@
     fetch(copies, high_ref, highs, sems)
     fetch(copies, low_ref, lows, sems)
     early = len(copies)
-    for step in range(half + 1):
-        lane = pl.multiple_of(chip_at(place + step, chips, snake) * chip_rows, chip_rows)
-        at = step * chip_rows
-        for k in range(2):
-            into = left.at[k * rows : (k + 1) * rows, at : at + chip_rows]
-            fetch(copies, a_refs[k].at[:, pl.ds(lane, chip_rows)], into, sems)
     wide[...] = jnp.zeros_like(wide)
     for slot in range(chips):
         source = chip_at(place + chips - slot, chips, snake)
@@ -162,6 +156,12 @@
                     block = parts[2 * slot + side].at[i * TILE : (i + 1) * TILE, :]
                     pltpu.make_async_copy(block, wide.at[pl.ds(to, TILE), :], embed_sem).start()
 
+    for step in range(half + 1):
+        lane = pl.multiple_of(chip_at(place + step, chips, snake) * chip_rows, chip_rows)
+        at = step * chip_rows
+        for k in range(2):
+            into = left.at[k * rows : (k + 1) * rows, at : at + chip_rows]
+            fetch(copies, a_refs[k].at[:, pl.ds(lane, chip_rows)], into, sems)
     every = wide.at[: chips * count * TILE, :]
     pltpu.make_async_copy(every, every, embed_sem).wait()
     for step in range(half + 1):
@@ -302,7 +302,7 @@
             if step < chips - 1:
                 leaf_swaps.append(swap(leaf_flows[-1]))
         flow_swaps.append(swap(tie(flows[-1], leaf_flows[-2])))
-        mid_word = tie(device_word, leaf_flows[-2], leaf_swaps[-2])
+        mid_word = tie(device_word, leaf_flows[-2])
 
         strip = mid // devices
         outs = pl.pallas_call(

time: 123 us -> 121 us (0.984)
  transfers between devices with their start and end apart: 42 -> 42, of which waited for: 21 -> 22; matrix products, arithmetic and copies ran while one was open for 2% -> 2% of each run, Pallas kernels for 20% -> 20%
where the time goes in v4:
time: 121 us
  waiting for transfers between devices  61.6 us (51%)
  starting transfers between devices  29.9 us (25%)
  Pallas kernels  24 us (20%)
  other arithmetic  2.74 us (2%)
  local copies, waits for them, and re-layouts  2.01 us (2%)
    ppermute x7, waiting for transfers between devices, leaf_step(): leaf_flows.append(lax.ppermute(tie(leaf_flows[-1], *deps), 'row', perm(1)))  32.6 us
    ppermute x7, starting transfers between devices, send(): lax.ppermute(up, 'row', perm(1))  12.8 us
    ppermute x7, waiting for transfers between devices, send(): lax.ppermute(up, 'row', perm(1))  10.5 us
    pallas_call x1, Pallas kernels, local(): pl.pallas_call(lambda *refs: leaf_kernel(chips, snake, *refs), out_shape=...  9.95 us
    ppermute x4, waiting for transfers between devices, factor_step(): flows.append(lax.ppermute(tie(flows[-1], *deps), 'row', pairs))  9.82 us
    ppermute x4, starting transfers between devices, factor_step(): flows.append(lax.ppermute(tie(flows[-1], *deps), 'row', pairs))  7.23 us
    pallas_call x1, Pallas kernels, local(): pl.pallas_call(lambda *refs: mid_kernel(chips, snake, *refs), out_shape=[...  7.17 us
    pallas_call x1, Pallas kernels, near(): pl.pallas_call(lambda *refs: near_kernel(chips, snake, *refs), out_shape=...  6.88 us
  transfers between devices with their start and end apart: 42, of which 22 were waited for; matrix products, arithmetic and copies ran while one was open for 2% of the time, Pallas kernels for 20%

profile of v4, /device:TPU:0, one launch (start us, length us, event | category | flops | bytes accessed | tf_op | source)
XLA Modules:
  0.0 121.2 jit_solution(6068495355266416035)
XLA Ops:
  0.6 0.5 collective-permute-start.12
  1.1 2.6 %collective-permute-start.4 = (bf16[256,1024]{1,0:T(8,128)(2,1)}, bf16[256,1024]{1,0:T(8,128)(2,1)S(1)}, u32[]{:S(2)}, u32[]{:S(2)}) collective-permute-start(bf16[256,1024]{1,0:T(8,128)(2,1)} %refs_4_.1), channel_id=1, source_target_pairs={{0,2},{1,3},{4,0},{5,1},{8,4},{9,5},{12,8},{13,9},{14,12},{15,13},... | collective-permute-start | bytes 1572872 | tf_op jit(solution)/shard_map/ppermute | solution.py:280
  3.7 0.2 collective-permute-start.10
  3.9 0.3 collective-permute-start
  4.2 9.8 %collective-permute-done.refs_12_ = bf16[320,512]{1,0:T(8,128)(2,1)S(1)} collective-permute-done((bf16[320,512]{1,0:T(8,128)(2,1)}, bf16[320,512]{1,0:T(8,128)(2,1)S(1)}, u32[]{:S(2)}, u32[]{:S(2)}) %collective-permute-start) | collective-permute-done | bytes 327712 | tf_op jit(solution)/shard_map/ppermute | solution.py:290
  14.1 0.3 collective-permute-start.2
  14.4 2.1 %collective-permute-done.4.refs_5_ = bf16[256,1024]{1,0:T(8,128)(2,1)S(1)} collective-permute-done((bf16[256,1024]{1,0:T(8,128)(2,1)}, bf16[256,1024]{1,0:T(8,128)(2,1)S(1)}, u32[]{:S(2)}, u32[]{:S(2)}) %collective-permute-start.4) | collective-permute-done | bytes 524320 | tf_op jit(solution)/shard_map/ppermute | solution.py:280
  16.5 1.7 %collective-permute-start.11 = (bf16[256,1024]{1,0:T(8,128)(2,1)S(1)}, bf16[256,1024]{1,0:T(8,128)(2,1)}, u32[]{:S(2)}, u32[]{:S(2)}) collective-permute-start(bf16[256,1024]{1,0:T(8,128)(2,1)S(1)} %collective-permute-done.4.refs_5_), channel_id=1, source_target_pairs={{0,2},{1,3},{4,0},{5,1},{8,4},{9,5},{12,8},{13,9},{14,12},{15,13},... | collective-permute-start | bytes 1572872 | tf_op jit(solution)/shard_map/ppermute | solution.py:280
  18.3 5.0 %collective-permute-done.2.refs_14_ = bf16[320,512]{1,0:T(8,128)(2,1)S(1)} collective-permute-done((bf16[320,512]{1,0:T(8,128)(2,1)S(1)}, bf16[320,512]{1,0:T(8,128)(2,1)S(1)}, u32[]{:S(2)}, u32[]{:S(2)}) %collective-permute-start.2) | collective-permute-done | bytes 327712 | tf_op jit(solution)/shard_map/ppermute | solution.py:290
  23.3 0.3 collective-permute-start.5
  23.6 8.1 %collective-permute-done.5.refs_16_ = bf16[320,512]{1,0:T(8,128)(2,1)S(1)} collective-permute-done((bf16[320,512]{1,0:T(8,128)(2,1)S(1)}, bf16[320,512]{1,0:T(8,128)(2,1)S(1)}, u32[]{:S(2)}, u32[]{:S(2)}) %collective-permute-start.5) | collective-permute-done | bytes 327712 | tf_op jit(solution)/shard_map/ppermute | solution.py:290
  31.7 1.6 %collective-permute-start.16 = (bf16[256,1024]{1,0:T(8,128)(2,1)}, bf16[256,1024]{1,0:T(8,128)(2,1)}, u32[]{:S(2)}, u32[]{:S(2)}) collective-permute-start(bf16[256,1024]{1,0:T(8,128)(2,1)} %collective-permute-done.11.refs_7_), channel_id=1, source_target_pairs={{0,2},{1,3},{4,0},{5,1},{8,4},{9,5},{12,8},{13,9},{14,12},{15,13},... | collective-permute-start | bytes 1572872 | tf_op jit(solution)/shard_map/ppermute | solution.py:280
  33.3 0.5 collective-permute-start.7
  33.9 1.3 %collective-permute-done.7.refs_7_ = bf16[64,1024]{1,0:T(8,128)(2,1)S(1)} collective-permute-done((bf16[64,1024]{1,0:T(8,128)(2,1)}, bf16[64,1024]{1,0:T(8,128)(2,1)S(1)}, u32[]{:S(2)}, u32[]{:S(2)}) %collective-permute-start.7) | collective-permute-done | bytes 131104 | tf_op jit(solution)/shard_map/ppermute | solution.py:225
  35.2 0.5 collective-permute-start.8
  35.6 0.5 collective-permute-start.18
  36.1 7.7 %collective-permute-done.16.refs_9_ = bf16[256,1024]{1,0:T(8,128)(2,1)} collective-permute-done((bf16[256,1024]{1,0:T(8,128)(2,1)}, bf16[256,1024]{1,0:T(8,128)(2,1)}, u32[]{:S(2)}, u32[]{:S(2)}) %collective-permute-start.16) | collective-permute-done | bytes 524320 | tf_op jit(solution)/shard_map/ppermute | solution.py:280
  43.8 1.2 %collective-permute-done.8.refs_18_ = bf16[320,512]{1,0:T(8,128)(2,1)S(1)} collective-permute-done((bf16[320,512]{1,0:T(8,128)(2,1)S(1)}, bf16[320,512]{1,0:T(8,128)(2,1)S(1)}, u32[]{:S(2)}, u32[]{:S(2)}) %collective-permute-start.8) | collective-permute-done | bytes 327712 | tf_op jit(solution)/shard_map/ppermute | solution.py:290
  45.1 0.5 collective-permute-start.13
  45.7 0.2 copy-done.28
  45.9 1.3 %collective-permute-start.20 = (bf16[256,1024]{1,0:T(8,128)(2,1)}, bf16[256,1024]{1,0:T(8,128)(2,1)S(1)}, u32[]{:S(2)}, u32[]{:S(2)}) collective-permute-start(bf16[256,1024]{1,0:T(8,128)(2,1)} %collective-permute-done.16.refs_9_), channel_id=1, source_target_pairs={{4,0},{5,1},{8,4},{9,5},{12,8},{13,9},{14,12},{15,13},{20,16},{21,... | collective-permute-start | bytes 1572872 | tf_op jit(solution)/shard_map/ppermute | solution.py:280
  47.1 7.2 %collective-permute-done.13.refs_20_ = bf16[320,512]{1,0:T(8,128)(2,1)} collective-permute-done((bf16[320,512]{1,0:T(8,128)(2,1)S(1)}, bf16[320,512]{1,0:T(8,128)(2,1)}, u32[]{:S(2)}, u32[]{:S(2)}) %collective-permute-start.13) | collective-permute-done | bytes 327712 | tf_op jit(solution)/shard_map/ppermute | solution.py:290
  54.4 0.8 collective-permute-start.17
  55.2 6.9 %near_product.1.refs_7_ = f32[512,1024]{1,0:T(8,128)} custom-call(s32[1]{0:T(128)} %bitcast.refs_0_, bf16[256,4096]{1,0:T(8,128)(2,1)} %refs_2_.1, bf16[256,4096]{1,0:T(8,128)(2,1)} %copy-done.15, bf16[256,1024]{1,0:T(8,128)(2,1)} %refs_4_.1, bf16[256,1024]{1,0:T(8,128)(2,1)} %copy-done.16, bf16[256,1024]{1,0:T(8,128)(2,1)} %copy-done.17, ...), custom_call_target="tpu_custom_call" | custom-call | flops 7000000000 | bytes 10485760 | tf_op jit(solution)/shard_map/near_product/pallas_call | solution.py:250
  62.1 0.8 collective-permute-done.17.refs_22_
  62.9 0.5 collective-permute-start.29
  63.4 1.2 collective-permute-start.31
  64.6 0.3 collective-permute-done.21.refs_6_
  64.8 0.8 copy-done.20
  65.6 7.2 %mid_blocks.1 = (bf16[512,1024]{1,0:T(8,128)(2,1)}, bf16[512,1024]{1,0:T(8,128)(2,1)}, f32[64,1024]{1,0:T(8,128)}, f32[64,1024]{1,0:T(8,128)}, f32[64,1024]{1,0:...) custom-call(s32[1]{0:T(128)} %bitcast.refs_0_, ...), custom_call_target="tpu_custom_call" | custom-call | flops 20000000000 | bytes 14680064 | tf_op jit(solution)/shard_map/mid_blocks/pallas_call | solution.py:308
  72.8 0.5 collective-permute-done.31.refs_24_
  73.3 2.2 %collective-permute-start.22 = (f32[64,1024]{1,0:T(8,128)}, f32[64,1024]{1,0:T(8,128)S(1)}, u32[]{:S(2)}, u32[]{:S(2)}) collective-permute-start(f32[64,1024]{1,0:T(8,128)} %get-tuple-element.51), channel_id=1, source_target_pairs={{0,4},{1,5},{4,8},{5,9},{8,12},{9,13},{12,14},{13,15},{14,10},{15,... | collective-permute-start | bytes 786440 | tf_op jit(solution)/shard_map/ppermute | solution.py:231
  75.5 0.7 copy-done.29
  76.2 0.1 copy-done.31
  76.3 0.1 copy-done.32
  76.5 10.0 %leaf_blocks.1 = (f32[64,512]{1,0:T(8,128)}, f32[64,512]{1,0:T(8,128)}, f32[64,512]{1,0:T(8,128)}, f32[64,512]{1,0:T(8,128)}, f32[64,512]{1,0:T(8,128)}, /*index...) custom-call(s32[1]{0:T(128)} %bitcast.refs_0_, s32[2,80]{1,0:T(2,128)} %refs_1_.5, ...), custom_call_target="tpu_custom_call" | custom-call | flops 20000000000 | bytes 20971520 | tf_op jit(solution)/shard_map/leaf_blocks/pallas_call | solution.py:335
  86.5 0.1 collective-permute-start.33
  86.6 2.0 %collective-permute-start.23 = (f32[64,1024]{1,0:T(8,128)S(1)}, f32[64,1024]{1,0:T(8,128)S(1)}, u32[]{:S(2)}, u32[]{:S(2)}) collective-permute-start(f32[64,1024]{1,0:T(8,128)S(1)} %add.79), channel_id=1, source_target_pairs={{0,4},{1,5},{4,8},{5,9},{8,12},{9,13},{12,14},{13,15},{14,10},{15,... | collective-permute-start | bytes 786440 | tf_op jit(solution)/shard_map/ppermute | solution.py:231
  88.7 0.1 collective-permute-start.27
  88.8 0.6 collective-permute-done.33
  89.4 1.0 slice_add_fusion.5
  90.4 2.1 %collective-permute-start.34 = (f32[32,512]{1,0:T(8,128)S(1)}, f32[32,512]{1,0:T(8,128)S(1)}, u32[]{:S(2)}, u32[]{:S(2)}) collective-permute-start(f32[32,512]{1,0:T(8,128)S(1)} %get-tuple-element.81), channel_id=1, source_target_pairs={{0,4},{1,5},{4,8},{5,9},{8,12},{9,13},{12,14},{13,15},{14,10},{15,... | collective-permute-start | bytes 196616 | tf_op jit(solution)/shard_map/ppermute | solution.py:231
  92.5 3.3 %collective-permute-done.23 = f32[64,1024]{1,0:T(8,128)S(1)} collective-permute-done((f32[64,1024]{1,0:T(8,128)S(1)}, f32[64,1024]{1,0:T(8,128)S(1)}, u32[]{:S(2)}, u32[]{:S(2)}) %collective-permute-start.23) | collective-permute-done | bytes 262176 | tf_op jit(solution)/shard_map/ppermute | solution.py:231
  95.8 2.1 %collective-permute-done.27 = f32[64,1024]{1,0:T(8,128)S(1)} collective-permute-done((f32[64,1024]{1,0:T(8,128)S(1)}, f32[64,1024]{1,0:T(8,128)S(1)}, u32[]{:S(2)}, u32[]{:S(2)}) %collective-permute-start.27) | collective-permute-done | bytes 262176 | tf_op jit(solution)/shard_map/ppermute | solution.py:231
  97.9 0.7 collective-permute-done.35
  98.6 1.6 %collective-permute-start.36 = (f32[64,512]{1,0:T(8,128)S(1)}, f32[64,512]{1,0:T(8,128)S(1)}, u32[]{:S(2)}, u32[]{:S(2)}) collective-permute-start(f32[64,512]{1,0:T(8,128)S(1)} %get-tuple-element.78), channel_id=1, source_target_pairs={{0,4},{1,5},{4,8},{5,9},{8,12},{9,13},{12,14},{13,15},{14,10},{15,... | collective-permute-start | bytes 393224 | tf_op jit(solution)/shard_map/ppermute | solution.py:231
  100.3 0.4 collective-permute-start.39
  100.8 1.6 %collective-permute-start.24 = (f32[64,1024]{1,0:T(8,128)S(1)}, f32[64,1024]{1,0:T(8,128)S(1)}, u32[]{:S(2)}, u32[]{:S(2)}) collective-permute-start(f32[64,1024]{1,0:T(8,128)S(1)} %add.80), channel_id=1, source_target_pairs={{0,4},{1,5},{4,8},{5,9},{8,12},{9,13},{12,14},{13,15},{14,10},{15,... | collective-permute-start | bytes 786440 | tf_op jit(solution)/shard_map/ppermute | solution.py:231
  102.4 2.7 %collective-permute-done.36 = f32[64,512]{1,0:T(8,128)S(1)} collective-permute-done((f32[64,512]{1,0:T(8,128)S(1)}, f32[64,512]{1,0:T(8,128)S(1)}, u32[]{:S(2)}, u32[]{:S(2)}) %collective-permute-start.36) | collective-permute-done | bytes 131104 | tf_op jit(solution)/shard_map/ppermute | solution.py:231
  105.1 0.2 collective-permute-done.39
  105.3 1.6 %collective-permute-start.37 = (f32[64,512]{1,0:T(8,128)S(1)}, f32[64,512]{1,0:T(8,128)S(1)}, u32[]{:S(2)}, u32[]{:S(2)}) collective-permute-start(f32[64,512]{1,0:T(8,128)S(1)} %get-tuple-element.76), channel_id=1, source_target_pairs={{0,4},{1,5},{4,8},{5,9},{8,12},{9,13},{12,14},{13,15},{14,10},{15,... | collective-permute-start | bytes 393224 | tf_op jit(solution)/shard_map/ppermute | solution.py:231
  106.9 0.5 collective-permute-start.40
  107.4 0.5 collective-permute-start.28
  107.9 2.7 %collective-permute-done.24 = f32[64,1024]{1,0:T(8,128)S(1)} collective-permute-done((f32[64,1024]{1,0:T(8,128)S(1)}, f32[64,1024]{1,0:T(8,128)S(1)}, u32[]{:S(2)}, u32[]{:S(2)}) %collective-permute-start.24) | collective-permute-done | bytes 262176 | tf_op jit(solution)/shard_map/ppermute | solution.py:231
  110.7 1.6 %collective-permute-start.25 = (f32[64,1024]{1,0:T(8,128)S(1)}, f32[64,1024]{1,0:T(8,128)S(1)}, u32[]{:S(2)}, u32[]{:S(2)}) collective-permute-start(f32[64,1024]{1,0:T(8,128)S(1)} %add.81), channel_id=1, source_target_pairs={{0,4},{1,5},{4,8},{5,9},{8,12},{9,13},{12,14},{13,15},{14,10},{15,... | collective-permute-start | bytes 786440 | tf_op jit(solution)/shard_map/ppermute | solution.py:369
  112.4 1.1 collective-permute-done.37
  113.5 0.1 fusion.3
  113.6 1.6 %collective-permute-start.38 = (f32[64,512]{1,0:T(8,128)S(1)}, f32[64,512]{1,0:T(8,128)S(1)}, u32[]{:S(2)}, u32[]{:S(2)}) collective-permute-start(f32[64,512]{1,0:T(8,128)S(1)} %get-tuple-element.74), channel_id=1, source_target_pairs={{0,4},{1,5},{4,8},{5,9},{8,12},{9,13},{12,14},{13,15},{14,10},{15,... | collective-permute-start | bytes 393224 | tf_op jit(solution)/shard_map/ppermute | solution.py:231
  115.2 0.4 collective-permute-start.41
  115.7 1.3 %collective-permute-done.28 = f32[64,1024]{1,0:T(8,128)S(1)} collective-permute-done((f32[64,1024]{1,0:T(8,128)S(1)}, f32[64,1024]{1,0:T(8,128)S(1)}, u32[]{:S(2)}, u32[]{:S(2)}) %collective-permute-start.28) | collective-permute-done | bytes 262176 | tf_op jit(solution)/shard_map/ppermute | solution.py:231
  117.0 2.1 %collective-permute-done.25 = f32[64,1024]{1,0:T(8,128)S(1)} collective-permute-done((f32[64,1024]{1,0:T(8,128)S(1)}, f32[64,1024]{1,0:T(8,128)S(1)}, u32[]{:S(2)}, u32[]{:S(2)}) %collective-permute-start.25) | collective-permute-done | bytes 262176 | tf_op jit(solution)/shard_map/ppermute | solution.py:369
  119.1 0.8 add_add_fusion
  119.9 0.6 collective-permute-done.38
  120.5 0.7 fusion.8
  (103 shorter events, 0.5 us)
Async XLA Ops:
  0.6 44.5 %collective-permute-start.12 = (bf16[256,4096]{1,0:T(8,128)(2,1)}, bf16[256,4096]{1,0:T(8,128)(2,1)S(1)}, u32[]{:S(2)}, u32[]{:S(2)}) collective-permute-start(bf16[256,4096]{1,0:T(8,128)(2,1)} %refs_2_.1), channel_id=1, source_target_pairs={{0,1},{1,0},{2,3},{3,2},{4,5},{5,4},{6,7},{7,6},{8,9},{9,8},{10,11... | collective-permute-start | bytes 6291464 | tf_op jit(solution)/shard_map/ppermute | solution.py:225
  1.1 15.4 %collective-permute-start.4 = (bf16[256,1024]{1,0:T(8,128)(2,1)}, bf16[256,1024]{1,0:T(8,128)(2,1)S(1)}, u32[]{:S(2)}, u32[]{:S(2)}) collective-permute-start(bf16[256,1024]{1,0:T(8,128)(2,1)} %refs_4_.1), channel_id=1, source_target_pairs={{0,2},{1,3},{4,0},{5,1},{8,4},{9,5},{12,8},{13,9},{14,12},{15,13},... | collective-permute-start | bytes 1572872 | tf_op jit(solution)/shard_map/ppermute | solution.py:280
  3.7 12.8 %collective-permute-start.10 = (bf16[256,1024]{1,0:T(8,128)(2,1)}, bf16[256,1024]{1,0:T(8,128)(2,1)S(1)}, u32[]{:S(2)}, u32[]{:S(2)}) collective-permute-start(bf16[256,1024]{1,0:T(8,128)(2,1)} %refs_4_.1), channel_id=1, source_target_pairs={{0,1},{1,0},{2,3},{3,2},{4,5},{5,4},{6,7},{7,6},{8,9},{9,8},{10,11... | collective-permute-start | bytes 1572872 | tf_op jit(solution)/shard_map/ppermute | solution.py:225
  3.9 10.2 %collective-permute-start = (bf16[320,512]{1,0:T(8,128)(2,1)}, bf16[320,512]{1,0:T(8,128)(2,1)S(1)}, u32[]{:S(2)}, u32[]{:S(2)}) collective-permute-start(bf16[320,512]{1,0:T(8,128)(2,1)} %refs_10_.1), channel_id=1, source_target_pairs={{0,4},{1,5},{4,8},{5,9},{8,12},{9,13},{12,14},{13,15},{14,10},{15,... | collective-permute-start | bytes 983048 | tf_op jit(solution)/shard_map/ppermute | solution.py:290
  4.2 9.8 %collective-permute-start.1 = (bf16[320,512]{1,0:T(8,128)(2,1)}, bf16[320,512]{1,0:T(8,128)(2,1)S(1)}, u32[]{:S(2)}, u32[]{:S(2)}) collective-permute-start(bf16[320,512]{1,0:T(8,128)(2,1)} %refs_10_.1), channel_id=1, source_target_pairs={{0,1},{1,0},{2,3},{3,2},{4,5},{5,4},{6,7},{7,6},{8,9},{9,8},{10,11... | collective-permute-start | bytes 983048 | tf_op jit(solution)/shard_map/ppermute | solution.py:225
  14.1 48.0 %copy-start.21 = (bf16[320,512]{1,0:T(8,128)(2,1)}, bf16[320,512]{1,0:T(8,128)(2,1)S(1)}, u32[]{:S(2)}) copy-start(bf16[320,512]{1,0:T(8,128)(2,1)S(1)} %collective-permute-done.refs_12_) | copy-start | bytes 983044
  14.1 9.2 %collective-permute-start.2 = (bf16[320,512]{1,0:T(8,128)(2,1)S(1)}, bf16[320,512]{1,0:T(8,128)(2,1)S(1)}, u32[]{:S(2)}, u32[]{:S(2)}) collective-permute-start(bf16[320,512]{1,0:T(8,128)(2,1)S(1)} %collective-permute-done.refs_12_), channel_id=1, source_target_pairs={{0,4},{1,5},{4,8},{5,9},{8,12},{9,13},{12,14},{13,15},{14,10},{15,... | collective-permute-start | bytes 983048 | tf_op jit(solution)/shard_map/ppermute | solution.py:290
  14.4 8.9 %collective-permute-start.3 = (bf16[320,512]{1,0:T(8,128)(2,1)S(1)}, bf16[320,512]{1,0:T(8,128)(2,1)S(1)}, u32[]{:S(2)}, u32[]{:S(2)}) collective-permute-start(bf16[320,512]{1,0:T(8,128)(2,1)S(1)} %collective-permute-done.refs_12_), channel_id=1, source_target_pairs={{0,1},{1,0},{2,3},{3,2},{4,5},{5,4},{6,7},{7,6},{8,9},{9,8},{10,11... | collective-permute-start | bytes 983048 | tf_op jit(solution)/shard_map/ppermute | solution.py:225
  16.5 28.6 %copy-start.17 = (bf16[256,1024]{1,0:T(8,128)(2,1)}, bf16[256,1024]{1,0:T(8,128)(2,1)S(1)}, u32[]{:S(2)}) copy-start(bf16[256,1024]{1,0:T(8,128)(2,1)S(1)} %collective-permute-done.4.refs_5_) | copy-start | bytes 1572868
  16.5 38.6 %copy-start.16 = (bf16[256,1024]{1,0:T(8,128)(2,1)}, bf16[256,1024]{1,0:T(8,128)(2,1)S(1)}, u32[]{:S(2)}) copy-start(bf16[256,1024]{1,0:T(8,128)(2,1)S(1)} %collective-permute-done.10.refs_4_.refs_5_) | copy-start | bytes 1572868
  16.5 15.2 %collective-permute-start.11 = (bf16[256,1024]{1,0:T(8,128)(2,1)S(1)}, bf16[256,1024]{1,0:T(8,128)(2,1)}, u32[]{:S(2)}, u32[]{:S(2)}) collective-permute-start(bf16[256,1024]{1,0:T(8,128)(2,1)S(1)} %collective-permute-done.4.refs_5_), channel_id=1, source_target_pairs={{0,2},{1,3},{4,0},{5,1},{8,4},{9,5},{12,8},{13,9},{14,12},{15,13},... | collective-permute-start | bytes 1572872 | tf_op jit(solution)/shard_map/ppermute | solution.py:280
  18.3 13.4 %collective-permute-start.15 = (bf16[256,1024]{1,0:T(8,128)(2,1)S(1)}, bf16[256,1024]{1,0:T(8,128)(2,1)S(1)}, u32[]{:S(2)}, u32[]{:S(2)}) collective-permute-start(bf16[256,1024]{1,0:T(8,128)(2,1)S(1)} %collective-permute-done.4.refs_5_), channel_id=1, source_target_pairs={{0,1},{1,0},{2,3},{3,2},{4,5},{5,4},{6,7},{7,6},{8,9},{9,8},{10,11... | collective-permute-start | bytes 1572872 | tf_op jit(solution)/shard_map/ppermute | solution.py:225
  23.3 22.3 %copy-start.23 = (bf16[320,512]{1,0:T(8,128)(2,1)}, bf16[320,512]{1,0:T(8,128)(2,1)S(1)}, u32[]{:S(2)}) copy-start(bf16[320,512]{1,0:T(8,128)(2,1)S(1)} %collective-permute-done.2.refs_14_) | copy-start | bytes 983044
  23.3 22.3 %copy-start.24 = (bf16[320,512]{1,0:T(8,128)(2,1)}, bf16[320,512]{1,0:T(8,128)(2,1)S(1)}, u32[]{:S(2)}) copy-start(bf16[320,512]{1,0:T(8,128)(2,1)S(1)} %collective-permute-done.3.refs_13_) | copy-start | bytes 983044
  23.3 8.4 %collective-permute-start.5 = (bf16[320,512]{1,0:T(8,128)(2,1)S(1)}, bf16[320,512]{1,0:T(8,128)(2,1)S(1)}, u32[]{:S(2)}, u32[]{:S(2)}) collective-permute-start(bf16[320,512]{1,0:T(8,128)(2,1)S(1)} %collective-permute-done.2.refs_14_), channel_id=1, source_target_pairs={{0,4},{1,5},{4,8},{5,9},{8,12},{9,13},{12,14},{13,15},{14,10},{15,... | collective-permute-start | bytes 983048 | tf_op jit(solution)/shard_map/ppermute | solution.py:290
  31.7 13.9 %copy-start.25 = (bf16[320,512]{1,0:T(8,128)(2,1)}, bf16[320,512]{1,0:T(8,128)(2,1)S(1)}, u32[]{:S(2)}) copy-start(bf16[320,512]{1,0:T(8,128)(2,1)S(1)} %collective-permute-done.5.refs_16_) | copy-start | bytes 983044
  31.7 13.9 %copy-start.18 = (bf16[256,1024]{1,0:T(8,128)(2,1)}, bf16[256,1024]{1,0:T(8,128)(2,1)S(1)}, u32[]{:S(2)}) copy-start(bf16[256,1024]{1,0:T(8,128)(2,1)S(1)} %collective-permute-done.15.refs_6_) | copy-start | bytes 1572868
  31.7 12.1 %collective-permute-start.16 = (bf16[256,1024]{1,0:T(8,128)(2,1)}, bf16[256,1024]{1,0:T(8,128)(2,1)}, u32[]{:S(2)}, u32[]{:S(2)}) collective-permute-start(bf16[256,1024]{1,0:T(8,128)(2,1)} %collective-permute-done.11.refs_7_), channel_id=1, source_target_pairs={{0,2},{1,3},{4,0},{5,1},{8,4},{9,5},{12,8},{13,9},{14,12},{15,13},... | collective-permute-start | bytes 1572872 | tf_op jit(solution)/shard_map/ppermute | solution.py:280
  33.3 1.8 %collective-permute-start.6 = (bf16[320,512]{1,0:T(8,128)(2,1)S(1)}, bf16[320,512]{1,0:T(8,128)(2,1)S(1)}, u32[]{:S(2)}, u32[]{:S(2)}) collective-permute-start(bf16[320,512]{1,0:T(8,128)(2,1)S(1)} %collective-permute-done.2.refs_14_), channel_id=1, source_target_pairs={{0,1},{1,0},{2,3},{3,2},{4,5},{5,4},{6,7},{7,6},{8,9},{9,8},{10,11... | collective-permute-start | bytes 983048 | tf_op jit(solution)/shard_map/ppermute | solution.py:225
  33.3 1.8 %collective-permute-start.7 = (bf16[64,1024]{1,0:T(8,128)(2,1)}, bf16[64,1024]{1,0:T(8,128)(2,1)S(1)}, u32[]{:S(2)}, u32[]{:S(2)}) collective-permute-start(bf16[64,1024]{1,0:T(8,128)(2,1)} %refs_6_.1), channel_id=1, source_target_pairs={{0,1},{1,0},{2,3},{3,2},{4,5},{5,4},{6,7},{7,6},{8,9},{9,8},{10,11... | collective-permute-start | bytes 393224 | tf_op jit(solution)/shard_map/ppermute | solution.py:225
  35.1 27.0 %copy-start.33 = (bf16[64,1024]{1,0:T(8,128)(2,1)}, bf16[64,1024]{1,0:T(8,128)(2,1)S(1)}, u32[]{:S(2)}) copy-start(bf16[64,1024]{1,0:T(8,128)(2,1)S(1)} %collective-permute-done.7.refs_7_) | copy-start | bytes 393220
  35.2 9.9 %collective-permute-start.8 = (bf16[320,512]{1,0:T(8,128)(2,1)S(1)}, bf16[320,512]{1,0:T(8,128)(2,1)S(1)}, u32[]{:S(2)}, u32[]{:S(2)}) collective-permute-start(bf16[320,512]{1,0:T(8,128)(2,1)S(1)} %collective-permute-done.5.refs_16_), channel_id=1, source_target_pairs={{0,4},{1,5},{4,8},{5,9},{8,12},{9,13},{12,14},{13,15},{14,10},{15,... | collective-permute-start | bytes 983048 | tf_op jit(solution)/shard_map/ppermute | solution.py:290
  35.6 9.5 %collective-permute-start.9 = (bf16[320,512]{1,0:T(8,128)(2,1)S(1)}, bf16[320,512]{1,0:T(8,128)(2,1)S(1)}, u32[]{:S(2)}, u32[]{:S(2)}) collective-permute-start(bf16[320,512]{1,0:T(8,128)(2,1)S(1)} %collective-permute-done.5.refs_16_), channel_id=1, source_target_pairs={{0,1},{1,0},{2,3},{3,2},{4,5},{5,4},{6,7},{7,6},{8,9},{9,8},{10,11... | collective-permute-start | bytes 983048 | tf_op jit(solution)/shard_map/ppermute | solution.py:225
  35.6 10.2 %collective-permute-start.18 = (bf16[256,1024]{1,0:T(8,128)(2,1)}, bf16[256,1024]{1,0:T(8,128)(2,1)}, u32[]{:S(2)}, u32[]{:S(2)}) collective-permute-start(bf16[256,1024]{1,0:T(8,128)(2,1)} %collective-permute-done.11.refs_7_), channel_id=1, source_target_pairs={{0,1},{1,0},{2,3},{3,2},{4,5},{5,4},{6,7},{7,6},{8,9},{9,8},{10,11... | collective-permute-start | bytes 1572872 | tf_op jit(solution)/shard_map/ppermute | solution.py:225
  43.8 11.3 %collective-permute-start.19 = (bf16[256,1024]{1,0:T(8,128)(2,1)}, bf16[256,1024]{1,0:T(8,128)(2,1)}, u32[]{:S(2)}, u32[]{:S(2)}) collective-permute-start(bf16[256,1024]{1,0:T(8,128)(2,1)} %collective-permute-done.16.refs_9_), channel_id=1, source_target_pairs={{0,1},{1,0},{2,3},{3,2},{4,5},{5,4},{6,7},{7,6},{8,9},{9,8},{10,11... | collective-permute-start | bytes 1572872 | tf_op jit(solution)/shard_map/ppermute | solution.py:225
  45.1 17.0 %copy-start.27 = (bf16[320,512]{1,0:T(8,128)(2,1)}, bf16[320,512]{1,0:T(8,128)(2,1)S(1)}, u32[]{:S(2)}) copy-start(bf16[320,512]{1,0:T(8,128)(2,1)S(1)} %collective-permute-done.8.refs_18_) | copy-start | bytes 983044
  45.1 9.3 %collective-permute-start.13 = (bf16[320,512]{1,0:T(8,128)(2,1)S(1)}, bf16[320,512]{1,0:T(8,128)(2,1)}, u32[]{:S(2)}, u32[]{:S(2)}) collective-permute-start(bf16[320,512]{1,0:T(8,128)(2,1)S(1)} %collective-permute-done.8.refs_18_), channel_id=1, source_target_pairs={{0,4},{1,5},{4,8},{5,9},{8,12},{9,13},{12,14},{13,15},{14,10},{15,... | collective-permute-start | bytes 983048 | tf_op jit(solution)/shard_map/ppermute | solution.py:290
  45.6 8.8 %collective-permute-start.14 = (bf16[320,512]{1,0:T(8,128)(2,1)S(1)}, bf16[320,512]{1,0:T(8,128)(2,1)}, u32[]{:S(2)}, u32[]{:S(2)}) collective-permute-start(bf16[320,512]{1,0:T(8,128)(2,1)S(1)} %collective-permute-done.8.refs_18_), channel_id=1, source_target_pairs={{0,1},{1,0},{2,3},{3,2},{4,5},{5,4},{6,7},{7,6},{8,9},{9,8},{10,11... | collective-permute-start | bytes 983048 | tf_op jit(solution)/shard_map/ppermute | solution.py:225
  45.9 17.0 %collective-permute-start.20 = (bf16[256,1024]{1,0:T(8,128)(2,1)}, bf16[256,1024]{1,0:T(8,128)(2,1)S(1)}, u32[]{:S(2)}, u32[]{:S(2)}) collective-permute-start(bf16[256,1024]{1,0:T(8,128)(2,1)} %collective-permute-done.16.refs_9_), channel_id=1, source_target_pairs={{4,0},{5,1},{8,4},{9,5},{12,8},{13,9},{14,12},{15,13},{20,16},{21,... | collective-permute-start | bytes 1572872 | tf_op jit(solution)/shard_map/ppermute | solution.py:280
  54.4 8.5 %collective-permute-start.17 = (bf16[320,512]{1,0:T(8,128)(2,1)}, bf16[320,512]{1,0:T(8,128)(2,1)}, u32[]{:S(2)}, u32[]{:S(2)}) collective-permute-start(bf16[320,512]{1,0:T(8,128)(2,1)} %collective-permute-done.13.refs_20_), channel_id=1, source_target_pairs={{0,4},{1,5},{4,8},{5,9},{8,12},{9,13},{12,14},{13,15},{14,10},{15,... | collective-permute-start | bytes 983048 | tf_op jit(solution)/shard_map/ppermute | solution.py:290
  62.9 2.0 %collective-permute-start.21 = (bf16[256,1024]{1,0:T(8,128)(2,1)S(1)}, bf16[256,1024]{1,0:T(8,128)(2,1)S(1)}, u32[]{:S(2)}, u32[]{:S(2)}) collective-permute-start(bf16[256,1024]{1,0:T(8,128)(2,1)S(1)} %collective-permute-done.20.refs_5_), channel_id=1, source_target_pairs={{0,1},{1,0},{2,3},{3,2},{4,5},{5,4},{6,7},{7,6},{8,9},{9,8},{10,11... | collective-permute-start | bytes 1572872 | tf_op jit(solution)/shard_map/ppermute | solution.py:225
  62.9 12.6 %collective-permute-start.29 = (bf16[320,512]{1,0:T(8,128)(2,1)}, bf16[320,512]{1,0:T(8,128)(2,1)S(1)}, u32[]{:S(2)}, u32[]{:S(2)}) collective-permute-start(bf16[320,512]{1,0:T(8,128)(2,1)} %collective-permute-done.13.refs_20_), channel_id=1, source_target_pairs={{0,1},{1,0},{2,3},{3,2},{4,5},{5,4},{6,7},{7,6},{8,9},{9,8},{10,11... | collective-permute-start | bytes 983048 | tf_op jit(solution)/shard_map/ppermute | solution.py:225
  63.4 9.9 %collective-permute-start.31 = (bf16[320,512]{1,0:T(8,128)(2,1)}, bf16[320,512]{1,0:T(8,128)(2,1)S(1)}, u32[]{:S(2)}, u32[]{:S(2)}) collective-permute-start(bf16[320,512]{1,0:T(8,128)(2,1)} %collective-permute-done.17.refs_22_), channel_id=1, source_target_pairs={{0,4},{1,5},{4,8},{5,9},{8,12},{9,13},{12,14},{13,15},{14,10},{15,... | collective-permute-start | bytes 983048 | tf_op jit(solution)/shard_map/ppermute | solution.py:290
  64.6 10.9 %collective-permute-start.30 = (bf16[320,512]{1,0:T(8,128)(2,1)}, bf16[320,512]{1,0:T(8,128)(2,1)S(1)}, u32[]{:S(2)}, u32[]{:S(2)}) collective-permute-start(bf16[320,512]{1,0:T(8,128)(2,1)} %collective-permute-done.17.refs_22_), channel_id=1, source_target_pairs={{0,1},{1,0},{2,3},{3,2},{4,5},{5,4},{6,7},{7,6},{8,9},{9,8},{10,11... | collective-permute-start | bytes 983048 | tf_op jit(solution)/shard_map/ppermute | solution.py:225
  73.3 2.2 %collective-permute-start.32 = (bf16[320,512]{1,0:T(8,128)(2,1)S(1)}, bf16[320,512]{1,0:T(8,128)(2,1)S(1)}, u32[]{:S(2)}, u32[]{:S(2)}) collective-permute-start(bf16[320,512]{1,0:T(8,128)(2,1)S(1)} %collective-permute-done.31.refs_24_), channel_id=1, source_target_pairs={{0,1},{1,0},{2,3},{3,2},{4,5},{5,4},{6,7},{7,6},{8,9},{9,8},{10,11... | collective-permute-start | bytes 983048 | tf_op jit(solution)/shard_map/ppermute | solution.py:225
  73.3 13.2 %collective-permute-start.22 = (f32[64,1024]{1,0:T(8,128)}, f32[64,1024]{1,0:T(8,128)S(1)}, u32[]{:S(2)}, u32[]{:S(2)}) collective-permute-start(f32[64,1024]{1,0:T(8,128)} %get-tuple-element.51), channel_id=1, source_target_pairs={{0,4},{1,5},{4,8},{5,9},{8,12},{9,13},{12,14},{13,15},{14,10},{15,... | collective-permute-start | bytes 786440 | tf_op jit(solution)/shard_map/ppermute | solution.py:231
  75.5 11.0 %collective-permute-start.26 = (f32[64,1024]{1,0:T(8,128)}, f32[64,1024]{1,0:T(8,128)S(1)}, u32[]{:S(2)}, u32[]{:S(2)}) collective-permute-start(f32[64,1024]{1,0:T(8,128)} %get-tuple-element.55), channel_id=1, source_target_pairs={{0,2},{1,3},{4,0},{5,1},{8,4},{9,5},{12,8},{13,9},{14,12},{15,13},... | collective-permute-start | bytes 786440 | tf_op jit(solution)/shard_map/ppermute | solution.py:231
  76.4 12.2 %copy-start.3 = (f32[64,1024]{1,0:T(8,128)S(1)}, f32[64,1024]{1,0:T(8,128)}, u32[]{:S(2)}) copy-start(f32[64,1024]{1,0:T(8,128)} %get-tuple-element.56) | copy-start | bytes 786436
  86.4 12.2 %copy-start.7 = (f32[64,512]{1,0:T(8,128)S(1)}, f32[64,512]{1,0:T(8,128)}, u32[]{:S(2)}) copy-start(f32[64,512]{1,0:T(8,128)} %get-tuple-element.65) | copy-start | bytes 393220
  86.4 14.3 %copy-start.2 = (f32[64,1024]{1,0:T(8,128)S(1)}, f32[64,1024]{1,0:T(8,128)}, u32[]{:S(2)}) copy-start(f32[64,1024]{1,0:T(8,128)} %get-tuple-element.53) | copy-start | bytes 786436
  86.4 18.8 %copy-start.12 = (f32[64,512]{1,0:T(8,128)S(1)}, f32[64,512]{1,0:T(8,128)}, u32[]{:S(2)}) copy-start(f32[64,512]{1,0:T(8,128)} %get-tuple-element.68) | copy-start | bytes 393220
  86.5 18.8 %copy-start.13 = (f32[64,512]{1,0:T(8,128)S(1)}, f32[64,512]{1,0:T(8,128)}, u32[]{:S(2)}) copy-start(f32[64,512]{1,0:T(8,128)} %get-tuple-element.72) | copy-start | bytes 393220
  86.5 2.9 %collective-permute-start.33 = (f32[512,512]{1,0:T(8,128)}, f32[512,512]{1,0:T(8,128)S(1)}, u32[]{:S(2)}, u32[]{:S(2)}) collective-permute-start(f32[512,512]{1,0:T(8,128)} %get-tuple-element.64), channel_id=1, source_target_pairs={{0,1},{1,0},{2,3},{3,2},{4,5},{5,4},{6,7},{7,6},{8,9},{9,8},{10,11... | collective-permute-start | bytes 3145736 | tf_op jit(solution)/shard_map/ppermute | solution.py:225
  86.6 9.1 %collective-permute-start.23 = (f32[64,1024]{1,0:T(8,128)S(1)}, f32[64,1024]{1,0:T(8,128)S(1)}, u32[]{:S(2)}, u32[]{:S(2)}) collective-permute-start(f32[64,1024]{1,0:T(8,128)S(1)} %add.79), channel_id=1, source_target_pairs={{0,4},{1,5},{4,8},{5,9},{8,12},{9,13},{12,14},{13,15},{14,10},{15,... | collective-permute-start | bytes 786440 | tf_op jit(solution)/shard_map/ppermute | solution.py:231
  88.7 18.7 %copy-start.1 = (f32[64,1024]{1,0:T(8,128)S(1)}, f32[64,1024]{1,0:T(8,128)}, u32[]{:S(2)}) copy-start(f32[64,1024]{1,0:T(8,128)} %get-tuple-element.57) | copy-start | bytes 786436
  88.7 9.2 %collective-permute-start.27 = (f32[64,1024]{1,0:T(8,128)S(1)}, f32[64,1024]{1,0:T(8,128)S(1)}, u32[]{:S(2)}, u32[]{:S(2)}) collective-permute-start(f32[64,1024]{1,0:T(8,128)S(1)} %add.83), channel_id=1, source_target_pairs={{0,2},{1,3},{4,0},{5,1},{8,4},{9,5},{12,8},{13,9},{14,12},{15,13},... | collective-permute-start | bytes 786440 | tf_op jit(solution)/shard_map/ppermute | solution.py:231
  89.4 21.3 %copy-start = (f32[64,1024]{1,0:T(8,128)S(1)}, f32[64,1024]{1,0:T(8,128)}, u32[]{:S(2)}) copy-start(f32[64,1024]{1,0:T(8,128)} %get-tuple-element.54) | copy-start | bytes 786436
  90.4 7.5 %collective-permute-start.34 = (f32[32,512]{1,0:T(8,128)S(1)}, f32[32,512]{1,0:T(8,128)S(1)}, u32[]{:S(2)}, u32[]{:S(2)}) collective-permute-start(f32[32,512]{1,0:T(8,128)S(1)} %get-tuple-element.81), channel_id=1, source_target_pairs={{0,4},{1,5},{4,8},{5,9},{8,12},{9,13},{12,14},{13,15},{14,10},{15,... | collective-permute-start | bytes 196616 | tf_op jit(solution)/shard_map/ppermute | solution.py:231
  92.5 6.1 %collective-permute-start.35 = (f32[32,512]{1,0:T(8,128)S(1)}, f32[32,512]{1,0:T(8,128)S(1)}, u32[]{:S(2)}, u32[]{:S(2)}) collective-permute-start(f32[32,512]{1,0:T(8,128)S(1)} %get-tuple-element.80), channel_id=1, source_target_pairs={{0,2},{1,3},{4,0},{5,1},{8,4},{9,5},{12,8},{13,9},{14,12},{15,13},... | collective-permute-start | bytes 196616 | tf_op jit(solution)/shard_map/ppermute | solution.py:231
  98.6 14.9 %copy-start.10 = (f32[64,512]{1,0:T(8,128)S(1)}, f32[64,512]{1,0:T(8,128)}, u32[]{:S(2)}) copy-start(f32[64,512]{1,0:T(8,128)} %get-tuple-element.69) | copy-start | bytes 393220
  98.6 14.9 %copy-start.11 = (f32[64,512]{1,0:T(8,128)S(1)}, f32[64,512]{1,0:T(8,128)}, u32[]{:S(2)}) copy-start(f32[64,512]{1,0:T(8,128)} %get-tuple-element.73) | copy-start | bytes 393220
  98.6 6.4 %collective-permute-start.36 = (f32[64,512]{1,0:T(8,128)S(1)}, f32[64,512]{1,0:T(8,128)S(1)}, u32[]{:S(2)}, u32[]{:S(2)}) collective-permute-start(f32[64,512]{1,0:T(8,128)S(1)} %get-tuple-element.78), channel_id=1, source_target_pairs={{0,4},{1,5},{4,8},{5,9},{8,12},{9,13},{12,14},{13,15},{14,10},{15,... | collective-permute-start | bytes 393224 | tf_op jit(solution)/shard_map/ppermute | solution.py:231
  100.3 5.0 %collective-permute-start.39 = (f32[64,512]{1,0:T(8,128)S(1)}, f32[64,512]{1,0:T(8,128)S(1)}, u32[]{:S(2)}, u32[]{:S(2)}) collective-permute-start(f32[64,512]{1,0:T(8,128)S(1)} %get-tuple-element.79), channel_id=1, source_target_pairs={{0,2},{1,3},{4,0},{5,1},{8,4},{9,5},{12,8},{13,9},{14,12},{15,13},... | collective-permute-start | bytes 393224 | tf_op jit(solution)/shard_map/ppermute | solution.py:231
  100.7 18.4 %copy-start.5 = (f32[64,1024]{1,0:T(8,128)S(1)}, f32[64,1024]{1,0:T(8,128)}, u32[]{:S(2)}) copy-start(f32[64,1024]{1,0:T(8,128)} %get-tuple-element.50) | copy-start | bytes 786436
  100.7 18.4 %copy-start.6 = (bf16[64,1024]{1,0:T(8,128)(2,1)S(1)}, bf16[64,1024]{1,0:T(8,128)(2,1)}, u32[]{:S(2)}) copy-start(bf16[64,1024]{1,0:T(8,128)(2,1)} %refs_6_.1) | copy-start | bytes 393220
  100.8 9.9 %collective-permute-start.24 = (f32[64,1024]{1,0:T(8,128)S(1)}, f32[64,1024]{1,0:T(8,128)S(1)}, u32[]{:S(2)}, u32[]{:S(2)}) collective-permute-start(f32[64,1024]{1,0:T(8,128)S(1)} %add.80), channel_id=1, source_target_pairs={{0,4},{1,5},{4,8},{5,9},{8,12},{9,13},{12,14},{13,15},{14,10},{15,... | collective-permute-start | bytes 786440 | tf_op jit(solution)/shard_map/ppermute | solution.py:231
  105.3 15.2 %copy-start.9 = (f32[64,512]{1,0:T(8,128)S(1)}, f32[64,512]{1,0:T(8,128)}, u32[]{:S(2)}) copy-start(f32[64,512]{1,0:T(8,128)} %get-tuple-element.62) | copy-start | bytes 393220
  105.3 15.2 %copy-start.14 = (bf16[64,512]{1,0:T(8,128)(2,1)S(1)}, bf16[64,512]{1,0:T(8,128)(2,1)}, u32[]{:S(2)}) copy-start(bf16[64,512]{1,0:T(8,128)(2,1)} %param.10) | copy-start | bytes 196612
  105.3 8.2 %collective-permute-start.37 = (f32[64,512]{1,0:T(8,128)S(1)}, f32[64,512]{1,0:T(8,128)S(1)}, u32[]{:S(2)}, u32[]{:S(2)}) collective-permute-start(f32[64,512]{1,0:T(8,128)S(1)} %get-tuple-element.76), channel_id=1, source_target_pairs={{0,4},{1,5},{4,8},{5,9},{8,12},{9,13},{12,14},{13,15},{14,10},{15,... | collective-permute-start | bytes 393224 | tf_op jit(solution)/shard_map/ppermute | solution.py:231
  106.9 6.6 %collective-permute-start.40 = (f32[64,512]{1,0:T(8,128)S(1)}, f32[64,512]{1,0:T(8,128)S(1)}, u32[]{:S(2)}, u32[]{:S(2)}) collective-permute-start(f32[64,512]{1,0:T(8,128)S(1)} %get-tuple-element.77), channel_id=1, source_target_pairs={{0,2},{1,3},{4,0},{5,1},{8,4},{9,5},{12,8},{13,9},{14,12},{15,13},... | collective-permute-start | bytes 393224 | tf_op jit(solution)/shard_map/ppermute | solution.py:231
  107.4 9.5 %collective-permute-start.28 = (f32[64,1024]{1,0:T(8,128)S(1)}, f32[64,1024]{1,0:T(8,128)S(1)}, u32[]{:S(2)}, u32[]{:S(2)}) collective-permute-start(f32[64,1024]{1,0:T(8,128)S(1)} %add.84), channel_id=1, source_target_pairs={{0,2},{1,3},{4,0},{5,1},{8,4},{9,5},{12,8},{13,9},{14,12},{15,13},... | collective-permute-start | bytes 786440 | tf_op jit(solution)/shard_map/ppermute | solution.py:231
  110.7 8.4 %collective-permute-start.25 = (f32[64,1024]{1,0:T(8,128)S(1)}, f32[64,1024]{1,0:T(8,128)S(1)}, u32[]{:S(2)}, u32[]{:S(2)}) collective-permute-start(f32[64,1024]{1,0:T(8,128)S(1)} %add.81), channel_id=1, source_target_pairs={{0,4},{1,5},{4,8},{5,9},{8,12},{9,13},{12,14},{13,15},{14,10},{15,... | collective-permute-start | bytes 786440 | tf_op jit(solution)/shard_map/ppermute | solution.py:369
  113.6 6.9 %collective-permute-start.38 = (f32[64,512]{1,0:T(8,128)S(1)}, f32[64,512]{1,0:T(8,128)S(1)}, u32[]{:S(2)}, u32[]{:S(2)}) collective-permute-start(f32[64,512]{1,0:T(8,128)S(1)} %get-tuple-element.74), channel_id=1, source_target_pairs={{0,4},{1,5},{4,8},{5,9},{8,12},{9,13},{12,14},{13,15},{14,10},{15,... | collective-permute-start | bytes 393224 | tf_op jit(solution)/shard_map/ppermute | solution.py:231
  115.2 5.3 %collective-permute-start.41 = (f32[64,512]{1,0:T(8,128)S(1)}, f32[64,512]{1,0:T(8,128)S(1)}, u32[]{:S(2)}, u32[]{:S(2)}) collective-permute-start(f32[64,512]{1,0:T(8,128)S(1)} %get-tuple-element.75), channel_id=1, source_target_pairs={{0,2},{1,3},{4,0},{5,1},{8,4},{9,5},{12,8},{13,9},{14,12},{15,13},... | collective-permute-start | bytes 393224 | tf_op jit(solution)/shard_map/ppermute | solution.py:231
  (12 other events, 53.6 us)

commit v5 on v4

--- a/solution.py
+++ b/solution.py
@@ -88,7 +88,6 @@
     place = place_of(chip, chips, snake)
     rows, mid = own_refs[0].shape
     copies = []
-    fetch(copies, cross_ref, cross, sems)
     for side in range(2):
         fetch(copies, own_refs[side], own.at[side * rows : (side + 1) * rows, :], sems)
     owner = chip_at(place + half, chips, snake)
@@ -96,10 +95,13 @@
         lane = (2 * owner + (core if side == 0 else 1 - core)) * rows
         fetch_columns(copies, a_refs, lane, rows, left, side * rows, sems)
         fetch(copies, far_refs[side], right.at[side * rows : (side + 1) * rows, :], sems)
-    for copy in copies:
-        copy.wait()
+    fetch(copies, cross_ref, cross, sems)
+    for copy in copies[:-1]:
+        copy.wait()
+    far = mm(left[...], right[...])
+    copies[-1].wait()
     factor = own[...]
-    high, low = split(cross[...] + mm(left[...], right[...]))
+    high, low = split(cross[...] + far)
     high_ref[...] = high
     low_ref[...] = low
     for k, x in enumerate((factor, high, low)):

time: 121 us -> 121 us (level)
  no operation moved by 1% of the time
where the time goes in v5:
time: 121 us
  waiting for transfers between devices  61.5 us (51%)
  starting transfers between devices  29.9 us (25%)
  Pallas kernels  24 us (20%)
  other arithmetic  2.75 us (2%)
  local copies, waits for them, and re-layouts  2.01 us (2%)
    ppermute x7, waiting for transfers between devices, leaf_step(): leaf_flows.append(lax.ppermute(tie(leaf_flows[-1], *deps), 'row', perm(1)))  32.6 us
    ppermute x7, starting transfers between devices, send(): lax.ppermute(up, 'row', perm(1))  12.8 us
    ppermute x7, waiting for transfers between devices, send(): lax.ppermute(up, 'row', perm(1))  10.5 us
    pallas_call x1, Pallas kernels, local(): pl.pallas_call(lambda *refs: leaf_kernel(chips, snake, *refs), out_shape=...  9.95 us
    ppermute x4, waiting for transfers between devices, factor_step(): flows.append(lax.ppermute(tie(flows[-1], *deps), 'row', pairs))  9.82 us
    ppermute x4, starting transfers between devices, factor_step(): flows.append(lax.ppermute(tie(flows[-1], *deps), 'row', pairs))  7.23 us
    pallas_call x1, Pallas kernels, local(): pl.pallas_call(lambda *refs: mid_kernel(chips, snake, *refs), out_shape=[...  7.22 us
    pallas_call x1, Pallas kernels, near(): pl.pallas_call(lambda *refs: near_kernel(chips, snake, *refs), out_shape=...  6.88 us
  transfers between devices with their start and end apart: 42, of which 22 were waited for; matrix products, arithmetic and copies ran while one was open for 2% of the time, Pallas kernels for 20%

profile of v5, /device:TPU:0, one launch (start us, length us, event | category | flops | bytes accessed | tf_op | source)
XLA Modules:
  0.0 121.3 jit_solution(1324651756849670699)
XLA Ops:
  0.6 0.5 collective-permute-start.12
  1.1 2.6 %collective-permute-start.4 = (bf16[256,1024]{1,0:T(8,128)(2,1)}, bf16[256,1024]{1,0:T(8,128)(2,1)S(1)}, u32[]{:S(2)}, u32[]{:S(2)}) collective-permute-start(bf16[256,1024]{1,0:T(8,128)(2,1)} %refs_4_.1), channel_id=1, source_target_pairs={{0,2},{1,3},{4,0},{5,1},{8,4},{9,5},{12,8},{13,9},{14,12},{15,13},... | collective-permute-start | bytes 1572872 | tf_op jit(solution)/shard_map/ppermute | solution.py:282
  3.7 0.2 collective-permute-start.10
  3.9 0.3 collective-permute-start
  4.2 9.8 %collective-permute-done.refs_12_ = bf16[320,512]{1,0:T(8,128)(2,1)S(1)} collective-permute-done((bf16[320,512]{1,0:T(8,128)(2,1)}, bf16[320,512]{1,0:T(8,128)(2,1)S(1)}, u32[]{:S(2)}, u32[]{:S(2)}) %collective-permute-start) | collective-permute-done | bytes 327712 | tf_op jit(solution)/shard_map/ppermute | solution.py:292
  14.1 0.3 collective-permute-start.2
  14.4 2.1 %collective-permute-done.4.refs_5_ = bf16[256,1024]{1,0:T(8,128)(2,1)S(1)} collective-permute-done((bf16[256,1024]{1,0:T(8,128)(2,1)}, bf16[256,1024]{1,0:T(8,128)(2,1)S(1)}, u32[]{:S(2)}, u32[]{:S(2)}) %collective-permute-start.4) | collective-permute-done | bytes 524320 | tf_op jit(solution)/shard_map/ppermute | solution.py:282
  16.5 1.7 %collective-permute-start.11 = (bf16[256,1024]{1,0:T(8,128)(2,1)S(1)}, bf16[256,1024]{1,0:T(8,128)(2,1)}, u32[]{:S(2)}, u32[]{:S(2)}) collective-permute-start(bf16[256,1024]{1,0:T(8,128)(2,1)S(1)} %collective-permute-done.4.refs_5_), channel_id=1, source_target_pairs={{0,2},{1,3},{4,0},{5,1},{8,4},{9,5},{12,8},{13,9},{14,12},{15,13},... | collective-permute-start | bytes 1572872 | tf_op jit(solution)/shard_map/ppermute | solution.py:282
  18.3 5.0 %collective-permute-done.2.refs_14_ = bf16[320,512]{1,0:T(8,128)(2,1)S(1)} collective-permute-done((bf16[320,512]{1,0:T(8,128)(2,1)S(1)}, bf16[320,512]{1,0:T(8,128)(2,1)S(1)}, u32[]{:S(2)}, u32[]{:S(2)}) %collective-permute-start.2) | collective-permute-done | bytes 327712 | tf_op jit(solution)/shard_map/ppermute | solution.py:292
  23.3 0.3 collective-permute-start.5
  23.6 8.1 %collective-permute-done.5.refs_16_ = bf16[320,512]{1,0:T(8,128)(2,1)S(1)} collective-permute-done((bf16[320,512]{1,0:T(8,128)(2,1)S(1)}, bf16[320,512]{1,0:T(8,128)(2,1)S(1)}, u32[]{:S(2)}, u32[]{:S(2)}) %collective-permute-start.5) | collective-permute-done | bytes 327712 | tf_op jit(solution)/shard_map/ppermute | solution.py:292
  31.7 1.6 %collective-permute-start.16 = (bf16[256,1024]{1,0:T(8,128)(2,1)}, bf16[256,1024]{1,0:T(8,128)(2,1)}, u32[]{:S(2)}, u32[]{:S(2)}) collective-permute-start(bf16[256,1024]{1,0:T(8,128)(2,1)} %collective-permute-done.11.refs_7_), channel_id=1, source_target_pairs={{0,2},{1,3},{4,0},{5,1},{8,4},{9,5},{12,8},{13,9},{14,12},{15,13},... | collective-permute-start | bytes 1572872 | tf_op jit(solution)/shard_map/ppermute | solution.py:282
  33.3 0.5 collective-permute-start.7
  33.9 1.3 %collective-permute-done.7.refs_7_ = bf16[64,1024]{1,0:T(8,128)(2,1)S(1)} collective-permute-done((bf16[64,1024]{1,0:T(8,128)(2,1)}, bf16[64,1024]{1,0:T(8,128)(2,1)S(1)}, u32[]{:S(2)}, u32[]{:S(2)}) %collective-permute-start.7) | collective-permute-done | bytes 131104 | tf_op jit(solution)/shard_map/ppermute | solution.py:227
  35.2 0.5 collective-permute-start.8
  35.6 0.5 collective-permute-start.18
  36.1 7.7 %collective-permute-done.16.refs_9_ = bf16[256,1024]{1,0:T(8,128)(2,1)} collective-permute-done((bf16[256,1024]{1,0:T(8,128)(2,1)}, bf16[256,1024]{1,0:T(8,128)(2,1)}, u32[]{:S(2)}, u32[]{:S(2)}) %collective-permute-start.16) | collective-permute-done | bytes 524320 | tf_op jit(solution)/shard_map/ppermute | solution.py:282
  43.8 1.2 %collective-permute-done.8.refs_18_ = bf16[320,512]{1,0:T(8,128)(2,1)S(1)} collective-permute-done((bf16[320,512]{1,0:T(8,128)(2,1)S(1)}, bf16[320,512]{1,0:T(8,128)(2,1)S(1)}, u32[]{:S(2)}, u32[]{:S(2)}) %collective-permute-start.8) | collective-permute-done | bytes 327712 | tf_op jit(solution)/shard_map/ppermute | solution.py:292
  45.1 0.5 collective-permute-start.13
  45.7 0.2 copy-done.28
  45.9 1.3 %collective-permute-start.20 = (bf16[256,1024]{1,0:T(8,128)(2,1)}, bf16[256,1024]{1,0:T(8,128)(2,1)S(1)}, u32[]{:S(2)}, u32[]{:S(2)}) collective-permute-start(bf16[256,1024]{1,0:T(8,128)(2,1)} %collective-permute-done.16.refs_9_), channel_id=1, source_target_pairs={{4,0},{5,1},{8,4},{9,5},{12,8},{13,9},{14,12},{15,13},{20,16},{21,... | collective-permute-start | bytes 1572872 | tf_op jit(solution)/shard_map/ppermute | solution.py:282
  47.1 7.2 %collective-permute-done.13.refs_20_ = bf16[320,512]{1,0:T(8,128)(2,1)} collective-permute-done((bf16[320,512]{1,0:T(8,128)(2,1)S(1)}, bf16[320,512]{1,0:T(8,128)(2,1)}, u32[]{:S(2)}, u32[]{:S(2)}) %collective-permute-start.13) | collective-permute-done | bytes 327712 | tf_op jit(solution)/shard_map/ppermute | solution.py:292
  54.4 0.8 collective-permute-start.17
  55.2 6.9 %near_product.1.refs_7_ = f32[512,1024]{1,0:T(8,128)} custom-call(s32[1]{0:T(128)} %bitcast.refs_0_, bf16[256,4096]{1,0:T(8,128)(2,1)} %refs_2_.1, bf16[256,4096]{1,0:T(8,128)(2,1)} %copy-done.15, bf16[256,1024]{1,0:T(8,128)(2,1)} %refs_4_.1, bf16[256,1024]{1,0:T(8,128)(2,1)} %copy-done.16, bf16[256,1024]{1,0:T(8,128)(2,1)} %copy-done.17, ...), custom_call_target="tpu_custom_call" | custom-call | flops 7000000000 | bytes 10485760 | tf_op jit(solution)/shard_map/near_product/pallas_call | solution.py:252
  62.1 0.8 collective-permute-done.17.refs_22_
  62.9 0.5 collective-permute-start.29
  63.4 1.2 collective-permute-start.31
  64.6 0.3 collective-permute-done.21.refs_6_
  64.8 0.8 copy-done.20
  65.6 7.2 %mid_blocks.1 = (bf16[512,1024]{1,0:T(8,128)(2,1)}, bf16[512,1024]{1,0:T(8,128)(2,1)}, f32[64,1024]{1,0:T(8,128)}, f32[64,1024]{1,0:T(8,128)}, f32[64,1024]{1,0:...) custom-call(s32[1]{0:T(128)} %bitcast.refs_0_, ...), custom_call_target="tpu_custom_call" | custom-call | flops 20000000000 | bytes 14680064 | tf_op jit(solution)/shard_map/mid_blocks/pallas_call | solution.py:310
  72.9 0.4 collective-permute-done.31.refs_24_
  73.3 2.2 %collective-permute-start.22 = (f32[64,1024]{1,0:T(8,128)}, f32[64,1024]{1,0:T(8,128)S(1)}, u32[]{:S(2)}, u32[]{:S(2)}) collective-permute-start(f32[64,1024]{1,0:T(8,128)} %get-tuple-element.51), channel_id=1, source_target_pairs={{0,4},{1,5},{4,8},{5,9},{8,12},{9,13},{12,14},{13,15},{14,10},{15,... | collective-permute-start | bytes 786440 | tf_op jit(solution)/shard_map/ppermute | solution.py:233
  75.6 0.7 copy-done.29
  76.3 0.1 copy-done.31
  76.4 0.1 copy-done.32
  76.5 10.0 %leaf_blocks.1 = (f32[64,512]{1,0:T(8,128)}, f32[64,512]{1,0:T(8,128)}, f32[64,512]{1,0:T(8,128)}, f32[64,512]{1,0:T(8,128)}, f32[64,512]{1,0:T(8,128)}, /*index...) custom-call(s32[1]{0:T(128)} %bitcast.refs_0_, s32[2,80]{1,0:T(2,128)} %refs_1_.5, ...), custom_call_target="tpu_custom_call" | custom-call | flops 20000000000 | bytes 20971520 | tf_op jit(solution)/shard_map/leaf_blocks/pallas_call | solution.py:337
  86.5 0.1 collective-permute-start.33
  86.7 2.1 %collective-permute-start.23 = (f32[64,1024]{1,0:T(8,128)S(1)}, f32[64,1024]{1,0:T(8,128)S(1)}, u32[]{:S(2)}, u32[]{:S(2)}) collective-permute-start(f32[64,1024]{1,0:T(8,128)S(1)} %add.79), channel_id=1, source_target_pairs={{0,4},{1,5},{4,8},{5,9},{8,12},{9,13},{12,14},{13,15},{14,10},{15,... | collective-permute-start | bytes 786440 | tf_op jit(solution)/shard_map/ppermute | solution.py:233
  88.8 0.1 collective-permute-start.27
  88.8 0.6 collective-permute-done.33
  89.5 1.0 slice_add_fusion.5
  90.5 2.1 %collective-permute-start.34 = (f32[32,512]{1,0:T(8,128)S(1)}, f32[32,512]{1,0:T(8,128)S(1)}, u32[]{:S(2)}, u32[]{:S(2)}) collective-permute-start(f32[32,512]{1,0:T(8,128)S(1)} %get-tuple-element.81), channel_id=1, source_target_pairs={{0,4},{1,5},{4,8},{5,9},{8,12},{9,13},{12,14},{13,15},{14,10},{15,... | collective-permute-start | bytes 196616 | tf_op jit(solution)/shard_map/ppermute | solution.py:233
  92.5 3.3 %collective-permute-done.23 = f32[64,1024]{1,0:T(8,128)S(1)} collective-permute-done((f32[64,1024]{1,0:T(8,128)S(1)}, f32[64,1024]{1,0:T(8,128)S(1)}, u32[]{:S(2)}, u32[]{:S(2)}) %collective-permute-start.23) | collective-permute-done | bytes 262176 | tf_op jit(solution)/shard_map/ppermute | solution.py:233
  95.8 2.1 %collective-permute-done.27 = f32[64,1024]{1,0:T(8,128)S(1)} collective-permute-done((f32[64,1024]{1,0:T(8,128)S(1)}, f32[64,1024]{1,0:T(8,128)S(1)}, u32[]{:S(2)}, u32[]{:S(2)}) %collective-permute-start.27) | collective-permute-done | bytes 262176 | tf_op jit(solution)/shard_map/ppermute | solution.py:233
  97.9 0.7 collective-permute-done.35
  98.7 1.6 %collective-permute-start.36 = (f32[64,512]{1,0:T(8,128)S(1)}, f32[64,512]{1,0:T(8,128)S(1)}, u32[]{:S(2)}, u32[]{:S(2)}) collective-permute-start(f32[64,512]{1,0:T(8,128)S(1)} %get-tuple-element.78), channel_id=1, source_target_pairs={{0,4},{1,5},{4,8},{5,9},{8,12},{9,13},{12,14},{13,15},{14,10},{15,... | collective-permute-start | bytes 393224 | tf_op jit(solution)/shard_map/ppermute | solution.py:233
  100.3 0.4 collective-permute-start.39
  100.8 1.6 %collective-permute-start.24 = (f32[64,1024]{1,0:T(8,128)S(1)}, f32[64,1024]{1,0:T(8,128)S(1)}, u32[]{:S(2)}, u32[]{:S(2)}) collective-permute-start(f32[64,1024]{1,0:T(8,128)S(1)} %add.80), channel_id=1, source_target_pairs={{0,4},{1,5},{4,8},{5,9},{8,12},{9,13},{12,14},{13,15},{14,10},{15,... | collective-permute-start | bytes 786440 | tf_op jit(solution)/shard_map/ppermute | solution.py:233
  102.5 2.7 %collective-permute-done.36 = f32[64,512]{1,0:T(8,128)S(1)} collective-permute-done((f32[64,512]{1,0:T(8,128)S(1)}, f32[64,512]{1,0:T(8,128)S(1)}, u32[]{:S(2)}, u32[]{:S(2)}) %collective-permute-start.36) | collective-permute-done | bytes 131104 | tf_op jit(solution)/shard_map/ppermute | solution.py:233
  105.1 0.2 collective-permute-done.39
  105.4 1.6 %collective-permute-start.37 = (f32[64,512]{1,0:T(8,128)S(1)}, f32[64,512]{1,0:T(8,128)S(1)}, u32[]{:S(2)}, u32[]{:S(2)}) collective-permute-start(f32[64,512]{1,0:T(8,128)S(1)} %get-tuple-element.76), channel_id=1, source_target_pairs={{0,4},{1,5},{4,8},{5,9},{8,12},{9,13},{12,14},{13,15},{14,10},{15,... | collective-permute-start | bytes 393224 | tf_op jit(solution)/shard_map/ppermute | solution.py:233
  107.0 0.5 collective-permute-start.40
  107.5 0.5 collective-permute-start.28
  108.0 2.7 %collective-permute-done.24 = f32[64,1024]{1,0:T(8,128)S(1)} collective-permute-done((f32[64,1024]{1,0:T(8,128)S(1)}, f32[64,1024]{1,0:T(8,128)S(1)}, u32[]{:S(2)}, u32[]{:S(2)}) %collective-permute-start.24) | collective-permute-done | bytes 262176 | tf_op jit(solution)/shard_map/ppermute | solution.py:233
  110.8 1.6 %collective-permute-start.25 = (f32[64,1024]{1,0:T(8,128)S(1)}, f32[64,1024]{1,0:T(8,128)S(1)}, u32[]{:S(2)}, u32[]{:S(2)}) collective-permute-start(f32[64,1024]{1,0:T(8,128)S(1)} %add.81), channel_id=1, source_target_pairs={{0,4},{1,5},{4,8},{5,9},{8,12},{9,13},{12,14},{13,15},{14,10},{15,... | collective-permute-start | bytes 786440 | tf_op jit(solution)/shard_map/ppermute | solution.py:371
  112.4 1.1 collective-permute-done.37
  113.6 0.1 fusion.3
  113.6 1.6 %collective-permute-start.38 = (f32[64,512]{1,0:T(8,128)S(1)}, f32[64,512]{1,0:T(8,128)S(1)}, u32[]{:S(2)}, u32[]{:S(2)}) collective-permute-start(f32[64,512]{1,0:T(8,128)S(1)} %get-tuple-element.74), channel_id=1, source_target_pairs={{0,4},{1,5},{4,8},{5,9},{8,12},{9,13},{12,14},{13,15},{14,10},{15,... | collective-permute-start | bytes 393224 | tf_op jit(solution)/shard_map/ppermute | solution.py:233
  115.3 0.4 collective-permute-start.41
  115.7 1.3 %collective-permute-done.28 = f32[64,1024]{1,0:T(8,128)S(1)} collective-permute-done((f32[64,1024]{1,0:T(8,128)S(1)}, f32[64,1024]{1,0:T(8,128)S(1)}, u32[]{:S(2)}, u32[]{:S(2)}) %collective-permute-start.28) | collective-permute-done | bytes 262176 | tf_op jit(solution)/shard_map/ppermute | solution.py:233
  117.0 2.2 %collective-permute-done.25 = f32[64,1024]{1,0:T(8,128)S(1)} collective-permute-done((f32[64,1024]{1,0:T(8,128)S(1)}, f32[64,1024]{1,0:T(8,128)S(1)}, u32[]{:S(2)}, u32[]{:S(2)}) %collective-permute-start.25) | collective-permute-done | bytes 262176 | tf_op jit(solution)/shard_map/ppermute | solution.py:371
  119.1 0.8 add_add_fusion
  119.9 0.6 collective-permute-done.38
  120.6 0.7 fusion.8
  (103 shorter events, 0.6 us)
Async XLA Ops:
  0.6 44.5 %collective-permute-start.12 = (bf16[256,4096]{1,0:T(8,128)(2,1)}, bf16[256,4096]{1,0:T(8,128)(2,1)S(1)}, u32[]{:S(2)}, u32[]{:S(2)}) collective-permute-start(bf16[256,4096]{1,0:T(8,128)(2,1)} %refs_2_.1), channel_id=1, source_target_pairs={{0,1},{1,0},{2,3},{3,2},{4,5},{5,4},{6,7},{7,6},{8,9},{9,8},{10,11... | collective-permute-start | bytes 6291464 | tf_op jit(solution)/shard_map/ppermute | solution.py:227
  1.1 15.4 %collective-permute-start.4 = (bf16[256,1024]{1,0:T(8,128)(2,1)}, bf16[256,1024]{1,0:T(8,128)(2,1)S(1)}, u32[]{:S(2)}, u32[]{:S(2)}) collective-permute-start(bf16[256,1024]{1,0:T(8,128)(2,1)} %refs_4_.1), channel_id=1, source_target_pairs={{0,2},{1,3},{4,0},{5,1},{8,4},{9,5},{12,8},{13,9},{14,12},{15,13},... | collective-permute-start | bytes 1572872 | tf_op jit(solution)/shard_map/ppermute | solution.py:282
  3.7 12.8 %collective-permute-start.10 = (bf16[256,1024]{1,0:T(8,128)(2,1)}, bf16[256,1024]{1,0:T(8,128)(2,1)S(1)}, u32[]{:S(2)}, u32[]{:S(2)}) collective-permute-start(bf16[256,1024]{1,0:T(8,128)(2,1)} %refs_4_.1), channel_id=1, source_target_pairs={{0,1},{1,0},{2,3},{3,2},{4,5},{5,4},{6,7},{7,6},{8,9},{9,8},{10,11... | collective-permute-start | bytes 1572872 | tf_op jit(solution)/shard_map/ppermute | solution.py:227
  3.9 10.2 %collective-permute-start = (bf16[320,512]{1,0:T(8,128)(2,1)}, bf16[320,512]{1,0:T(8,128)(2,1)S(1)}, u32[]{:S(2)}, u32[]{:S(2)}) collective-permute-start(bf16[320,512]{1,0:T(8,128)(2,1)} %refs_10_.1), channel_id=1, source_target_pairs={{0,4},{1,5},{4,8},{5,9},{8,12},{9,13},{12,14},{13,15},{14,10},{15,... | collective-permute-start | bytes 983048 | tf_op jit(solution)/shard_map/ppermute | solution.py:292
  4.2 9.8 %collective-permute-start.1 = (bf16[320,512]{1,0:T(8,128)(2,1)}, bf16[320,512]{1,0:T(8,128)(2,1)S(1)}, u32[]{:S(2)}, u32[]{:S(2)}) collective-permute-start(bf16[320,512]{1,0:T(8,128)(2,1)} %refs_10_.1), channel_id=1, source_target_pairs={{0,1},{1,0},{2,3},{3,2},{4,5},{5,4},{6,7},{7,6},{8,9},{9,8},{10,11... | collective-permute-start | bytes 983048 | tf_op jit(solution)/shard_map/ppermute | solution.py:227
  14.1 48.0 %copy-start.21 = (bf16[320,512]{1,0:T(8,128)(2,1)}, bf16[320,512]{1,0:T(8,128)(2,1)S(1)}, u32[]{:S(2)}) copy-start(bf16[320,512]{1,0:T(8,128)(2,1)S(1)} %collective-permute-done.refs_12_) | copy-start | bytes 983044
  14.1 9.2 %collective-permute-start.2 = (bf16[320,512]{1,0:T(8,128)(2,1)S(1)}, bf16[320,512]{1,0:T(8,128)(2,1)S(1)}, u32[]{:S(2)}, u32[]{:S(2)}) collective-permute-start(bf16[320,512]{1,0:T(8,128)(2,1)S(1)} %collective-permute-done.refs_12_), channel_id=1, source_target_pairs={{0,4},{1,5},{4,8},{5,9},{8,12},{9,13},{12,14},{13,15},{14,10},{15,... | collective-permute-start | bytes 983048 | tf_op jit(solution)/shard_map/ppermute | solution.py:292
  14.4 8.9 %collective-permute-start.3 = (bf16[320,512]{1,0:T(8,128)(2,1)S(1)}, bf16[320,512]{1,0:T(8,128)(2,1)S(1)}, u32[]{:S(2)}, u32[]{:S(2)}) collective-permute-start(bf16[320,512]{1,0:T(8,128)(2,1)S(1)} %collective-permute-done.refs_12_), channel_id=1, source_target_pairs={{0,1},{1,0},{2,3},{3,2},{4,5},{5,4},{6,7},{7,6},{8,9},{9,8},{10,11... | collective-permute-start | bytes 983048 | tf_op jit(solution)/shard_map/ppermute | solution.py:227
  16.5 28.6 %copy-start.17 = (bf16[256,1024]{1,0:T(8,128)(2,1)}, bf16[256,1024]{1,0:T(8,128)(2,1)S(1)}, u32[]{:S(2)}) copy-start(bf16[256,1024]{1,0:T(8,128)(2,1)S(1)} %collective-permute-done.4.refs_5_) | copy-start | bytes 1572868
  16.5 38.6 %copy-start.16 = (bf16[256,1024]{1,0:T(8,128)(2,1)}, bf16[256,1024]{1,0:T(8,128)(2,1)S(1)}, u32[]{:S(2)}) copy-start(bf16[256,1024]{1,0:T(8,128)(2,1)S(1)} %collective-permute-done.10.refs_4_.refs_5_) | copy-start | bytes 1572868
  16.5 15.2 %collective-permute-start.11 = (bf16[256,1024]{1,0:T(8,128)(2,1)S(1)}, bf16[256,1024]{1,0:T(8,128)(2,1)}, u32[]{:S(2)}, u32[]{:S(2)}) collective-permute-start(bf16[256,1024]{1,0:T(8,128)(2,1)S(1)} %collective-permute-done.4.refs_5_), channel_id=1, source_target_pairs={{0,2},{1,3},{4,0},{5,1},{8,4},{9,5},{12,8},{13,9},{14,12},{15,13},... | collective-permute-start | bytes 1572872 | tf_op jit(solution)/shard_map/ppermute | solution.py:282
  18.3 13.4 %collective-permute-start.15 = (bf16[256,1024]{1,0:T(8,128)(2,1)S(1)}, bf16[256,1024]{1,0:T(8,128)(2,1)S(1)}, u32[]{:S(2)}, u32[]{:S(2)}) collective-permute-start(bf16[256,1024]{1,0:T(8,128)(2,1)S(1)} %collective-permute-done.4.refs_5_), channel_id=1, source_target_pairs={{0,1},{1,0},{2,3},{3,2},{4,5},{5,4},{6,7},{7,6},{8,9},{9,8},{10,11... | collective-permute-start | bytes 1572872 | tf_op jit(solution)/shard_map/ppermute | solution.py:227
  23.3 22.3 %copy-start.23 = (bf16[320,512]{1,0:T(8,128)(2,1)}, bf16[320,512]{1,0:T(8,128)(2,1)S(1)}, u32[]{:S(2)}) copy-start(bf16[320,512]{1,0:T(8,128)(2,1)S(1)} %collective-permute-done.2.refs_14_) | copy-start | bytes 983044
  23.3 22.3 %copy-start.24 = (bf16[320,512]{1,0:T(8,128)(2,1)}, bf16[320,512]{1,0:T(8,128)(2,1)S(1)}, u32[]{:S(2)}) copy-start(bf16[320,512]{1,0:T(8,128)(2,1)S(1)} %collective-permute-done.3.refs_13_) | copy-start | bytes 983044
  23.3 8.4 %collective-permute-start.5 = (bf16[320,512]{1,0:T(8,128)(2,1)S(1)}, bf16[320,512]{1,0:T(8,128)(2,1)S(1)}, u32[]{:S(2)}, u32[]{:S(2)}) collective-permute-start(bf16[320,512]{1,0:T(8,128)(2,1)S(1)} %collective-permute-done.2.refs_14_), channel_id=1, source_target_pairs={{0,4},{1,5},{4,8},{5,9},{8,12},{9,13},{12,14},{13,15},{14,10},{15,... | collective-permute-start | bytes 983048 | tf_op jit(solution)/shard_map/ppermute | solution.py:292
  31.7 13.9 %copy-start.25 = (bf16[320,512]{1,0:T(8,128)(2,1)}, bf16[320,512]{1,0:T(8,128)(2,1)S(1)}, u32[]{:S(2)}) copy-start(bf16[320,512]{1,0:T(8,128)(2,1)S(1)} %collective-permute-done.5.refs_16_) | copy-start | bytes 983044
  31.7 13.9 %copy-start.18 = (bf16[256,1024]{1,0:T(8,128)(2,1)}, bf16[256,1024]{1,0:T(8,128)(2,1)S(1)}, u32[]{:S(2)}) copy-start(bf16[256,1024]{1,0:T(8,128)(2,1)S(1)} %collective-permute-done.15.refs_6_) | copy-start | bytes 1572868
  31.7 12.1 %collective-permute-start.16 = (bf16[256,1024]{1,0:T(8,128)(2,1)}, bf16[256,1024]{1,0:T(8,128)(2,1)}, u32[]{:S(2)}, u32[]{:S(2)}) collective-permute-start(bf16[256,1024]{1,0:T(8,128)(2,1)} %collective-permute-done.11.refs_7_), channel_id=1, source_target_pairs={{0,2},{1,3},{4,0},{5,1},{8,4},{9,5},{12,8},{13,9},{14,12},{15,13},... | collective-permute-start | bytes 1572872 | tf_op jit(solution)/shard_map/ppermute | solution.py:282
  33.3 1.8 %collective-permute-start.6 = (bf16[320,512]{1,0:T(8,128)(2,1)S(1)}, bf16[320,512]{1,0:T(8,128)(2,1)S(1)}, u32[]{:S(2)}, u32[]{:S(2)}) collective-permute-start(bf16[320,512]{1,0:T(8,128)(2,1)S(1)} %collective-permute-done.2.refs_14_), channel_id=1, source_target_pairs={{0,1},{1,0},{2,3},{3,2},{4,5},{5,4},{6,7},{7,6},{8,9},{9,8},{10,11... | collective-permute-start | bytes 983048 | tf_op jit(solution)/shard_map/ppermute | solution.py:227
  33.3 1.8 %collective-permute-start.7 = (bf16[64,1024]{1,0:T(8,128)(2,1)}, bf16[64,1024]{1,0:T(8,128)(2,1)S(1)}, u32[]{:S(2)}, u32[]{:S(2)}) collective-permute-start(bf16[64,1024]{1,0:T(8,128)(2,1)} %refs_6_.1), channel_id=1, source_target_pairs={{0,1},{1,0},{2,3},{3,2},{4,5},{5,4},{6,7},{7,6},{8,9},{9,8},{10,11... | collective-permute-start | bytes 393224 | tf_op jit(solution)/shard_map/ppermute | solution.py:227
  35.1 27.0 %copy-start.33 = (bf16[64,1024]{1,0:T(8,128)(2,1)}, bf16[64,1024]{1,0:T(8,128)(2,1)S(1)}, u32[]{:S(2)}) copy-start(bf16[64,1024]{1,0:T(8,128)(2,1)S(1)} %collective-permute-done.7.refs_7_) | copy-start | bytes 393220
  35.2 9.9 %collective-permute-start.8 = (bf16[320,512]{1,0:T(8,128)(2,1)S(1)}, bf16[320,512]{1,0:T(8,128)(2,1)S(1)}, u32[]{:S(2)}, u32[]{:S(2)}) collective-permute-start(bf16[320,512]{1,0:T(8,128)(2,1)S(1)} %collective-permute-done.5.refs_16_), channel_id=1, source_target_pairs={{0,4},{1,5},{4,8},{5,9},{8,12},{9,13},{12,14},{13,15},{14,10},{15,... | collective-permute-start | bytes 983048 | tf_op jit(solution)/shard_map/ppermute | solution.py:292
  35.6 9.5 %collective-permute-start.9 = (bf16[320,512]{1,0:T(8,128)(2,1)S(1)}, bf16[320,512]{1,0:T(8,128)(2,1)S(1)}, u32[]{:S(2)}, u32[]{:S(2)}) collective-permute-start(bf16[320,512]{1,0:T(8,128)(2,1)S(1)} %collective-permute-done.5.refs_16_), channel_id=1, source_target_pairs={{0,1},{1,0},{2,3},{3,2},{4,5},{5,4},{6,7},{7,6},{8,9},{9,8},{10,11... | collective-permute-start | bytes 983048 | tf_op jit(solution)/shard_map/ppermute | solution.py:227
  35.6 10.2 %collective-permute-start.18 = (bf16[256,1024]{1,0:T(8,128)(2,1)}, bf16[256,1024]{1,0:T(8,128)(2,1)}, u32[]{:S(2)}, u32[]{:S(2)}) collective-permute-start(bf16[256,1024]{1,0:T(8,128)(2,1)} %collective-permute-done.11.refs_7_), channel_id=1, source_target_pairs={{0,1},{1,0},{2,3},{3,2},{4,5},{5,4},{6,7},{7,6},{8,9},{9,8},{10,11... | collective-permute-start | bytes 1572872 | tf_op jit(solution)/shard_map/ppermute | solution.py:227
  43.8 11.3 %collective-permute-start.19 = (bf16[256,1024]{1,0:T(8,128)(2,1)}, bf16[256,1024]{1,0:T(8,128)(2,1)}, u32[]{:S(2)}, u32[]{:S(2)}) collective-permute-start(bf16[256,1024]{1,0:T(8,128)(2,1)} %collective-permute-done.16.refs_9_), channel_id=1, source_target_pairs={{0,1},{1,0},{2,3},{3,2},{4,5},{5,4},{6,7},{7,6},{8,9},{9,8},{10,11... | collective-permute-start | bytes 1572872 | tf_op jit(solution)/shard_map/ppermute | solution.py:227
  45.1 17.0 %copy-start.27 = (bf16[320,512]{1,0:T(8,128)(2,1)}, bf16[320,512]{1,0:T(8,128)(2,1)S(1)}, u32[]{:S(2)}) copy-start(bf16[320,512]{1,0:T(8,128)(2,1)S(1)} %collective-permute-done.8.refs_18_) | copy-start | bytes 983044
  45.1 9.3 %collective-permute-start.13 = (bf16[320,512]{1,0:T(8,128)(2,1)S(1)}, bf16[320,512]{1,0:T(8,128)(2,1)}, u32[]{:S(2)}, u32[]{:S(2)}) collective-permute-start(bf16[320,512]{1,0:T(8,128)(2,1)S(1)} %collective-permute-done.8.refs_18_), channel_id=1, source_target_pairs={{0,4},{1,5},{4,8},{5,9},{8,12},{9,13},{12,14},{13,15},{14,10},{15,... | collective-permute-start | bytes 983048 | tf_op jit(solution)/shard_map/ppermute | solution.py:292
  45.6 8.8 %collective-permute-start.14 = (bf16[320,512]{1,0:T(8,128)(2,1)S(1)}, bf16[320,512]{1,0:T(8,128)(2,1)}, u32[]{:S(2)}, u32[]{:S(2)}) collective-permute-start(bf16[320,512]{1,0:T(8,128)(2,1)S(1)} %collective-permute-done.8.refs_18_), channel_id=1, source_target_pairs={{0,1},{1,0},{2,3},{3,2},{4,5},{5,4},{6,7},{7,6},{8,9},{9,8},{10,11... | collective-permute-start | bytes 983048 | tf_op jit(solution)/shard_map/ppermute | solution.py:227
  45.9 17.0 %collective-permute-start.20 = (bf16[256,1024]{1,0:T(8,128)(2,1)}, bf16[256,1024]{1,0:T(8,128)(2,1)S(1)}, u32[]{:S(2)}, u32[]{:S(2)}) collective-permute-start(bf16[256,1024]{1,0:T(8,128)(2,1)} %collective-permute-done.16.refs_9_), channel_id=1, source_target_pairs={{4,0},{5,1},{8,4},{9,5},{12,8},{13,9},{14,12},{15,13},{20,16},{21,... | collective-permute-start | bytes 1572872 | tf_op jit(solution)/shard_map/ppermute | solution.py:282
  54.4 8.5 %collective-permute-start.17 = (bf16[320,512]{1,0:T(8,128)(2,1)}, bf16[320,512]{1,0:T(8,128)(2,1)}, u32[]{:S(2)}, u32[]{:S(2)}) collective-permute-start(bf16[320,512]{1,0:T(8,128)(2,1)} %collective-permute-done.13.refs_20_), channel_id=1, source_target_pairs={{0,4},{1,5},{4,8},{5,9},{8,12},{9,13},{12,14},{13,15},{14,10},{15,... | collective-permute-start | bytes 983048 | tf_op jit(solution)/shard_map/ppermute | solution.py:292
  62.9 2.0 %collective-permute-start.21 = (bf16[256,1024]{1,0:T(8,128)(2,1)S(1)}, bf16[256,1024]{1,0:T(8,128)(2,1)S(1)}, u32[]{:S(2)}, u32[]{:S(2)}) collective-permute-start(bf16[256,1024]{1,0:T(8,128)(2,1)S(1)} %collective-permute-done.20.refs_5_), channel_id=1, source_target_pairs={{0,1},{1,0},{2,3},{3,2},{4,5},{5,4},{6,7},{7,6},{8,9},{9,8},{10,11... | collective-permute-start | bytes 1572872 | tf_op jit(solution)/shard_map/ppermute | solution.py:227
  62.9 12.7 %collective-permute-start.29 = (bf16[320,512]{1,0:T(8,128)(2,1)}, bf16[320,512]{1,0:T(8,128)(2,1)S(1)}, u32[]{:S(2)}, u32[]{:S(2)}) collective-permute-start(bf16[320,512]{1,0:T(8,128)(2,1)} %collective-permute-done.13.refs_20_), channel_id=1, source_target_pairs={{0,1},{1,0},{2,3},{3,2},{4,5},{5,4},{6,7},{7,6},{8,9},{9,8},{10,11... | collective-permute-start | bytes 983048 | tf_op jit(solution)/shard_map/ppermute | solution.py:227
  63.4 9.9 %collective-permute-start.31 = (bf16[320,512]{1,0:T(8,128)(2,1)}, bf16[320,512]{1,0:T(8,128)(2,1)S(1)}, u32[]{:S(2)}, u32[]{:S(2)}) collective-permute-start(bf16[320,512]{1,0:T(8,128)(2,1)} %collective-permute-done.17.refs_22_), channel_id=1, source_target_pairs={{0,4},{1,5},{4,8},{5,9},{8,12},{9,13},{12,14},{13,15},{14,10},{15,... | collective-permute-start | bytes 983048 | tf_op jit(solution)/shard_map/ppermute | solution.py:292
  64.6 11.0 %collective-permute-start.30 = (bf16[320,512]{1,0:T(8,128)(2,1)}, bf16[320,512]{1,0:T(8,128)(2,1)S(1)}, u32[]{:S(2)}, u32[]{:S(2)}) collective-permute-start(bf16[320,512]{1,0:T(8,128)(2,1)} %collective-permute-done.17.refs_22_), channel_id=1, source_target_pairs={{0,1},{1,0},{2,3},{3,2},{4,5},{5,4},{6,7},{7,6},{8,9},{9,8},{10,11... | collective-permute-start | bytes 983048 | tf_op jit(solution)/shard_map/ppermute | solution.py:227
  73.3 2.3 %collective-permute-start.32 = (bf16[320,512]{1,0:T(8,128)(2,1)S(1)}, bf16[320,512]{1,0:T(8,128)(2,1)S(1)}, u32[]{:S(2)}, u32[]{:S(2)}) collective-permute-start(bf16[320,512]{1,0:T(8,128)(2,1)S(1)} %collective-permute-done.31.refs_24_), channel_id=1, source_target_pairs={{0,1},{1,0},{2,3},{3,2},{4,5},{5,4},{6,7},{7,6},{8,9},{9,8},{10,11... | collective-permute-start | bytes 983048 | tf_op jit(solution)/shard_map/ppermute | solution.py:227
  73.3 13.2 %collective-permute-start.22 = (f32[64,1024]{1,0:T(8,128)}, f32[64,1024]{1,0:T(8,128)S(1)}, u32[]{:S(2)}, u32[]{:S(2)}) collective-permute-start(f32[64,1024]{1,0:T(8,128)} %get-tuple-element.51), channel_id=1, source_target_pairs={{0,4},{1,5},{4,8},{5,9},{8,12},{9,13},{12,14},{13,15},{14,10},{15,... | collective-permute-start | bytes 786440 | tf_op jit(solution)/shard_map/ppermute | solution.py:233
  75.5 11.0 %collective-permute-start.26 = (f32[64,1024]{1,0:T(8,128)}, f32[64,1024]{1,0:T(8,128)S(1)}, u32[]{:S(2)}, u32[]{:S(2)}) collective-permute-start(f32[64,1024]{1,0:T(8,128)} %get-tuple-element.55), channel_id=1, source_target_pairs={{0,2},{1,3},{4,0},{5,1},{8,4},{9,5},{12,8},{13,9},{14,12},{15,13},... | collective-permute-start | bytes 786440 | tf_op jit(solution)/shard_map/ppermute | solution.py:233
  76.5 12.2 %copy-start.3 = (f32[64,1024]{1,0:T(8,128)S(1)}, f32[64,1024]{1,0:T(8,128)}, u32[]{:S(2)}) copy-start(f32[64,1024]{1,0:T(8,128)} %get-tuple-element.56) | copy-start | bytes 786436
  86.5 12.2 %copy-start.7 = (f32[64,512]{1,0:T(8,128)S(1)}, f32[64,512]{1,0:T(8,128)}, u32[]{:S(2)}) copy-start(f32[64,512]{1,0:T(8,128)} %get-tuple-element.65) | copy-start | bytes 393220
  86.5 14.3 %copy-start.2 = (f32[64,1024]{1,0:T(8,128)S(1)}, f32[64,1024]{1,0:T(8,128)}, u32[]{:S(2)}) copy-start(f32[64,1024]{1,0:T(8,128)} %get-tuple-element.53) | copy-start | bytes 786436
  86.5 18.8 %copy-start.12 = (f32[64,512]{1,0:T(8,128)S(1)}, f32[64,512]{1,0:T(8,128)}, u32[]{:S(2)}) copy-start(f32[64,512]{1,0:T(8,128)} %get-tuple-element.68) | copy-start | bytes 393220
  86.5 18.8 %copy-start.13 = (f32[64,512]{1,0:T(8,128)S(1)}, f32[64,512]{1,0:T(8,128)}, u32[]{:S(2)}) copy-start(f32[64,512]{1,0:T(8,128)} %get-tuple-element.72) | copy-start | bytes 393220
  86.5 2.9 %collective-permute-start.33 = (f32[512,512]{1,0:T(8,128)}, f32[512,512]{1,0:T(8,128)S(1)}, u32[]{:S(2)}, u32[]{:S(2)}) collective-permute-start(f32[512,512]{1,0:T(8,128)} %get-tuple-element.64), channel_id=1, source_target_pairs={{0,1},{1,0},{2,3},{3,2},{4,5},{5,4},{6,7},{7,6},{8,9},{9,8},{10,11... | collective-permute-start | bytes 3145736 | tf_op jit(solution)/shard_map/ppermute | solution.py:227
  86.7 9.1 %collective-permute-start.23 = (f32[64,1024]{1,0:T(8,128)S(1)}, f32[64,1024]{1,0:T(8,128)S(1)}, u32[]{:S(2)}, u32[]{:S(2)}) collective-permute-start(f32[64,1024]{1,0:T(8,128)S(1)} %add.79), channel_id=1, source_target_pairs={{0,4},{1,5},{4,8},{5,9},{8,12},{9,13},{12,14},{13,15},{14,10},{15,... | collective-permute-start | bytes 786440 | tf_op jit(solution)/shard_map/ppermute | solution.py:233
  88.7 18.7 %copy-start.1 = (f32[64,1024]{1,0:T(8,128)S(1)}, f32[64,1024]{1,0:T(8,128)}, u32[]{:S(2)}) copy-start(f32[64,1024]{1,0:T(8,128)} %get-tuple-element.57) | copy-start | bytes 786436
  88.8 9.2 %collective-permute-start.27 = (f32[64,1024]{1,0:T(8,128)S(1)}, f32[64,1024]{1,0:T(8,128)S(1)}, u32[]{:S(2)}, u32[]{:S(2)}) collective-permute-start(f32[64,1024]{1,0:T(8,128)S(1)} %add.83), channel_id=1, source_target_pairs={{0,2},{1,3},{4,0},{5,1},{8,4},{9,5},{12,8},{13,9},{14,12},{15,13},... | collective-permute-start | bytes 786440 | tf_op jit(solution)/shard_map/ppermute | solution.py:233
  89.5 21.3 %copy-start = (f32[64,1024]{1,0:T(8,128)S(1)}, f32[64,1024]{1,0:T(8,128)}, u32[]{:S(2)}) copy-start(f32[64,1024]{1,0:T(8,128)} %get-tuple-element.54) | copy-start | bytes 786436
  90.5 7.5 %collective-permute-start.34 = (f32[32,512]{1,0:T(8,128)S(1)}, f32[32,512]{1,0:T(8,128)S(1)}, u32[]{:S(2)}, u32[]{:S(2)}) collective-permute-start(f32[32,512]{1,0:T(8,128)S(1)} %get-tuple-element.81), channel_id=1, source_target_pairs={{0,4},{1,5},{4,8},{5,9},{8,12},{9,13},{12,14},{13,15},{14,10},{15,... | collective-permute-start | bytes 196616 | tf_op jit(solution)/shard_map/ppermute | solution.py:233
  92.5 6.1 %collective-permute-start.35 = (f32[32,512]{1,0:T(8,128)S(1)}, f32[32,512]{1,0:T(8,128)S(1)}, u32[]{:S(2)}, u32[]{:S(2)}) collective-permute-start(f32[32,512]{1,0:T(8,128)S(1)} %get-tuple-element.80), channel_id=1, source_target_pairs={{0,2},{1,3},{4,0},{5,1},{8,4},{9,5},{12,8},{13,9},{14,12},{15,13},... | collective-permute-start | bytes 196616 | tf_op jit(solution)/shard_map/ppermute | solution.py:233
  98.6 14.9 %copy-start.10 = (f32[64,512]{1,0:T(8,128)S(1)}, f32[64,512]{1,0:T(8,128)}, u32[]{:S(2)}) copy-start(f32[64,512]{1,0:T(8,128)} %get-tuple-element.69) | copy-start | bytes 393220
  98.6 14.9 %copy-start.11 = (f32[64,512]{1,0:T(8,128)S(1)}, f32[64,512]{1,0:T(8,128)}, u32[]{:S(2)}) copy-start(f32[64,512]{1,0:T(8,128)} %get-tuple-element.73) | copy-start | bytes 393220
  98.7 6.4 %collective-permute-start.36 = (f32[64,512]{1,0:T(8,128)S(1)}, f32[64,512]{1,0:T(8,128)S(1)}, u32[]{:S(2)}, u32[]{:S(2)}) collective-permute-start(f32[64,512]{1,0:T(8,128)S(1)} %get-tuple-element.78), channel_id=1, source_target_pairs={{0,4},{1,5},{4,8},{5,9},{8,12},{9,13},{12,14},{13,15},{14,10},{15,... | collective-permute-start | bytes 393224 | tf_op jit(solution)/shard_map/ppermute | solution.py:233
  100.3 5.0 %collective-permute-start.39 = (f32[64,512]{1,0:T(8,128)S(1)}, f32[64,512]{1,0:T(8,128)S(1)}, u32[]{:S(2)}, u32[]{:S(2)}) collective-permute-start(f32[64,512]{1,0:T(8,128)S(1)} %get-tuple-element.79), channel_id=1, source_target_pairs={{0,2},{1,3},{4,0},{5,1},{8,4},{9,5},{12,8},{13,9},{14,12},{15,13},... | collective-permute-start | bytes 393224 | tf_op jit(solution)/shard_map/ppermute | solution.py:233
  100.8 18.4 %copy-start.5 = (f32[64,1024]{1,0:T(8,128)S(1)}, f32[64,1024]{1,0:T(8,128)}, u32[]{:S(2)}) copy-start(f32[64,1024]{1,0:T(8,128)} %get-tuple-element.50) | copy-start | bytes 786436
  100.8 18.4 %copy-start.6 = (bf16[64,1024]{1,0:T(8,128)(2,1)S(1)}, bf16[64,1024]{1,0:T(8,128)(2,1)}, u32[]{:S(2)}) copy-start(bf16[64,1024]{1,0:T(8,128)(2,1)} %refs_6_.1) | copy-start | bytes 393220
  100.8 9.9 %collective-permute-start.24 = (f32[64,1024]{1,0:T(8,128)S(1)}, f32[64,1024]{1,0:T(8,128)S(1)}, u32[]{:S(2)}, u32[]{:S(2)}) collective-permute-start(f32[64,1024]{1,0:T(8,128)S(1)} %add.80), channel_id=1, source_target_pairs={{0,4},{1,5},{4,8},{5,9},{8,12},{9,13},{12,14},{13,15},{14,10},{15,... | collective-permute-start | bytes 786440 | tf_op jit(solution)/shard_map/ppermute | solution.py:233
  105.4 15.2 %copy-start.9 = (f32[64,512]{1,0:T(8,128)S(1)}, f32[64,512]{1,0:T(8,128)}, u32[]{:S(2)}) copy-start(f32[64,512]{1,0:T(8,128)} %get-tuple-element.62) | copy-start | bytes 393220
  105.4 15.2 %copy-start.14 = (bf16[64,512]{1,0:T(8,128)(2,1)S(1)}, bf16[64,512]{1,0:T(8,128)(2,1)}, u32[]{:S(2)}) copy-start(bf16[64,512]{1,0:T(8,128)(2,1)} %param.10) | copy-start | bytes 196612
  105.4 8.2 %collective-permute-start.37 = (f32[64,512]{1,0:T(8,128)S(1)}, f32[64,512]{1,0:T(8,128)S(1)}, u32[]{:S(2)}, u32[]{:S(2)}) collective-permute-start(f32[64,512]{1,0:T(8,128)S(1)} %get-tuple-element.76), channel_id=1, source_target_pairs={{0,4},{1,5},{4,8},{5,9},{8,12},{9,13},{12,14},{13,15},{14,10},{15,... | collective-permute-start | bytes 393224 | tf_op jit(solution)/shard_map/ppermute | solution.py:233
  107.0 6.6 %collective-permute-start.40 = (f32[64,512]{1,0:T(8,128)S(1)}, f32[64,512]{1,0:T(8,128)S(1)}, u32[]{:S(2)}, u32[]{:S(2)}) collective-permute-start(f32[64,512]{1,0:T(8,128)S(1)} %get-tuple-element.77), channel_id=1, source_target_pairs={{0,2},{1,3},{4,0},{5,1},{8,4},{9,5},{12,8},{13,9},{14,12},{15,13},... | collective-permute-start | bytes 393224 | tf_op jit(solution)/shard_map/ppermute | solution.py:233
  107.5 9.5 %collective-permute-start.28 = (f32[64,1024]{1,0:T(8,128)S(1)}, f32[64,1024]{1,0:T(8,128)S(1)}, u32[]{:S(2)}, u32[]{:S(2)}) collective-permute-start(f32[64,1024]{1,0:T(8,128)S(1)} %add.84), channel_id=1, source_target_pairs={{0,2},{1,3},{4,0},{5,1},{8,4},{9,5},{12,8},{13,9},{14,12},{15,13},... | collective-permute-start | bytes 786440 | tf_op jit(solution)/shard_map/ppermute | solution.py:233
  110.8 8.4 %collective-permute-start.25 = (f32[64,1024]{1,0:T(8,128)S(1)}, f32[64,1024]{1,0:T(8,128)S(1)}, u32[]{:S(2)}, u32[]{:S(2)}) collective-permute-start(f32[64,1024]{1,0:T(8,128)S(1)} %add.81), channel_id=1, source_target_pairs={{0,4},{1,5},{4,8},{5,9},{8,12},{9,13},{12,14},{13,15},{14,10},{15,... | collective-permute-start | bytes 786440 | tf_op jit(solution)/shard_map/ppermute | solution.py:371
  113.6 6.9 %collective-permute-start.38 = (f32[64,512]{1,0:T(8,128)S(1)}, f32[64,512]{1,0:T(8,128)S(1)}, u32[]{:S(2)}, u32[]{:S(2)}) collective-permute-start(f32[64,512]{1,0:T(8,128)S(1)} %get-tuple-element.74), channel_id=1, source_target_pairs={{0,4},{1,5},{4,8},{5,9},{8,12},{9,13},{12,14},{13,15},{14,10},{15,... | collective-permute-start | bytes 393224 | tf_op jit(solution)/shard_map/ppermute | solution.py:233
  115.3 5.3 %collective-permute-start.41 = (f32[64,512]{1,0:T(8,128)S(1)}, f32[64,512]{1,0:T(8,128)S(1)}, u32[]{:S(2)}, u32[]{:S(2)}) collective-permute-start(f32[64,512]{1,0:T(8,128)S(1)} %get-tuple-element.75), channel_id=1, source_target_pairs={{0,2},{1,3},{4,0},{5,1},{8,4},{9,5},{12,8},{13,9},{14,12},{15,13},... | collective-permute-start | bytes 393224 | tf_op jit(solution)/shard_map/ppermute | solution.py:233
  (12 other events, 53.6 us)
